TPU v7x, 32 devices: a whole 2x2x4 slice. The times are simulated.
32 devices in a mesh: replica: 4 (over x, core), fsdp: 8 (over z, y).
Axes of the slice: x: 2, y: 2, z: 4, core: 2. Of those that a mesh axis runs over, the one named last changes fastest.
Arguments:
- tokens: bfloat16 [12288, 1536], P(('replica', 'fsdp')), may hold values from -6 to 6
- seg_ids: int32 [32, 384], P(('replica', 'fsdp')), may hold values from 0 to 11, never falling along the last dimension, each value on 1 to 192 neighbouring positions
- routes: int32 [12288, 4], P(('replica', 'fsdp')), may hold values from 0 to 7, all different within a row; in each aligned block of 384 rows (0 to 383, 384 to 767, ...) at most 288 rows name the same one
- in_proj: bfloat16 [1536, 2048], P('fsdp'), may hold values from -0.15625 to 0.15625
- out_proj: bfloat16 [1536, 1536], P('fsdp'), may hold values from -0.625 to 0.625
- router: bfloat16 [1536, 8], P('fsdp'), may hold values from -0.078125 to 0.078125
- norm_gains: bfloat16 [1536, 2], P('fsdp'), may hold values from 0.5 to 1.5
- expert_in: bfloat16 [1536, 8, 1536], P('fsdp'), may hold values from -0.15625 to 0.15625
- expert_out: bfloat16 [1536, 8, 768], P('fsdp'), may hold values from -0.625 to 0.625
- out_grad: bfloat16 [12288, 1536], P(('replica', 'fsdp')), may hold values from -6 to 6
Outputs:
- mixed: bfloat16 [12288, 1536], P(('replica', 'fsdp'))
- tokens_grad: bfloat16 [12288, 1536], P(('replica', 'fsdp'))
- in_proj_grad: float32 [1536, 2048], P('fsdp')
- out_proj_grad: float32 [1536, 1536], P('fsdp')
- router_grad: float32 [1536, 8], P('fsdp')
- gains_grad: float32 [1536, 2], P('fsdp')
- expert_in_grad: float32 [1536, 8, 1536], P('fsdp')
- expert_out_grad: float32 [1536, 8, 768], P('fsdp')
Inputs may be any that keep to these rules, and one draw needn't show every extreme that they name: `routes`: each token names 4 different experts. In the rows of one device no expert is named more than 288 times, a bound that some block reaches. `seg_ids`: along a sequence document numbers never fall; a document covers at most 192 positions.
All inputs are finite; a program needn't handle non-finite values.
Results may differ from a plain program's by a relative error of at most 0.017.
Values may be sent and summed in bfloat16 or wider, within the bound.
A program may use at most 448 MiB of HBM per device.

v0:
```python
import jax
import jax.numpy as jnp
from jax import lax
from jax.sharding import PartitionSpec as P

HQ = 12
KV = 2
HD = 128
CAP = 288


epsilon = 1e-06
rope_base = 1000000.0


def rms_scale(v):
    return lax.rsqrt(jnp.mean(v * v, axis=-1, keepdims=True) + epsilon)


def tables(length):
    half = HD // 2
    freq = jnp.power(rope_base, -(jnp.arange(half, dtype=jnp.float32) * 2.0 / HD))
    angle = jnp.arange(length, dtype=jnp.float32)[:, None] * freq[None, :]
    return (jnp.cos(angle)[:, None, :], jnp.sin(angle)[:, None, :])


def rotate(v, cosine, sine):
    half = v.shape[-1] // 2
    first = v[..., :half]
    second = v[..., half:]
    return jnp.concatenate(
        [first * cosine - second * sine, second * cosine + first * sine], axis=-1
    )


def unrotate(grad, cosine, sine):
    half = grad.shape[-1] // 2
    first = grad[..., :half]
    second = grad[..., half:]
    return jnp.concatenate(
        [first * cosine + second * sine, second * cosine - first * sine], axis=-1
    )


def contract_rows(left, right):
    return lax.dot_general(
        left, right, (((0,), (0,)), ((), ())), preferred_element_type=jnp.float32
    )


def contract_cols(left, right):
    return lax.dot_general(
        left, right, (((1,), (1,)), ((), ())), preferred_element_type=jnp.float32
    )


def shards(
    tokens, seg_ids, routes, in_proj, out_proj, router, norm_gains, expert_in, expert_out, out_grad
):
    length = tokens.shape[0]
    width = tokens.shape[1]
    experts = router.shape[1]
    hidden_w = expert_out.shape[2]
    top = routes.shape[1]
    group = HQ // KV
    width_q = HQ * HD
    width_k = KV * HD
    scale = HD ** (-0.5)
    cosine, sine = tables(length)
    segment = seg_ids[0]
    place = jnp.arange(length)
    allowed = ((place[:, None] >= place[None, :]) & (segment[:, None] == segment[None, :]))[
        None, None
    ]
    proj_in, proj_out, router_all, gains_all = (
        lax.all_gather(in_proj, "fsdp", axis=0, tiled=True),
        lax.all_gather(out_proj, "fsdp", axis=0, tiled=True),
        lax.all_gather(router, "fsdp", axis=0, tiled=True),
        lax.all_gather(norm_gains, "fsdp", axis=0, tiled=True),
    )
    gain_one = gains_all[:, 0].astype(jnp.float32)
    gain_two = gains_all[:, 1].astype(jnp.float32)
    inputs = tokens.astype(jnp.float32)
    scale_one = rms_scale(inputs)
    unit_one = inputs * scale_one
    normed = (unit_one * gain_one).astype(jnp.bfloat16)
    proj = jnp.dot(normed, proj_in, preferred_element_type=jnp.float32)
    queries = (
        rotate(proj[:, :width_q].reshape(length, HQ, HD), cosine, sine)
        .astype(jnp.bfloat16)
        .reshape(length, KV, group, HD)
    )
    keys = rotate(
        proj[:, width_q : width_q + width_k].reshape(length, KV, HD), cosine, sine
    ).astype(jnp.bfloat16)
    values = proj[:, width_q + width_k :].reshape(length, KV, HD).astype(jnp.bfloat16)
    scores = jnp.einsum("qkgd,tkd->kgqt", queries, keys, preferred_element_type=jnp.float32) * scale
    masked = jnp.where(allowed, scores, -1e30)
    highest = jnp.max(masked, axis=-1, keepdims=True)
    expo = jnp.exp(masked - highest)
    total = jnp.sum(expo, axis=-1, keepdims=True)
    log_total = highest + jnp.log(total)
    probs_low = (expo / total).astype(jnp.bfloat16)
    attn = jnp.einsum("kgqt,tkd->qkgd", probs_low, values, preferred_element_type=jnp.float32)
    attn = attn.astype(jnp.bfloat16).reshape(length, width_q)
    first = inputs + contract_cols(attn, proj_out)
    scale_two = rms_scale(first)
    unit_two = first * scale_two
    normed_two = (unit_two * gain_two).astype(jnp.bfloat16)
    logits = jnp.dot(normed_two, router_all, preferred_element_type=jnp.float32)
    onehot = (routes[:, :, None] == jnp.arange(experts)[None, None, :]).astype(jnp.float32)
    chosen = jnp.sum(onehot * logits[:, None, :], axis=-1)
    gates = jax.nn.softmax(chosen, axis=-1)
    flat_route = routes.reshape(-1)
    hot = (flat_route[:, None] == jnp.arange(experts)[None, :]).astype(jnp.int32)
    running = jnp.cumsum(hot, axis=0)
    within = jnp.sum(running * hot, axis=1) - 1
    slot_buf = flat_route * CAP + within
    slot_count = length * top
    slot_of_buf = (
        jnp.full((experts * CAP,), slot_count, jnp.int32)
        .at[slot_buf]
        .set(jnp.arange(slot_count, dtype=jnp.int32))
    )
    token_of_buf = slot_of_buf // top
    padded_x = jnp.concatenate([normed_two, jnp.zeros((1, width), jnp.bfloat16)], axis=0)
    x_buf = padded_x[token_of_buf].reshape(experts, CAP, width)
    cols = x_buf
    gate_up = jnp.einsum(
        "ecd,def->ecf",
        cols,
        lax.all_gather(expert_in, "fsdp", axis=0, tiled=True),
        preferred_element_type=jnp.float32,
    )
    gate_part = gate_up[..., :hidden_w]
    up_part = gate_up[..., hidden_w:]
    sigma = jax.nn.sigmoid(gate_part)
    activated = gate_part * sigma
    hidden = (activated * up_part).astype(jnp.bfloat16)
    y_buf = jnp.einsum(
        "ecf,def->ecd",
        hidden,
        lax.all_gather(expert_out, "fsdp", axis=0, tiled=True),
        preferred_element_type=jnp.float32,
    )
    y_buf = y_buf.astype(jnp.bfloat16).reshape(experts * CAP, width)
    y_slots = y_buf[slot_buf].reshape(length, top, width).astype(jnp.float32)
    mixed = (first + jnp.sum(gates[:, :, None] * y_slots, axis=1)).astype(jnp.bfloat16)
    proj_in, proj_out, router_all, gains_all = (
        lax.all_gather(in_proj, "fsdp", axis=0, tiled=True),
        lax.all_gather(out_proj, "fsdp", axis=0, tiled=True),
        lax.all_gather(router, "fsdp", axis=0, tiled=True),
        lax.all_gather(norm_gains, "fsdp", axis=0, tiled=True),
    )
    grad_out = out_grad.astype(jnp.float32)
    dgate = jnp.sum(grad_out[:, None, :] * y_slots, axis=-1)
    dy_slots = (
        (gates[:, :, None] * grad_out[:, None, :]).astype(jnp.bfloat16).reshape(slot_count, width)
    )
    padded_dy = jnp.concatenate([dy_slots, jnp.zeros((1, width), jnp.bfloat16)], axis=0)
    dy_buf = padded_dy[slot_of_buf].reshape(experts, CAP, width)
    cols = dy_buf
    dhidden = jnp.einsum(
        "ecd,def->ecf",
        cols,
        lax.all_gather(expert_out, "fsdp", axis=0, tiled=True),
        preferred_element_type=jnp.float32,
    )
    dgate_part = dhidden * up_part * sigma * (1.0 + gate_part * (1.0 - sigma))
    dup_part = dhidden * activated
    dgu = jnp.concatenate([dgate_part, dup_part], axis=-1).astype(jnp.bfloat16)
    dx_buf = jnp.einsum(
        "ecf,def->ecd",
        dgu,
        lax.all_gather(expert_in, "fsdp", axis=0, tiled=True),
        preferred_element_type=jnp.float32,
    )
    dx_expert = jnp.sum(
        dx_buf.reshape(experts * CAP, width)[slot_buf].reshape(length, top, width), axis=1
    )
    dchosen = gates * (dgate - jnp.sum(gates * dgate, axis=-1, keepdims=True))
    dlogits = jnp.sum(dchosen[:, :, None] * onehot, axis=1).astype(jnp.bfloat16)
    dnormed_two = dx_expert + contract_cols(dlogits, router_all)
    gain_two_grad = jnp.sum(dnormed_two * unit_two, axis=0)
    dunit_two = dnormed_two * gain_two
    dfirst = grad_out + scale_two * (
        dunit_two - unit_two * jnp.mean(dunit_two * unit_two, axis=-1, keepdims=True)
    )
    dres = dfirst.astype(jnp.bfloat16)
    dattn = (
        jnp.dot(dres, proj_out, preferred_element_type=jnp.float32)
        .astype(jnp.bfloat16)
        .reshape(length, KV, group, HD)
    )
    probs = jnp.exp(masked - log_total)
    probs_again = probs.astype(jnp.bfloat16)
    dprobs = jnp.einsum("qkgd,tkd->kgqt", dattn, values, preferred_element_type=jnp.float32)
    dvalues = jnp.einsum("kgqt,qkgd->tkd", probs_again, dattn, preferred_element_type=jnp.float32)
    delta = jnp.sum(probs * dprobs, axis=-1, keepdims=True)
    dscores = (probs * (dprobs - delta)).astype(jnp.bfloat16)
    dqueries = (
        jnp.einsum("kgqt,tkd->qkgd", dscores, keys, preferred_element_type=jnp.float32) * scale
    )
    dkeys = (
        jnp.einsum("kgqt,qkgd->tkd", dscores, queries, preferred_element_type=jnp.float32) * scale
    )
    dqueries = unrotate(dqueries.reshape(length, HQ, HD), cosine, sine).reshape(length, width_q)
    dkeys = unrotate(dkeys, cosine, sine).reshape(length, width_k)
    dproj = jnp.concatenate([dqueries, dkeys, dvalues.reshape(length, width_k)], axis=1).astype(
        jnp.bfloat16
    )
    dnormed = contract_cols(dproj, proj_in)
    gain_one_grad = jnp.sum(dnormed * unit_one, axis=0)
    dunit_one = dnormed * gain_one
    dinputs = dfirst + scale_one * (
        dunit_one - unit_one * jnp.mean(dunit_one * unit_one, axis=-1, keepdims=True)
    )
    tokens_grad = dinputs.astype(jnp.bfloat16)
    cols = normed
    dense_shard = lax.psum_scatter(
        jnp.concatenate([contract_rows(cols, dproj), contract_rows(dres, attn)], axis=1),
        "fsdp",
        scatter_dimension=0,
        tiled=True,
    )
    router_term = contract_rows(normed_two, dlogits)
    gains_term = jnp.stack([gain_one_grad, gain_two_grad], axis=1)
    router_shard, gains_shard = (
        lax.psum_scatter(router_term, "fsdp", scatter_dimension=0, tiled=True),
        lax.psum_scatter(gains_term, "fsdp", scatter_dimension=0, tiled=True),
    )
    part_in = jnp.einsum("ecd,ecf->def", x_buf, dgu, preferred_element_type=jnp.float32)
    part_out = jnp.einsum("ecd,ecf->def", dy_buf, hidden, preferred_element_type=jnp.float32)
    expert_shard = lax.psum_scatter(
        jnp.concatenate([part_in, part_out], axis=2), "fsdp", scatter_dimension=0, tiled=True
    )
    dense_sum, expert_sum, router_sum, gains_sum = (
        lax.psum(dense_shard.astype(jnp.bfloat16), "replica").astype(jnp.float32),
        lax.psum(expert_shard.astype(jnp.bfloat16), "replica").astype(jnp.float32),
        lax.psum(router_shard.astype(jnp.bfloat16), "replica").astype(jnp.float32),
        lax.psum(gains_shard.astype(jnp.bfloat16), "replica").astype(jnp.float32),
    )
    in_proj_grad = dense_sum[:, : width_q + 2 * width_k]
    out_proj_grad = dense_sum[:, width_q + 2 * width_k :]
    expert_in_grad = expert_sum[..., : 2 * hidden_w]
    expert_out_grad = expert_sum[..., 2 * hidden_w :]
    return (
        mixed,
        tokens_grad,
        in_proj_grad,
        out_proj_grad,
        router_sum,
        gains_sum,
        expert_in_grad,
        expert_out_grad,
    )


def solution(mesh):
    in_specs = (
        P(("replica", "fsdp"), None),
        P(("replica", "fsdp"), None),
        P(("replica", "fsdp"), None),
        P("fsdp", None),
        P("fsdp", None),
        P("fsdp", None),
        P("fsdp", None),
        P("fsdp", None, None),
        P("fsdp", None, None),
        P(("replica", "fsdp"), None),
    )
    out_specs = (
        P(("replica", "fsdp"), None),
        P(("replica", "fsdp"), None),
        P("fsdp", None),
        P("fsdp", None),
        P("fsdp", None),
        P("fsdp", None),
        P("fsdp", None, None),
        P("fsdp", None, None),
    )
    return jax.shard_map(shards, mesh=mesh, in_specs=in_specs, out_specs=out_specs, check_vma=False)
```

profile of v0, /device:TPU:1, one launch (start us, length us, event | category | flops | bytes accessed | tf_op | source)
XLA Modules:
  0.0 3847.2 jit_solution(15931663149111968714)
XLA Ops:
  18.8 18.1 all-gather
  37.0 24.3 all-gather.1
  74.3 11.9 mul.504
  95.0 16.1 all-gather.7.cloned.1.call-done
  139.1 51.9 %all-gather.9.cloned.1.call-done = bf16[1536,1536]{1,0:T(8,128)(2,1)} async-done(((bf16[192,1536]{1,0:T(8,128)(2,1)}), bf16[1536,1536]{1,0:T(8,128)(2,1)}) %all-gather.9.cloned.1.call-update) | async-done | bytes 4718608 | tf_op jit(solution)/shard_map/all_gather | solution.py:77
  207.6 9.2 gather_fusion
  216.8 17.9 gather_fusion.2
  235.3 673.4 %all-gather.11.cloned.1.call-done = bf16[1536,8,1536]{2,0,1:T(8,128)(2,1)} async-done(((bf16[192,8,1536]{2,0,1:T(8,128)(2,1)}), bf16[1536,8,1536]{2,0,1:T(8,128)(2,1)}) %all-gather.11.cloned.1.call-update) | async-done | bytes 37748752 | tf_op jit(solution)/shard_map/all_gather | solution.py:132
  908.7 24.6 fusion.71
  933.2 339.3 %all-gather.13.cloned.1.call-done = bf16[1536,8,768]{2,0,1:T(8,128)(2,1)} async-done(((bf16[192,8,768]{2,0,1:T(8,128)(2,1)}), bf16[1536,8,768]{2,0,1:T(8,128)(2,1)}) %all-gather.13.cloned.1.call-update) | async-done | bytes 18874384 | tf_op jit(solution)/shard_map/all_gather | solution.py:143
  1272.6 19.1 multiply_convert_fusion.2
  1291.6 24.0 fusion.6
  1315.6 15.4 gather_fusion.3
  1331.0 11.7 reshape.368
  1342.7 11.4 convolution_convert_fusion
  1354.1 14.3 gather_fusion.1
  1368.4 9.8 reshape.376
  1378.2 13.0 multiply_reduce_fusion
  1391.4 10.8 reduce_sum.151
  1448.2 7.9 pad_maximum_fusion.1
  1458.1 19.0 convolution_bitcast_fusion.1
  1477.1 35.0 convolution_bitcast_fusion
  1512.1 76.1 %pad_maximum_fusion = f32[1536,8,2304]{0,2,1:T(8,128)} fusion(f32[1536,8,768]{0,2,1:T(8,128)} %convolution_bitcast_fusion.1, f32[1536,8,1536]{0,2,1:T(8,128)} %convolution_bitcast_fusion), kind=kLoop, calls=%fused_computation.5 | loop fusion | flops 28311552 | bytes 226492416 | tf_op jit(solution)/shard_map/concatenate | solution.py:235
  1588.2 112.8 %copy.165 = f32[1536,8,2304]{2,1,0:T(8,128)} copy(f32[1536,8,2304]{0,2,1:T(8,128)} %pad_maximum_fusion) | data formatting | bytes 226492416 | tf_op jit(solution)/shard_map/concatenate | solution.py:235
  1702.6 8.1 fusion.21
  1713.8 101.1 %reduce-scatter.9.cloned.1.call-done = f32[192,3584]{1,0:T(8,128)} async-done(((f32[1536,3584]{1,0:T(8,128)}), f32[192,3584]{1,0:T(8,128)}) %reduce-scatter.9.cloned.1.call-update) | async-done | bytes 2752528 | tf_op jit(solution)/shard_map/reduce_scatter | solution.py:220
  1817.8 1722.5 %reduce-scatter.11.cloned.1.call-done = f32[192,8,2304]{2,1,0:T(8,128)} async-done(((f32[1536,8,2304]{2,1,0:T(8,128)}), f32[192,8,2304]{2,1,0:T(8,128)}) %reduce-scatter.11.cloned.1.call-update) | async-done | bytes 14155792 | tf_op jit(solution)/shard_map/reduce_scatter | solution.py:234
  3540.4 8.7 convert_element_type.152
  3554.1 49.4 %reduce-scatter.15.cloned.1.call-done = f32[192,2]{1,0:T(8,128)} async-done(((f32[1536,2]{1,0:T(8,128)}), f32[192,2]{1,0:T(8,128)}) %reduce-scatter.15.cloned.1.call-update) | async-done | bytes 1552
  3604.5 64.8 %reduce-scatter.13.cloned.1.call-done = f32[192,8]{1,0:T(8,128)} async-done(((f32[1536,8]{1,0:T(8,128)}), f32[192,8]{1,0:T(8,128)}) %reduce-scatter.13.cloned.1.call-update) | async-done | bytes 6160
  3670.3 7.5 all-reduce.2
  3678.9 148.4 %all-reduce.6.cloned.1.call-done = (bf16[192,3584]{1,0:T(8,128)(2,1)}, bf16[192,8,2304]{2,1,0:T(8,128)(2,1)}) async-done(((bf16[192,3584]{1,0:T(8,128)(2,1)}, bf16[192,8,2304]{2,1,0:T(8,128)(2,1)}), (bf16[192,3584]{1,0:T(8,128)(2,1)}, bf16[192,8,2304]{2,1,0:T(8,128)(2,1)})) %all-reduce.6.cloned.1.call-update) | async-done | bytes 8454160 | tf_op jit(solution)/shard_map/psum | solution.py:238
  (294 shorter events, 154.7 us)
Async XLA Ops:
  7.2 104.0 %all-gather.7.cloned.1.call-start = ((), (), s32[]{:S(2)}) async-start(), calls=%async_computation.4 | async-start | bytes 7077888 | tf_op jit(solution)/shard_map/all_gather | solution.py:76
  7.9 183.1 %all-gather.9.cloned.1.call-start = ((), (), s32[]{:S(2)}) async-start(), calls=%async_computation.5 | async-start | bytes 5308416 | tf_op jit(solution)/shard_map/all_gather | solution.py:77
  8.7 900.0 %all-gather.11.cloned.1.call-start = ((), (), s32[]{:S(2)}) async-start(), calls=%async_computation.6 | async-start | bytes 42467328 | tf_op jit(solution)/shard_map/all_gather | solution.py:132
  14.7 22.3 copy-start.72
  14.7 47.6 %copy-start.74 = (s32[1,384]{1,0:T(1,128)S(1)}, s32[1,384]{1,0:T(1,128)}, u32[]{:S(2)}) copy-start(s32[1,384]{1,0:T(1,128)} %param.11) | copy-start | bytes 4612
  14.8 1257.8 %all-gather.13.cloned.1.call-start = ((), (), s32[]{:S(2)}) async-start(), calls=%async_computation.7 | async-start | bytes 21233664 | tf_op jit(solution)/shard_map/all_gather | solution.py:143
  18.3 49.2 %copy-start.12 = (bf16[384,1536]{1,0:T(8,128)(2,1)S(1)}, bf16[384,1536]{1,0:T(8,128)(2,1)}, u32[]{:S(2)}) copy-start(bf16[384,1536]{1,0:T(8,128)(2,1)} %param.19) | copy-start | bytes 3538948
  18.3 1796.5 %reduce-scatter.9.cloned.1.call-start = ((), (), s32[]{:S(2)}) async-start(), calls=%async_computation.8 | async-start | bytes 24772608 | tf_op jit(solution)/shard_map/reduce_scatter | solution.py:220
  74.3 19.6 copy-start.8
  93.9 17.3 copy-start.50
  93.9 101.7 %copy-start.53 = (f32[1536]{0:T(1024)}, f32[1536]{0:T(1024)S(1)}, u32[]{:S(2)}) copy-start(f32[1536]{0:T(1024)S(1)} %get-tuple-element.30) | copy-start | bytes 18436
  94.2 16.9 copy-start.62
  139.1 56.4 %copy-start.36 = (bf16[2,128,6,384]{3,1,2,0:T(8,128)(2,1)}, bf16[2,128,6,384]{3,1,2,0:T(8,128)(2,1)S(1)}, u32[]{:S(2)}) copy-start(bf16[2,128,6,384]{3,1,2,0:T(8,128)(2,1)S(1)} %fusion.23) | copy-start | bytes 3538948
  216.8 17.9 copy-start.47
  1291.6 51.1 %copy-start.22 = (bf16[8,288,768]{2,1,0:T(8,128)(2,1)}, bf16[8,288,768]{2,1,0:T(8,128)(2,1)S(1)}, u32[]{:S(2)}) copy-start(bf16[8,288,768]{2,1,0:T(8,128)(2,1)S(1)} %get-tuple-element.38) | copy-start | bytes 10616836
  1291.6 24.0 copy-start.57
  1368.4 9.8 copy-start.30
  1378.2 13.1 copy-start.45
  1378.2 13.1 copy-start.61
  1378.2 13.1 copy-start.68
  1378.2 13.2 copy-start.56
  1391.4 10.9 copy-start.58
  1391.4 10.9 copy-start.4
  1391.4 10.9 copy-start.49
  1391.4 10.9 copy-start.54
  1391.4 10.8 copy-start.71
  1407.6 28.4 copy-start.1
  1413.5 12.8 slice-start
  1456.1 2084.2 %reduce-scatter.11.cloned.1.call-start = ((), (), s32[]{:S(2)}) async-start(), calls=%async_computation.9 | async-start | bytes 127401984 | tf_op jit(solution)/shard_map/reduce_scatter | solution.py:234
  1701.0 1902.5 %reduce-scatter.15.cloned.1.call-start = ((), (), s32[]{:S(2)}) async-start(), calls=%async_computation.11 | async-start | bytes 884736
  1712.0 1957.3 %reduce-scatter.13.cloned.1.call-start = ((), (), s32[]{:S(2)}) async-start(), calls=%async_computation.10 | async-start | bytes 884736
  1713.7 2113.6 %all-reduce.6.cloned.1.call-start = ((), (), s32[]{:S(2)}) async-start(), calls=%async_computation.12 | async-start | bytes 16908288 | tf_op jit(solution)/shard_map/psum | solution.py:238
  (62 other events, 235.7 us)
Sparse Core Ops, SparseCore 0:
  10.2 100.9 all-gather.6
  113.3 77.6 all-gather.8
  193.1 715.5 all-gather.10
  910.1 362.4 all-gather.12
  1456.3 358.5 reduce-scatter.8
  1819.1 1721.1 reduce-scatter.10
  3543.6 59.8 reduce-scatter.14
  3607.7 61.5 reduce-scatter.12
  3672.5 154.7 all-reduce.5
where the time goes:
time: 3860 us; the launch traced here: 3850 us
  waiting for transfers between devices  3170 us (82%)
  local copies, waits for them, and re-layouts  274 us (7%)
  matrix products  189 us (5%)
  other arithmetic  150 us (4%)
  blocking collectives  49.9 us (1%)
    reduce_scatter x1, waiting for transfers between devices, shards(): lax.psum_scatter(jnp.concatenate([part_in, part_out], axis=2), 'fsdp', sc...  1720 us
    all_gather x1, waiting for transfers between devices, shards(): lax.all_gather(expert_in, 'fsdp', axis=0, tiled=True)  673 us
    all_gather x1, waiting for transfers between devices, shards(): lax.all_gather(expert_out, 'fsdp', axis=0, tiled=True)  339 us
    psum x1, waiting for transfers between devices, shards(): lax.psum(dense_shard.astype(jnp.bfloat16), 'replica').astype(jnp.float32)  148 us
    unnamed x11, waiting for transfers between devices  116 us
    concatenate x1, local copies, waits for them, and re-layouts, shards(): jnp.concatenate([part_in, part_out], axis=2)  113 us
    reduce_scatter x1, waiting for transfers between devices, shards(): lax.psum_scatter(jnp.concatenate([contract_rows(cols, dproj), contract_ro...  101 us
  transfers between devices with their start and end apart: 9, of which 9 were waited for; matrix products, arithmetic and copies ran while one was open for 11% of the time, Pallas kernels for 0%

commit v1 on v0

v1 whole, which is shorter than its diff:
```python
import functools

import jax
import jax.numpy as jnp
from jax import lax
from jax.experimental import pallas as pl
from jax.experimental.pallas import tpu as pltpu
from jax.sharding import PartitionSpec as P

HQ = 12
KV = 2
HD = 128
GROUP = HQ // KV
WQ = HQ * HD
WK = KV * HD
EXTRA = 128
MIB = 1024 * 1024

epsilon = 1e-06
rope_base = 1000000.0
bf16 = jnp.bfloat16
f32 = jnp.float32


def rms_scale(v):
    return lax.rsqrt(jnp.mean(v * v, axis=-1, keepdims=True) + epsilon)


def tables(length):
    half = HD // 2
    freq = jnp.power(rope_base, -(jnp.arange(half, dtype=f32) * 2.0 / HD))
    angle = jnp.arange(length, dtype=f32)[:, None] * freq[None, :]
    return (jnp.cos(angle)[:, None, :], jnp.sin(angle)[:, None, :])


def rotate(v, cosine, sine):
    half = v.shape[-1] // 2
    first = v[..., :half]
    second = v[..., half:]
    return jnp.concatenate(
        [first * cosine - second * sine, second * cosine + first * sine], axis=-1
    )


def contract_rows(left, right):
    return lax.dot_general(left, right, (((0,), (0,)), ((), ())), preferred_element_type=f32)


def contract_cols(left, right):
    return lax.dot_general(left, right, (((1,), (1,)), ((), ())), preferred_element_type=f32)


def matmul(left, right):
    return lax.dot_general(left, right, (((1,), (0,)), ((), ())), preferred_element_type=f32)


class Links:
    def __init__(self, n_rep, n_fsdp):
        self.n_rep, self.n_fsdp = n_rep, n_fsdp

    def swap(self, value, d_rep, d_fsdp):
        pairs = [
            (r * self.n_fsdp + f, (r ^ d_rep) * self.n_fsdp + (f ^ d_fsdp))
            for r in range(self.n_rep)
            for f in range(self.n_fsdp)
        ]
        return lax.ppermute(value, ("replica", "fsdp"), pairs)


def place_kernel(n_src, rows, *refs):
    out = refs[n_src]
    sem = refs[n_src + 1]
    me_f = lax.axis_index("fsdp")
    me_r = lax.axis_index("replica")
    copies = []
    slot = 0
    for n, (src, layout) in enumerate(zip(refs[:n_src], PIECES)):
        for i, (j, k) in enumerate(layout):
            owner = jnp.bitwise_xor(me_f, j)
            if k is None:
                start, size = owner * (4 * rows), 4 * rows
            else:
                start = owner * (4 * rows) + jnp.bitwise_xor(me_r, k) * rows
                size = rows
            copy = pltpu.make_async_copy(
                src.at[pl.ds(i * rows, size)],
                out.at[pl.ds(pl.multiple_of(start, rows), size)],
                sem.at[slot],
            )
            copy.start()
            copies.append(copy)
            slot += 1
    for copy in copies:
        copy.wait()


PIECES = [
    [(0, None)],
    [(2, 0), (4, 0), (6, 0)],
    [(2, 2), (4, 2), (6, 2)],
    [(2, 1), (4, 1), (6, 1), (2, 3), (4, 3), (6, 3)],
    [(1, 0), (3, 0), (5, 0), (7, 0)],
    [(1, 2), (3, 2), (5, 2), (7, 2)],
    [(1, 1), (3, 1), (5, 1), (7, 1), (1, 3), (3, 3), (5, 3), (7, 3)],
]


def gather_dense(links, shard, me_r):
    rows = shard.shape[0] // 4
    quarter = lax.dynamic_slice_in_dim(shard, me_r * rows, rows, 0)
    z = [links.swap(quarter, 0, j) for j in (2, 4, 6)]
    zs = jnp.concatenate(z, 0)
    ys = links.swap(jnp.concatenate([quarter] + z, 0), 0, 1)
    zx = links.swap(zs, 2, 0)
    yx = links.swap(ys, 2, 0)
    zc = links.swap(jnp.concatenate([zs, zx], 0), 1, 0)
    yc = links.swap(jnp.concatenate([ys, yx], 0), 1, 0)
    pieces = [shard, zs, zx, zc, ys, yx, yc]
    count = sum(len(p) for p in PIECES)
    full = pl.pallas_call(
        functools.partial(place_kernel, len(pieces), rows),
        out_shape=jax.ShapeDtypeStruct((8 * shard.shape[0], shard.shape[1]), shard.dtype),
        in_specs=[pl.BlockSpec(memory_space=pl.ANY)] * len(pieces),
        out_specs=pl.BlockSpec(memory_space=pltpu.VMEM),
        scratch_shapes=[pltpu.SemaphoreType.DMA((count,))],
        compiler_params=pltpu.CompilerParams(vmem_limit_bytes=20 * MIB),
        name="place",
    )(*pieces)
    return full


def expert_kernel(nt, nw, length, width, hidden, rows, expert_of, offset_of, *refs):
    xs, gs, ws = refs[:nt], refs[nt : 2 * nt], refs[2 * nt : 2 * nt + nw]
    refs = refs[2 * nt + nw :]
    mixes, dxs, grads = refs[:nt], refs[nt : 2 * nt], refs[2 * nt : 2 * nt + nw]
    (
        wbuf, xbuf, gbuf, xt, gt_, hidg, dgu, mbuf, dbuf, acc, stage,
        sem_w, sem_x, sem_g, sem_m, sem_d, sem_s,
    ) = refs[2 * nt + nw :]
    cols = 3 * hidden
    step_cols = 256

    def load(k, slot):
        for i in range(nt):

            @pl.when(k == i)
            def _():
                pltpu.make_async_copy(xs[i], xbuf.at[slot], sem_x.at[slot]).start()
                pltpu.make_async_copy(gs[i], gbuf.at[slot], sem_g.at[slot]).start()

    def store(k, slot):
        for i in range(nt):

            @pl.when(k == i)
            def _():
                pltpu.make_async_copy(mbuf.at[slot], mixes[i], sem_m.at[slot]).start()
                pltpu.make_async_copy(dbuf.at[slot], dxs[i], sem_d.at[slot]).start()

    def stored(slot):
        pltpu.make_async_copy(mbuf.at[slot], mixes[0], sem_m.at[slot]).wait()
        pltpu.make_async_copy(dbuf.at[slot], dxs[0], sem_d.at[slot]).wait()

    for j in range(nw):
        pltpu.make_async_copy(
            ws[j], wbuf.at[pl.ds(pl.multiple_of(offset_of(j), 8), rows)], sem_w.at[j]
        ).start()
    load(0, 0)
    expert = expert_of()
    acc[...] = jnp.zeros_like(acc)
    lane = lax.broadcasted_iota(jnp.int32, (length, EXTRA), 1)
    for j in range(nw):
        pltpu.make_async_copy(
            ws[j], wbuf.at[pl.ds(pl.multiple_of(offset_of(j), 8), rows)], sem_w.at[j]
        ).wait()

    def block(k, carry):
        slot = lax.rem(k, 2)

        @pl.when(k + 1 < nt)
        def _():
            load(k + 1, 1 - slot)

        pltpu.make_async_copy(xs[0], xbuf.at[slot], sem_x.at[slot]).wait()
        pltpu.make_async_copy(gs[0], gbuf.at[slot], sem_g.at[slot]).wait()

        @pl.when(k >= 2)
        def _():
            stored(slot)

        extra = xbuf[slot, :, width:].astype(f32)
        mine = (lane == expert) | (lane == expert + 8)
        gate = jnp.sum(jnp.where(mine, extra, 0.0), axis=1, keepdims=True)
        xt[...] = xbuf[slot, :, :width].T
        gt_[...] = gbuf[slot].T

        def first(c, dgate):
            at = pl.multiple_of(c * step_cols, step_cols)
            u = matmul(xbuf[slot, :, :width], wbuf[:, pl.ds(at, step_cols)])
            up = matmul(xbuf[slot, :, :width], wbuf[:, pl.ds(hidden + at, step_cols)])
            back = matmul(gbuf[slot], wbuf[:, pl.ds(2 * hidden + at, step_cols)])
            sig = 1.0 / (1.0 + jnp.exp(-u))
            act = u * sig
            hid = act * up
            hidg[:, pl.ds(at, step_cols)] = (gate * hid).astype(bf16)
            dgate = dgate + jnp.sum(back * hid, axis=1, keepdims=True)
            dhid = gate * back
            dgu[:, pl.ds(at, step_cols)] = (
                dhid * up * sig * (1.0 + u * (1.0 - sig))
            ).astype(bf16)
            dgu[:, pl.ds(hidden + at, step_cols)] = (dhid * act).astype(bf16)
            return dgate

        dgate = lax.fori_loop(
            0, hidden // step_cols, first, jnp.zeros((length, 1), f32)
        )

        def second(c, carry):
            at = pl.multiple_of(c * step_cols, step_cols)
            mbuf[slot, :, pl.ds(at, step_cols)] = contract_cols(
                hidg[...], wbuf[pl.ds(at, step_cols), pl.ds(2 * hidden, hidden)]
            ).astype(bf16)
            dbuf[slot, :, pl.ds(at, step_cols)] = contract_cols(
                dgu[...], wbuf[pl.ds(at, step_cols), pl.ds(0, 2 * hidden)]
            ).astype(bf16)
            return carry

        lax.fori_loop(0, width // step_cols, second, 0)
        high = dgate.astype(bf16).astype(f32)
        low = dgate - high
        dbuf[slot, :, width:] = (
            jnp.where(lane == expert, high, 0.0) + jnp.where(lane == expert + 8, low, 0.0)
        ).astype(bf16)
        store(k, slot)

        def third(c, carry):
            at = pl.multiple_of(c * step_cols, step_cols)
            acc[:, pl.ds(at, step_cols)] += matmul(xt[...], dgu[:, pl.ds(at, step_cols)])
            return carry

        lax.fori_loop(0, 2 * hidden // step_cols, third, 0)

        def fourth(c, carry):
            at = pl.multiple_of(c * step_cols, step_cols)
            acc[:, pl.ds(2 * hidden + at, step_cols)] += matmul(
                gt_[...], hidg[:, pl.ds(at, step_cols)]
            )
            return carry

        lax.fori_loop(0, hidden // step_cols, fourth, 0)
        return carry

    lax.fori_loop(0, nt, block, 0)
    stored(0)
    stored(1)
    for j in range(nw):
        slot = j % 2
        if j >= 2:
            pltpu.make_async_copy(stage.at[slot], grads[j - 2], sem_s.at[slot]).wait()
        stage[slot] = acc[pl.ds(pl.multiple_of(offset_of(j), 8), rows)].astype(bf16)
        pltpu.make_async_copy(stage.at[slot], grads[j], sem_s.at[slot]).start()
    for j in range(max(0, nw - 2), nw):
        pltpu.make_async_copy(stage.at[j % 2], grads[j], sem_s.at[j % 2]).wait()


def run_expert(xs, gs, ws, expert_of, offset_of):
    nt, nw = len(xs), len(ws)
    length, width = gs[0].shape
    rows, cols = ws[0].shape
    hidden = cols // 3
    outs = (
        [jax.ShapeDtypeStruct((length, width), bf16)] * nt
        + [jax.ShapeDtypeStruct((length, width + EXTRA), bf16)] * nt
        + [jax.ShapeDtypeStruct((rows, cols), bf16)] * nw
    )
    any_spec = pl.BlockSpec(memory_space=pl.ANY)
    result = pl.pallas_call(
        functools.partial(
            expert_kernel, nt, nw, length, width, hidden, rows, expert_of, offset_of
        ),
        out_shape=outs,
        in_specs=[any_spec] * (2 * nt + nw),
        out_specs=[any_spec] * len(outs),
        scratch_shapes=[
            pltpu.VMEM((width, cols), bf16),
            pltpu.VMEM((2, length, width + EXTRA), bf16),
            pltpu.VMEM((2, length, width), bf16),
            pltpu.VMEM((width, length), bf16),
            pltpu.VMEM((width, length), bf16),
            pltpu.VMEM((length, hidden), bf16),
            pltpu.VMEM((length, 2 * hidden), bf16),
            pltpu.VMEM((2, length, width), bf16),
            pltpu.VMEM((2, length, width + EXTRA), bf16),
            pltpu.VMEM((width, cols), f32),
            pltpu.VMEM((2, rows, cols), bf16),
            pltpu.SemaphoreType.DMA((nw,)),
            pltpu.SemaphoreType.DMA((2,)),
            pltpu.SemaphoreType.DMA((2,)),
            pltpu.SemaphoreType.DMA((2,)),
            pltpu.SemaphoreType.DMA((2,)),
            pltpu.SemaphoreType.DMA((2,)),
        ],
        compiler_params=pltpu.CompilerParams(vmem_limit_bytes=60 * MIB),
        cost_estimate=pl.CostEstimate(
            flops=6 * nt * length * width * cols,
            bytes_accessed=8 * nt * length * width + 4 * width * cols,
            transcendentals=nt * length * hidden,
        ),
        name="expert",
    )(*xs, *gs, *ws)
    return result[:nt], result[nt : 2 * nt], result[2 * nt :]


class Near:
    group = ((0, 0), (1, 0), (2, 0), (3, 0), (0, 2), (1, 2), (2, 2), (3, 2))

    def __init__(self, n_rep, n_fsdp):
        self.links = Links(n_rep, n_fsdp)
        self.swap = self.links.swap

    def dense(self, shard):
        return gather_dense(self.links, shard, lax.axis_index("replica"))

    def small(self, shard):
        f = lax.axis_index("fsdp")
        got = shard[None]
        for bit in (1, 2, 4):
            other = self.swap(got, 0, bit)
            up = (f & bit) != 0
            got = jnp.concatenate(
                [jnp.where(up, other, got), jnp.where(up, got, other)], axis=0
            )
        return got

    def sum_all(self, value):
        for d in ((1, 0), (0, 1), (2, 0), (0, 2), (0, 4)):
            value = value + self.swap(value, *d)
        return value

    def spread(self, value):
        half = value.shape[0] // 2
        over_x = self.swap(value, 2, 0)
        over_z = self.swap(value, 0, 2)
        far = jnp.concatenate(
            [self.swap(over_z[:half], 2, 0), self.swap(over_x[half:], 0, 2)], axis=0
        )
        near = [value, over_x, over_z, far]
        cores = [self.swap(v, 1, 0) for v in near]
        return [near[0], cores[0], near[1], cores[1], near[2], cores[2], near[3], cores[3]]

    def collect(self, parts):
        sums = [
            (parts[k].astype(f32) + self.swap(parts[k + 1], 1, 0).astype(f32)).astype(bf16)
            for k in (0, 2, 4, 6)
        ]
        cut = sums[0].shape[0] // 2
        a = [s[:cut] for s in sums]
        b = [s[cut:] for s in sums]

        def add(u, v):
            return u.astype(f32) + v.astype(f32)

        a0 = add(a[0], self.swap(a[1], 2, 0))
        a2 = add(a[2], self.swap(a[3], 2, 0)).astype(bf16)
        b0 = add(b[0], self.swap(b[2], 0, 2))
        b1 = add(b[1], self.swap(b[3], 0, 2)).astype(bf16)
        a0 = a0 + self.swap(a2, 0, 2).astype(f32)
        b0 = b0 + self.swap(b1, 2, 0).astype(f32)
        return jnp.concatenate([a0, b0], axis=0)

    def expert_weights(self, expert_in, expert_out):
        r, f = lax.axis_index("replica"), lax.axis_index("fsdp")
        low = (f >> 1) & 1
        mine, other = [
            jnp.concatenate(
                [
                    lax.dynamic_index_in_dim(expert_in, e, 1, keepdims=False),
                    lax.dynamic_index_in_dim(expert_out, e, 1, keepdims=False),
                ],
                axis=1,
            )
            for e in (2 * r + low, 2 * r + 1 - low)
        ]
        blocks = {0: mine}
        blocks[2] = self.swap(other, 0, 2)
        blocks[4] = self.swap(mine, 0, 4)
        blocks[6] = self.swap(other, 0, 6)
        for j in (0, 2, 4, 6):
            blocks[j + 1] = self.swap(blocks[j], 0, 1)
        return [blocks[j] for j in range(8)]

    def experts(self, xs, gs, weights):
        rows = weights[0].shape[0]

        def expert_of():
            return 2 * lax.axis_index("replica") + lax.rem(lax.axis_index("fsdp") // 2, 2)

        def offset_of(j):
            return jnp.bitwise_xor(lax.axis_index("fsdp"), j) * rows

        return run_expert(xs, gs, weights, expert_of, offset_of)

    def expert_sums(self, grads):
        f = lax.axis_index("fsdp")
        r = lax.axis_index("replica")

        def add(u, v):
            return (u.astype(f32) + v.astype(f32)).astype(bf16)

        held = {j: add(grads[j], self.swap(grads[j + 1], 0, 1)) for j in (0, 2, 4, 6)}
        mine = add(held[0], self.swap(held[4], 0, 4))
        other = add(self.swap(held[2], 0, 2), self.swap(held[6], 0, 6))
        low = ((f >> 1) & 1) == 0
        pair = jnp.stack([jnp.where(low, mine, other), jnp.where(low, other, mine)])
        core = (r & 1) == 0
        peer = self.swap(pair, 1, 0)
        four = jnp.concatenate([jnp.where(core, pair, peer), jnp.where(core, peer, pair)])
        side = (r & 2) == 0
        far = self.swap(four, 2, 0)
        return jnp.concatenate([jnp.where(side, four, far), jnp.where(side, far, four)])

    def spread_quad(self, value):
        return [value] + [self.swap(value, k, 0) for k in (1, 2, 3)]

    def trade_quad(self, value):
        r = lax.axis_index("replica")
        width = value.shape[1] // 4
        return [
            (lambda part: part if k == 0 else self.swap(part, k, 0))(
                lax.dynamic_slice_in_dim(value, (r ^ k) * width, width, 1)
            )
            for k in range(4)
        ]

    def dense_sum(self, quarter):
        f = lax.axis_index("fsdp")
        r = lax.axis_index("replica")
        rows = quarter.shape[0] // 8
        blocks = [
            lax.dynamic_slice_in_dim(quarter, (f ^ j) * rows, rows, 0).astype(bf16)
            for j in range(8)
        ]

        def add(u, v):
            return (u.astype(f32) + v.astype(f32)).astype(bf16)

        got = self.swap(jnp.stack([blocks[j + 1] for j in (0, 2, 4, 6)]), 0, 1)
        held = {j: add(blocks[j], got[j // 2]) for j in (0, 2, 4, 6)}
        total = held[0].astype(f32)
        for j in (2, 4, 6):
            total = total + self.swap(held[j], 0, j).astype(f32)
        total = total.astype(bf16)
        core = (r & 1) == 0
        peer = self.swap(total, 1, 0)
        two = jnp.concatenate(
            [jnp.where(core, total, peer), jnp.where(core, peer, total)], axis=1
        )
        side = (r & 2) == 0
        far = self.swap(two, 2, 0)
        return jnp.concatenate([jnp.where(side, two, far), jnp.where(side, far, two)], axis=1)


class Wide:
    def __init__(self, n_rep, n_fsdp):
        self.n_rep, self.n_fsdp = n_rep, n_fsdp

    def dense(self, shard):
        return lax.all_gather(shard, "fsdp", axis=0, tiled=True)

    def small(self, shard):
        return lax.all_gather(shard, "fsdp", axis=0)

    def sum_all(self, value):
        return lax.psum(value, ("replica", "fsdp"))

    def spread(self, value):
        every = lax.all_gather(value, "replica", axis=0)
        return [every[k] for k in range(self.n_rep)]

    def collect(self, parts):
        return lax.psum_scatter(jnp.stack(parts), "replica", scatter_dimension=0).astype(f32)

    def expert_weights(self, expert_in, expert_out):
        r = lax.axis_index("replica")
        per = expert_in.shape[1] // self.n_rep
        out = []
        for i in range(per):
            both = jnp.concatenate(
                [
                    lax.dynamic_index_in_dim(expert_in, per * r + i, 1, keepdims=False),
                    lax.dynamic_index_in_dim(expert_out, per * r + i, 1, keepdims=False),
                ],
                axis=1,
            )
            out.append(lax.all_gather(both, "fsdp", axis=0, tiled=True))
        return out

    def experts(self, xs, gs, weights):
        per = len(weights)
        mixes, dxs, grads = None, None, []
        for i, w in enumerate(weights):

            def expert_of(i=i):
                return per * lax.axis_index("replica") + i

            mix, dx, grad = run_expert(xs, gs, [w], expert_of, lambda j: 0)
            mixes = mix if mixes is None else [a + b for a, b in zip(mixes, mix)]
            dxs = dx if dxs is None else [a + b for a, b in zip(dxs, dx)]
            grads.append(grad[0])
        return mixes, dxs, grads

    def expert_sums(self, grads):
        own = jnp.stack(
            [lax.psum_scatter(g, "fsdp", scatter_dimension=0, tiled=True) for g in grads]
        )
        return lax.all_gather(own, "replica", axis=0, tiled=True)

    def spread_quad(self, value):
        every = lax.all_gather(value, "replica", axis=0)
        return [every[k] for k in range(self.n_rep)]

    def trade_quad(self, value):
        cut = value.reshape(value.shape[0], self.n_rep, -1).transpose(1, 0, 2)
        got = lax.all_to_all(cut, "replica", 0, 0)
        return [got[k] for k in range(self.n_rep)]

    def dense_sum(self, quarter):
        own = lax.psum_scatter(quarter.astype(bf16), "fsdp", scatter_dimension=0, tiled=True)
        return lax.all_gather(own, "replica", axis=1, tiled=True)


def layer(
    net, tokens, seg_ids, routes, in_proj, out_proj, router, norm_gains, expert_in, expert_out,
    out_grad,
):
    length, width = tokens.shape
    experts = router.shape[1]
    hidden = expert_out.shape[2]
    shard = router.shape[0]
    scale = HD ** (-0.5)
    cosine, sine = tables(length)
    segment = seg_ids[0]
    place = jnp.arange(length)
    allowed = ((place[:, None] >= place[None, :]) & (segment[:, None] == segment[None, :]))[
        None, None
    ]
    tiny = jnp.concatenate(
        [router.T, norm_gains.T, jnp.zeros((16 - experts - 2, shard), bf16)], axis=0
    )
    tiny = net.small(tiny).transpose(1, 0, 2).reshape(16, width)
    router_rows = tiny[:experts]
    gain_one = tiny[experts].astype(f32)
    gain_two = tiny[experts + 1].astype(f32)
    proj_in = net.dense(in_proj)
    out_proj, proj_in = lax.optimization_barrier((out_proj, proj_in))
    proj_out = net.dense(out_proj)
    expert_in, expert_out, out_grad_sent, _ = lax.optimization_barrier(
        (expert_in, expert_out, out_grad, proj_out)
    )
    weights = net.expert_weights(expert_in, expert_out)
    gs = net.spread(out_grad_sent)

    inputs = tokens.astype(f32)
    scale_one = rms_scale(inputs)
    unit_one = inputs * scale_one
    normed = (unit_one * gain_one).astype(bf16)
    proj = matmul(normed, proj_in)
    queries = (
        rotate(proj[:, :WQ].reshape(length, HQ, HD), cosine, sine)
        .astype(bf16)
        .reshape(length, KV, GROUP, HD)
    )
    keys = rotate(proj[:, WQ : WQ + WK].reshape(length, KV, HD), cosine, sine).astype(bf16)
    values = proj[:, WQ + WK :].reshape(length, KV, HD).astype(bf16)
    scores = jnp.einsum("qkgd,tkd->kgqt", queries, keys, preferred_element_type=f32) * scale
    masked = jnp.where(allowed, scores, -1e30)
    highest = jnp.max(masked, axis=-1, keepdims=True)
    expo = jnp.exp(masked - highest)
    total = jnp.sum(expo, axis=-1, keepdims=True)
    log_total = highest + jnp.log(total)
    probs_low = (expo / total).astype(bf16)
    attn = jnp.einsum("kgqt,tkd->qkgd", probs_low, values, preferred_element_type=f32)
    attn = attn.astype(bf16).reshape(length, WQ)
    first = inputs + contract_cols(attn, proj_out)
    scale_two = rms_scale(first)
    unit_two = first * scale_two
    normed_two = (unit_two * gain_two).astype(bf16)
    logits = contract_cols(normed_two, router_rows)
    onehot = (routes[:, :, None] == jnp.arange(experts)[None, None, :]).astype(f32)
    chosen = jnp.sum(onehot * logits[:, None, :], axis=-1)
    gates = jax.nn.softmax(chosen, axis=-1)
    table = jnp.sum(gates[:, :, None] * onehot, axis=1)
    high = table.astype(bf16)
    low = (table - high.astype(f32)).astype(bf16)
    payload = jnp.concatenate(
        [normed_two, high, low, jnp.zeros((length, EXTRA - 2 * experts), bf16)], axis=1
    )
    xs = net.spread(payload)
    mixes, dxs, grads = net.experts(xs, gs, weights)
    dx = net.collect(dxs)
    mixed = (first + net.collect(mixes)).astype(bf16)

    grad_out = out_grad.astype(f32)
    dgate_all = dx[:, width : width + experts] + dx[:, width + experts : width + 2 * experts]
    dgate = jnp.sum(onehot * dgate_all[:, None, :], axis=-1)
    dchosen = gates * (dgate - jnp.sum(gates * dgate, axis=-1, keepdims=True))
    dlogits = jnp.sum(dchosen[:, :, None] * onehot, axis=1).astype(bf16)
    dnormed_two = dx[:, :width] + matmul(dlogits, router_rows)
    gain_two_grad = jnp.sum(dnormed_two * unit_two, axis=0)
    dunit_two = dnormed_two * gain_two
    dfirst = grad_out + scale_two * (
        dunit_two - unit_two * jnp.mean(dunit_two * unit_two, axis=-1, keepdims=True)
    )
    dres = dfirst.astype(bf16)
    dattn = matmul(dres, proj_out).astype(bf16).reshape(length, KV, GROUP, HD)
    probs = jnp.exp(masked - log_total)
    probs_again = probs.astype(bf16)
    dprobs = jnp.einsum("qkgd,tkd->kgqt", dattn, values, preferred_element_type=f32)
    dvalues = jnp.einsum("kgqt,qkgd->tkd", probs_again, dattn, preferred_element_type=f32)
    delta = jnp.sum(probs * dprobs, axis=-1, keepdims=True)
    dscores = (probs * (dprobs - delta)).astype(bf16)
    dqueries = jnp.einsum("kgqt,tkd->qkgd", dscores, keys, preferred_element_type=f32) * scale
    dkeys = jnp.einsum("kgqt,qkgd->tkd", dscores, queries, preferred_element_type=f32) * scale
    dqueries = rotate(dqueries.reshape(length, HQ, HD), cosine, -sine).reshape(length, WQ)
    dkeys = rotate(dkeys, cosine, -sine).reshape(length, WK)
    dproj = jnp.concatenate([dqueries, dkeys, dvalues.reshape(length, WK)], axis=1).astype(bf16)
    dnormed = contract_cols(dproj, proj_in)
    gain_one_grad = jnp.sum(dnormed * unit_one, axis=0)
    dunit_one = dnormed * gain_one
    tokens_grad = (
        dfirst
        + scale_one
        * (dunit_one - unit_one * jnp.mean(dunit_one * unit_one, axis=-1, keepdims=True))
    ).astype(bf16)

    expert_sum = net.expert_sums(grads).transpose(1, 0, 2)
    all_normed = jnp.concatenate(net.spread_quad(normed), axis=0)
    part_attn = jnp.concatenate(net.trade_quad(attn), axis=0)
    all_dres = jnp.concatenate(net.spread_quad(dres), axis=0)
    out_proj_grad = net.dense_sum(contract_rows(all_dres, part_attn)).astype(f32)
    part_dproj = jnp.concatenate(net.trade_quad(dproj), axis=0)
    in_proj_grad = net.dense_sum(contract_rows(all_normed, part_dproj)).astype(f32)

    terms = jnp.concatenate(
        [
            contract_rows(dlogits, normed_two),
            gain_one_grad[None],
            gain_two_grad[None],
            jnp.zeros((16 - experts - 2, width), f32),
        ],
        axis=0,
    )
    terms = lax.dynamic_slice_in_dim(
        net.sum_all(terms), lax.axis_index("fsdp") * shard, shard, 1
    ).T
    return (
        mixed,
        tokens_grad,
        in_proj_grad,
        out_proj_grad,
        terms[:, :experts],
        terms[:, experts : experts + 2],
        expert_sum[..., : 2 * hidden].astype(f32),
        expert_sum[..., 2 * hidden :].astype(f32),
    )


def solution(mesh):
    n_rep, n_fsdp = mesh.shape["replica"], mesh.shape["fsdp"]
    net = Near(n_rep, n_fsdp) if (n_rep, n_fsdp) == (4, 8) else Wide(n_rep, n_fsdp)
    both = P(("replica", "fsdp"), None)
    fsdp, deep = P("fsdp", None), P("fsdp", None, None)
    return jax.shard_map(
        functools.partial(layer, net),
        mesh=mesh,
        in_specs=(both, both, both, fsdp, fsdp, fsdp, fsdp, deep, deep, both),
        out_specs=(both, both, fsdp, fsdp, fsdp, fsdp, deep, deep),
        check_vma=False,
    )
```

time: 3860 us -> 964 us (0.25)
  waiting for transfers between devices: 3170 us -> 474 us
  local copies, waits for them, and re-layouts: 274 us -> 67.4 us
  starting transfers between devices: 0.58 us -> 167 us
  matrix products: 189 us -> 48.1 us
  Pallas kernels: 0 us -> 129 us
  other arithmetic: 150 us -> 70.5 us
  blocking collectives: 49.9 us -> 0 us
    reduce_scatter x2 -> x0, waiting for transfers between devices: 1820 us -> none  [the longest x1 1720 us: shards(): lax.psum_scatter(jnp.concatenate([part_in, part_out], axis=2), 'fsdp', sc...]
    all_gather x4 -> x0, waiting for transfers between devices: 1080 us -> none  [the longest x1 673 us: shards(): lax.all_gather(expert_in, 'fsdp', axis=0, tiled=True)]
    ppermute x0 -> x100, waiting for transfers between devices: none -> 474 us  [swap(): return lax.ppermute(value, ('replica', 'fsdp'), pairs)]
    ppermute x0 -> x100, starting transfers between devices: none -> 167 us  [swap(): return lax.ppermute(value, ('replica', 'fsdp'), pairs)]
    psum x1 -> x0, waiting for transfers between devices: 148 us -> none  [shards(): lax.psum(dense_shard.astype(jnp.bfloat16), 'replica').astype(jnp.float32)]
    dot_general x15 -> x9, matrix products: 163 us -> 30.3 us  [the longest x3 10.1 us: matmul(): lax.dot_general(left, right, (((1,), (0,)), ((), ())), preferred_element_...]
    pallas_call x0 -> x3, Pallas kernels: none -> 129 us  [the longest x1 117 us: run_expert(): pl.pallas_call(functools.partial(expert_kernel, nt, nw, length, width, hi...]
    unnamed x11 -> x0, waiting for transfers between devices: 116 us -> none
  transfers between devices with their start and end apart: 9 -> 100, of which waited for: 9 -> 39; matrix products, arithmetic and copies ran while one was open for 11% -> 14% of each run, Pallas kernels for 0% -> 0%
where the time goes in v1:
time: 964 us; the launch traced here: 959 us
  waiting for transfers between devices  474 us (49%)
  starting transfers between devices  167 us (17%)
  Pallas kernels  129 us (13%)
  other arithmetic  70.5 us (7%)
  local copies, waits for them, and re-layouts  67.4 us (7%)
  matrix products  48.1 us (5%)
    ppermute x100, waiting for transfers between devices, swap(): return lax.ppermute(value, ('replica', 'fsdp'), pairs)  474 us
    ppermute x100, starting transfers between devices, swap(): return lax.ppermute(value, ('replica', 'fsdp'), pairs)  167 us
    pallas_call x1, Pallas kernels, run_expert(): pl.pallas_call(functools.partial(expert_kernel, nt, nw, length, width, hi...  117 us
    unnamed x234, local copies, waits for them, and re-layouts  28.9 us
  transfers between devices with their start and end apart: 100, of which 39 were waited for; matrix products, arithmetic and copies ran while one was open for 14% of the time, Pallas kernels for 0%

profile of v1, /device:TPU:1, one launch (start us, length us, event | category | flops | bytes accessed | tf_op | source)
XLA Modules:
  0.0 958.6 jit_solution(1232972470176905886)
XLA Ops:
  11.7 7.1 collective-permute-done.5
  26.9 8.0 collective-permute-done.8.refs_4_
  36.5 13.3 %collective-permute-done.9.refs_5_ = bf16[192,2048]{1,0:T(8,128)(2,1)S(1)} collective-permute-done((bf16[192,2048]{1,0:T(8,128)(2,1)S(1)}, bf16[192,2048]{1,0:T(8,128)(2,1)S(1)}, u32[]{:S(2)}, u32[]{:S(2)}) %collective-permute-start.9) | collective-permute-done | bytes 786464 | tf_op jit(solution)/shard_map/ppermute | solution.py:67
  51.1 9.6 collective-permute-start.10
  118.8 8.8 collective-permute-done.16.refs_4_
  132.7 8.3 collective-permute-done.17.refs_5_
  183.9 7.7 collective-permute-done.36.refs_18_
  192.8 18.7 %collective-permute-done.40.refs_22_ = bf16[192,2304]{1,0:T(8,128)(2,1)} collective-permute-done((bf16[192,2304]{1,0:T(8,128)(2,1)}, bf16[192,2304]{1,0:T(8,128)(2,1)}, u32[]{:S(2)}, u32[]{:S(2)}) %collective-permute-start.40) | collective-permute-done | bytes 884768 | tf_op jit(solution)/shard_map/ppermute | solution.py:67
  211.5 17.7 %collective-permute-start.30 = (bf16[384,1536]{1,0:T(8,128)(2,1)}, bf16[384,1536]{1,0:T(8,128)(2,1)S(1)}, u32[]{:S(2)}, u32[]{:S(2)}) collective-permute-start(bf16[384,1536]{1,0:T(8,128)(2,1)} %refs_8_), channel_id=1, source_target_pairs={{0,2},{1,3},{2,0},{3,1},{4,6},{5,7},{6,4},{7,5},{8,10},{9,11},{10,... | collective-permute-start | bytes 3538952 | tf_op jit(solution)/shard_map/ppermute | solution.py:67
  229.3 20.2 %collective-permute-done.38.refs_20_ = bf16[192,2304]{1,0:T(8,128)(2,1)} collective-permute-done((bf16[192,2304]{1,0:T(8,128)(2,1)}, bf16[192,2304]{1,0:T(8,128)(2,1)}, u32[]{:S(2)}, u32[]{:S(2)}) %collective-permute-start.38) | collective-permute-done | bytes 884768 | tf_op jit(solution)/shard_map/ppermute | solution.py:67
  258.2 23.9 %collective-permute-done.30.refs_12_ = bf16[384,1536]{1,0:T(8,128)(2,1)S(1)} collective-permute-done((bf16[384,1536]{1,0:T(8,128)(2,1)}, bf16[384,1536]{1,0:T(8,128)(2,1)S(1)}, u32[]{:S(2)}, u32[]{:S(2)}) %collective-permute-start.30) | collective-permute-done | bytes 1179680 | tf_op jit(solution)/shard_map/ppermute | solution.py:67
  287.0 22.8 %collective-permute-done.32 = bf16[192,1536]{1,0:T(8,128)(2,1)S(1)} collective-permute-done((bf16[192,1536]{1,0:T(8,128)(2,1)S(1)}, bf16[192,1536]{1,0:T(8,128)(2,1)S(1)}, u32[]{:S(2)}, u32[]{:S(2)}) %collective-permute-start.32) | collective-permute-done | bytes 589856 | tf_op jit(solution)/shard_map/ppermute | solution.py:67
  314.5 14.9 %collective-permute-done.41.refs_23_ = bf16[192,2304]{1,0:T(8,128)(2,1)S(1)} collective-permute-done((bf16[192,2304]{1,0:T(8,128)(2,1)}, bf16[192,2304]{1,0:T(8,128)(2,1)S(1)}, u32[]{:S(2)}, u32[]{:S(2)}) %collective-permute-start.41) | collective-permute-done | bytes 884768 | tf_op jit(solution)/shard_map/ppermute | solution.py:67
  334.4 14.0 %collective-permute-done.39.refs_21_ = bf16[192,2304]{1,0:T(8,128)(2,1)S(1)} collective-permute-done((bf16[192,2304]{1,0:T(8,128)(2,1)}, bf16[192,2304]{1,0:T(8,128)(2,1)S(1)}, u32[]{:S(2)}, u32[]{:S(2)}) %collective-permute-start.39) | collective-permute-done | bytes 884768 | tf_op jit(solution)/shard_map/ppermute | solution.py:67
  358.2 117.2 %expert.1 = (bf16[384,1536]{1,0:T(8,128)(2,1)}, bf16[384,1536]{1,0:T(8,128)(2,1)}, bf16[384,1536]{1,0:T(8,128)(2,1)}, bf16[384,1536]{1,0:T(8,128)(2,1)}, bf16[38...) custom-call(bf16[384,1664]{1,0:T(8,128)(2,1)} %concatenate.133.refs_, ...), custom_call_target="tpu_custom_call" | custom-call | flops 65229815808 | bytes 51904512 | tf_op jit(solution)/shard_map/expert/pallas_call | solution.py:276
  483.9 12.8 %collective-permute-done.92 = bf16[192,2304]{1,0:T(8,128)(2,1)} collective-permute-done((bf16[192,2304]{1,0:T(8,128)(2,1)}, bf16[192,2304]{1,0:T(8,128)(2,1)}, u32[]{:S(2)}, u32[]{:S(2)}) %collective-permute-start.92) | collective-permute-done | bytes 884768 | tf_op jit(solution)/shard_map/ppermute | solution.py:67
  500.1 15.4 %collective-permute-done.94 = bf16[192,2304]{1,0:T(8,128)(2,1)S(1)} collective-permute-done((bf16[192,2304]{1,0:T(8,128)(2,1)}, bf16[192,2304]{1,0:T(8,128)(2,1)S(1)}, u32[]{:S(2)}, u32[]{:S(2)}) %collective-permute-start.94) | collective-permute-done | bytes 884768 | tf_op jit(solution)/shard_map/ppermute | solution.py:67
  517.8 16.7 %collective-permute-done.96 = bf16[192,2304]{1,0:T(8,128)(2,1)S(1)} collective-permute-done((bf16[192,2304]{1,0:T(8,128)(2,1)}, bf16[192,2304]{1,0:T(8,128)(2,1)S(1)}, u32[]{:S(2)}, u32[]{:S(2)}) %collective-permute-start.96) | collective-permute-done | bytes 884768 | tf_op jit(solution)/shard_map/ppermute | solution.py:67
  552.0 11.8 %collective-permute-done.57 = bf16[192,1664]{1,0:T(8,128)(2,1)S(1)} collective-permute-done((bf16[192,1664]{1,0:T(8,128)(2,1)S(1)}, bf16[192,1664]{1,0:T(8,128)(2,1)S(1)}, u32[]{:S(2)}, u32[]{:S(2)}) %collective-permute-start.57) | collective-permute-done | bytes 639008 | tf_op jit(solution)/shard_map/ppermute | solution.py:67
  565.1 35.8 %collective-permute-done.60 = bf16[192,1664]{1,0:T(8,128)(2,1)S(1)} collective-permute-done((bf16[192,1664]{1,0:T(8,128)(2,1)S(1)}, bf16[192,1664]{1,0:T(8,128)(2,1)S(1)}, u32[]{:S(2)}, u32[]{:S(2)}) %collective-permute-start.60) | collective-permute-done | bytes 639008 | tf_op jit(solution)/shard_map/ppermute | solution.py:67
  603.9 15.1 %collective-permute-done.97 = bf16[192,2304]{1,0:T(8,128)(2,1)S(1)} collective-permute-done((bf16[192,2304]{1,0:T(8,128)(2,1)S(1)}, bf16[192,2304]{1,0:T(8,128)(2,1)S(1)}, u32[]{:S(2)}, u32[]{:S(2)}) %collective-permute-start.97) | collective-permute-done | bytes 884768 | tf_op jit(solution)/shard_map/ppermute | solution.py:67
  622.0 6.9 collective-permute-done.50
  628.9 8.8 collective-permute-start.62
  644.0 12.3 %collective-permute-done.58 = bf16[192,1664]{1,0:T(8,128)(2,1)S(1)} collective-permute-done((bf16[192,1664]{1,0:T(8,128)(2,1)S(1)}, bf16[192,1664]{1,0:T(8,128)(2,1)S(1)}, u32[]{:S(2)}, u32[]{:S(2)}) %collective-permute-start.58) | collective-permute-done | bytes 639008 | tf_op jit(solution)/shard_map/ppermute | solution.py:67
  674.1 7.6 fusion
  728.3 25.5 %collective-permute-done.88 = f32[16,1536]{1,0:T(8,128)S(1)} collective-permute-done((f32[16,1536]{1,0:T(8,128)S(1)}, f32[16,1536]{1,0:T(8,128)S(1)}, u32[]{:S(2)}, u32[]{:S(2)}) %collective-permute-start.88) | collective-permute-done | bytes 98336 | tf_op jit(solution)/shard_map/ppermute | solution.py:67
  763.8 7.7 collective-permute-done.67
  780.8 53.3 %collective-permute-done.79 = bf16[384,384]{0,1:T(8,128)(2,1)S(1)} collective-permute-done((bf16[384,384]{0,1:T(8,128)(2,1)S(1)}, bf16[384,384]{0,1:T(8,128)(2,1)S(1)}, u32[]{:S(2)}, u32[]{:S(2)}) %collective-permute-start.79) | collective-permute-done | bytes 294944 | tf_op jit(solution)/shard_map/ppermute | solution.py:67
  839.7 13.7 %collective-permute-done.68 = bf16[4,192,512]{2,1,0:T(8,128)(2,1)S(1)} collective-permute-done((bf16[4,192,512]{2,1,0:T(8,128)(2,1)S(1)}, bf16[4,192,512]{2,1,0:T(8,128)(2,1)S(1)}, u32[]{:S(2)}, u32[]{:S(2)}) %collective-permute-start.68) | collective-permute-done | bytes 786464 | tf_op jit(solution)/shard_map/ppermute | solution.py:67
  862.9 10.0 %collective-permute-done.70 = bf16[192,512]{1,0:T(8,128)(2,1)} collective-permute-done((bf16[192,512]{1,0:T(8,128)(2,1)S(1)}, bf16[192,512]{1,0:T(8,128)(2,1)}, u32[]{:S(2)}, u32[]{:S(2)}) %collective-permute-start.70) | collective-permute-done | bytes 196640 | tf_op jit(solution)/shard_map/ppermute | solution.py:67
  899.4 22.1 %collective-permute-done.73 = bf16[192,1024]{1,0:T(8,128)(2,1)S(1)} collective-permute-done((bf16[192,1024]{1,0:T(8,128)(2,1)S(1)}, bf16[192,1024]{1,0:T(8,128)(2,1)S(1)}, u32[]{:S(2)}, u32[]{:S(2)}) %collective-permute-start.73) | collective-permute-done | bytes 393248 | tf_op jit(solution)/shard_map/ppermute | solution.py:67
  944.3 9.2 copy.127
  (574 shorter events, 358.9 us)
Async XLA Ops:
  170.3 41.3 %collective-permute-start.40 = (bf16[192,2304]{1,0:T(8,128)(2,1)}, bf16[192,2304]{1,0:T(8,128)(2,1)}, u32[]{:S(2)}, u32[]{:S(2)}) collective-permute-start(bf16[192,2304]{1,0:T(8,128)(2,1)} %pad_maximum_fusion.10), channel_id=1, source_target_pairs={{0,6},{1,7},{2,4},{3,5},{4,2},{5,3},{6,0},{7,1},{8,14},{9,15},{10,... | collective-permute-start | bytes 2654216 | tf_op jit(solution)/shard_map/ppermute | solution.py:67
  173.4 76.0 %collective-permute-start.38 = (bf16[192,2304]{1,0:T(8,128)(2,1)}, bf16[192,2304]{1,0:T(8,128)(2,1)}, u32[]{:S(2)}, u32[]{:S(2)}) collective-permute-start(bf16[192,2304]{1,0:T(8,128)(2,1)} %pad_maximum_fusion.9.refs_16_), channel_id=1, source_target_pairs={{0,4},{1,5},{2,6},{3,7},{4,0},{5,1},{6,2},{7,3},{8,12},{9,13},{10,... | collective-permute-start | bytes 2654216 | tf_op jit(solution)/shard_map/ppermute | solution.py:67
  181.6 75.2 %collective-permute-start.22 = (bf16[384,1664]{1,0:T(8,128)(2,1)}, bf16[384,1664]{1,0:T(8,128)(2,1)S(1)}, u32[]{:S(2)}, u32[]{:S(2)}) collective-permute-start(bf16[384,1664]{1,0:T(8,128)(2,1)} %concatenate.133.refs_0_), channel_id=1, source_target_pairs={{0,2},{1,3},{2,0},{3,1},{4,6},{5,7},{6,4},{7,5},{8,10},{9,11},{10,... | collective-permute-start | bytes 3833864 | tf_op jit(solution)/shard_map/ppermute | solution.py:67
  182.7 67.9 %collective-permute-start.35 = (bf16[192,2304]{1,0:T(8,128)(2,1)}, bf16[192,2304]{1,0:T(8,128)(2,1)}, u32[]{:S(2)}, u32[]{:S(2)}) collective-permute-start(bf16[192,2304]{1,0:T(8,128)(2,1)} %pad_maximum_fusion.9.refs_16_), channel_id=1, source_target_pairs={{0,1},{1,0},{2,3},{3,2},{4,5},{5,4},{6,7},{7,6},{8,9},{9,8},{10,11... | collective-permute-start | bytes 2654216 | tf_op jit(solution)/shard_map/ppermute | solution.py:67
  191.6 91.7 %collective-permute-start.20 = (bf16[384,1664]{1,0:T(8,128)(2,1)}, bf16[384,1664]{1,0:T(8,128)(2,1)S(1)}, u32[]{:S(2)}, u32[]{:S(2)}) collective-permute-start(bf16[384,1664]{1,0:T(8,128)(2,1)} %concatenate.133.refs_0_), channel_id=1, source_target_pairs={{0,16},{1,17},{2,18},{3,19},{4,20},{5,21},{6,22},{7,23},{8,24},{9,... | collective-permute-start | bytes 3833864 | tf_op jit(solution)/shard_map/ppermute | solution.py:67
  211.5 70.6 %collective-permute-start.30 = (bf16[384,1536]{1,0:T(8,128)(2,1)}, bf16[384,1536]{1,0:T(8,128)(2,1)S(1)}, u32[]{:S(2)}, u32[]{:S(2)}) collective-permute-start(bf16[384,1536]{1,0:T(8,128)(2,1)} %refs_8_), channel_id=1, source_target_pairs={{0,2},{1,3},{2,0},{3,1},{4,6},{5,7},{6,4},{7,5},{8,10},{9,11},{10,... | collective-permute-start | bytes 3538952 | tf_op jit(solution)/shard_map/ppermute | solution.py:67
  284.1 67.1 %collective-permute-start.29 = (bf16[384,1536]{1,0:T(8,128)(2,1)S(1)}, bf16[384,1536]{1,0:T(8,128)(2,1)S(1)}, u32[]{:S(2)}, u32[]{:S(2)}) collective-permute-start(bf16[384,1536]{1,0:T(8,128)(2,1)S(1)} %collective-permute-done.28.refs_10_), channel_id=1, source_target_pairs={{0,8},{1,9},{2,10},{3,11},{4,12},{5,13},{6,14},{7,15},{8,0},{9,1},... | collective-permute-start | bytes 3538952 | tf_op jit(solution)/shard_map/ppermute | solution.py:67
  311.3 39.7 %collective-permute-start.33 = (bf16[192,1536]{1,0:T(8,128)(2,1)S(1)}, bf16[192,1536]{1,0:T(8,128)(2,1)S(1)}, u32[]{:S(2)}, u32[]{:S(2)}) collective-permute-start(bf16[192,1536]{1,0:T(8,128)(2,1)S(1)} %slice.216), channel_id=1, source_target_pairs={{0,2},{1,3},{2,0},{3,1},{4,6},{5,7},{6,4},{7,5},{8,10},{9,11},{10,... | collective-permute-start | bytes 1769480 | tf_op jit(solution)/shard_map/ppermute | solution.py:67
  311.9 39.9 %collective-permute-start.31 = (bf16[384,1536]{1,0:T(8,128)(2,1)S(1)}, bf16[384,1536]{1,0:T(8,128)(2,1)S(1)}, u32[]{:S(2)}, u32[]{:S(2)}) collective-permute-start(bf16[384,1536]{1,0:T(8,128)(2,1)S(1)} %collective-permute-done.30.refs_12_), channel_id=1, source_target_pairs={{0,8},{1,9},{2,10},{3,11},{4,12},{5,13},{6,14},{7,15},{8,0},{9,1},... | collective-permute-start | bytes 3538952 | tf_op jit(solution)/shard_map/ppermute | solution.py:67
  481.0 53.5 %collective-permute-start.96 = (bf16[192,2304]{1,0:T(8,128)(2,1)}, bf16[192,2304]{1,0:T(8,128)(2,1)S(1)}, u32[]{:S(2)}, u32[]{:S(2)}) collective-permute-start(bf16[192,2304]{1,0:T(8,128)(2,1)} %get-tuple-element.65), channel_id=1, source_target_pairs={{0,1},{1,0},{2,3},{3,2},{4,5},{5,4},{6,7},{7,6},{8,9},{9,8},{10,11... | collective-permute-start | bytes 2654216 | tf_op jit(solution)/shard_map/ppermute | solution.py:67
  482.1 119.0 %collective-permute-start.91 = (bf16[192,2304]{1,0:T(8,128)(2,1)}, bf16[192,2304]{1,0:T(8,128)(2,1)S(1)}, u32[]{:S(2)}, u32[]{:S(2)}) collective-permute-start(bf16[192,2304]{1,0:T(8,128)(2,1)} %get-tuple-element.59), channel_id=1, source_target_pairs={{0,1},{1,0},{2,3},{3,2},{4,5},{5,4},{6,7},{7,6},{8,9},{9,8},{10,11... | collective-permute-start | bytes 2654216 | tf_op jit(solution)/shard_map/ppermute | solution.py:67
  482.5 64.7 %collective-permute-start.55 = (bf16[384,1664]{1,0:T(8,128)(2,1)S(1)}, bf16[384,1664]{1,0:T(8,128)(2,1)S(1)}, u32[]{:S(2)}, u32[]{:S(2)}) collective-permute-start(bf16[384,1664]{1,0:T(8,128)(2,1)S(1)} %copy-done.90), channel_id=1, source_target_pairs={{0,8},{1,9},{2,10},{3,11},{4,12},{5,13},{6,14},{7,15},{8,0},{9,1},... | collective-permute-start | bytes 3833864 | tf_op jit(solution)/shard_map/ppermute | solution.py:67
  496.7 40.1 %collective-permute-start.43 = (bf16[384,1536]{1,0:T(8,128)(2,1)}, bf16[384,1536]{1,0:T(8,128)(2,1)S(1)}, u32[]{:S(2)}, u32[]{:S(2)}) collective-permute-start(bf16[384,1536]{1,0:T(8,128)(2,1)} %get-tuple-element.45), channel_id=1, source_target_pairs={{0,8},{1,9},{2,10},{3,11},{4,12},{5,13},{6,14},{7,15},{8,0},{9,1},... | collective-permute-start | bytes 3538952 | tf_op jit(solution)/shard_map/ppermute | solution.py:67
  545.5 57.1 %collective-permute-start.93 = (bf16[192,2304]{1,0:T(8,128)(2,1)S(1)}, bf16[192,2304]{1,0:T(8,128)(2,1)S(1)}, u32[]{:S(2)}, u32[]{:S(2)}) collective-permute-start(bf16[192,2304]{1,0:T(8,128)(2,1)S(1)} %add_convert_fusion.12), channel_id=1, source_target_pairs={{0,4},{1,5},{2,6},{3,7},{4,0},{5,1},{6,2},{7,3},{8,12},{9,13},{10,... | collective-permute-start | bytes 2654216 | tf_op jit(solution)/shard_map/ppermute | solution.py:67
  547.2 56.6 %collective-permute-start.95 = (bf16[192,2304]{1,0:T(8,128)(2,1)S(1)}, bf16[192,2304]{1,0:T(8,128)(2,1)S(1)}, u32[]{:S(2)}, u32[]{:S(2)}) collective-permute-start(bf16[192,2304]{1,0:T(8,128)(2,1)S(1)} %add_convert_fusion.10), channel_id=1, source_target_pairs={{0,2},{1,3},{2,0},{3,1},{4,6},{5,7},{6,4},{7,5},{8,10},{9,11},{10,... | collective-permute-start | bytes 2654216 | tf_op jit(solution)/shard_map/ppermute | solution.py:67
  550.4 50.5 %collective-permute-start.60 = (bf16[192,1664]{1,0:T(8,128)(2,1)S(1)}, bf16[192,1664]{1,0:T(8,128)(2,1)S(1)}, u32[]{:S(2)}, u32[]{:S(2)}) collective-permute-start(bf16[192,1664]{1,0:T(8,128)(2,1)S(1)} %get-tuple-element.138), channel_id=1, source_target_pairs={{0,2},{1,3},{2,0},{3,1},{4,6},{5,7},{6,4},{7,5},{8,10},{9,11},{10,... | collective-permute-start | bytes 1916936 | tf_op jit(solution)/shard_map/ppermute | solution.py:67
  563.8 55.1 %collective-permute-start.97 = (bf16[192,2304]{1,0:T(8,128)(2,1)S(1)}, bf16[192,2304]{1,0:T(8,128)(2,1)S(1)}, u32[]{:S(2)}, u32[]{:S(2)}) collective-permute-start(bf16[192,2304]{1,0:T(8,128)(2,1)S(1)} %add_convert_fusion.9), channel_id=1, source_target_pairs={{0,6},{1,7},{2,4},{3,5},{4,2},{5,3},{6,0},{7,1},{8,14},{9,15},{10,... | collective-permute-start | bytes 2654216 | tf_op jit(solution)/shard_map/ppermute | solution.py:67
  601.1 41.5 %collective-permute-start.59 = (bf16[192,1664]{1,0:T(8,128)(2,1)S(1)}, bf16[192,1664]{1,0:T(8,128)(2,1)S(1)}, u32[]{:S(2)}, u32[]{:S(2)}) collective-permute-start(bf16[192,1664]{1,0:T(8,128)(2,1)S(1)} %slice.230), channel_id=1, source_target_pairs={{0,2},{1,3},{2,0},{3,1},{4,6},{5,7},{6,4},{7,5},{8,10},{9,11},{10,... | collective-permute-start | bytes 1916936 | tf_op jit(solution)/shard_map/ppermute | solution.py:67
  602.6 41.1 %collective-permute-start.54 = (bf16[192,1664]{1,0:T(8,128)(2,1)S(1)}, bf16[192,1664]{1,0:T(8,128)(2,1)S(1)}, u32[]{:S(2)}, u32[]{:S(2)}) collective-permute-start(bf16[192,1664]{1,0:T(8,128)(2,1)S(1)} %slice.226), channel_id=1, source_target_pairs={{0,16},{1,17},{2,18},{3,19},{4,20},{5,21},{6,22},{7,23},{8,24},{9,... | collective-permute-start | bytes 1916936 | tf_op jit(solution)/shard_map/ppermute | solution.py:67
  603.8 52.6 %collective-permute-start.58 = (bf16[192,1664]{1,0:T(8,128)(2,1)S(1)}, bf16[192,1664]{1,0:T(8,128)(2,1)S(1)}, u32[]{:S(2)}, u32[]{:S(2)}) collective-permute-start(bf16[192,1664]{1,0:T(8,128)(2,1)S(1)} %add_convert_fusion.15), channel_id=1, source_target_pairs={{0,2},{1,3},{2,0},{3,1},{4,6},{5,7},{6,4},{7,5},{8,10},{9,11},{10,... | collective-permute-start | bytes 1916936 | tf_op jit(solution)/shard_map/ppermute | solution.py:67
  628.9 82.9 %collective-permute-start.62 = (bf16[384,1536]{1,0:T(8,128)(2,1)}, bf16[384,1536]{1,0:T(8,128)(2,1)}, u32[]{:S(2)}, u32[]{:S(2)}) collective-permute-start(bf16[384,1536]{1,0:T(8,128)(2,1)} %fusion.31), channel_id=1, source_target_pairs={{0,8},{1,9},{2,10},{3,11},{4,12},{5,13},{6,14},{7,15},{8,0},{9,1},... | collective-permute-start | bytes 3538952 | tf_op jit(solution)/shard_map/ppermute | solution.py:67
  642.6 71.0 %collective-permute-start.63 = (bf16[384,1536]{1,0:T(8,128)(2,1)}, bf16[384,1536]{1,0:T(8,128)(2,1)}, u32[]{:S(2)}, u32[]{:S(2)}) collective-permute-start(bf16[384,1536]{1,0:T(8,128)(2,1)} %fusion.31), channel_id=1, source_target_pairs={{0,16},{1,17},{2,18},{3,19},{4,20},{5,21},{6,22},{7,23},{8,24},{9,... | collective-permute-start | bytes 3538952 | tf_op jit(solution)/shard_map/ppermute | solution.py:67
  643.8 76.7 %collective-permute-start.44 = (bf16[192,1536]{1,0:T(8,128)(2,1)}, bf16[192,1536]{1,0:T(8,128)(2,1)}, u32[]{:S(2)}, u32[]{:S(2)}) collective-permute-start(bf16[192,1536]{1,0:T(8,128)(2,1)} %slice.218), channel_id=1, source_target_pairs={{0,16},{1,17},{2,18},{3,19},{4,20},{5,21},{6,22},{7,23},{8,24},{9,... | collective-permute-start | bytes 1769480 | tf_op jit(solution)/shard_map/ppermute | solution.py:67
  656.4 48.3 %collective-permute-start.47 = (bf16[192,1536]{1,0:T(8,128)(2,1)}, bf16[192,1536]{1,0:T(8,128)(2,1)}, u32[]{:S(2)}, u32[]{:S(2)}) collective-permute-start(bf16[192,1536]{1,0:T(8,128)(2,1)} %get-tuple-element.150), channel_id=1, source_target_pairs={{0,16},{1,17},{2,18},{3,19},{4,20},{5,21},{6,22},{7,23},{8,24},{9,... | collective-permute-start | bytes 1769480 | tf_op jit(solution)/shard_map/ppermute | solution.py:67
  657.6 63.2 %collective-permute-start.49 = (bf16[192,1536]{1,0:T(8,128)(2,1)}, bf16[192,1536]{1,0:T(8,128)(2,1)}, u32[]{:S(2)}, u32[]{:S(2)}) collective-permute-start(bf16[192,1536]{1,0:T(8,128)(2,1)} %slice.222), channel_id=1, source_target_pairs={{0,2},{1,3},{2,0},{3,1},{4,6},{5,7},{6,4},{7,5},{8,10},{9,11},{10,... | collective-permute-start | bytes 1769480 | tf_op jit(solution)/shard_map/ppermute | solution.py:67
  720.8 55.7 %collective-permute-start.98 = (bf16[2,192,2304]{2,1,0:T(8,128)(2,1)S(1)}, bf16[2,192,2304]{2,1,0:T(8,128)(2,1)S(1)}, u32[]{:S(2)}, u32[]{:S(2)}) collective-permute-start(bf16[2,192,2304]{2,1,0:T(8,128)(2,1)S(1)} %pad_maximum_fusion.1), channel_id=1, source_target_pairs={{0,8},{1,9},{2,10},{3,11},{4,12},{5,13},{6,14},{7,15},{8,0},{9,1},... | collective-permute-start | bytes 5308424 | tf_op jit(solution)/shard_map/ppermute | solution.py:67
  762.2 73.2 %collective-permute-start.74 = (bf16[384,1536]{1,0:T(8,128)(2,1)S(1)}, bf16[384,1536]{1,0:T(8,128)(2,1)S(1)}, u32[]{:S(2)}, u32[]{:S(2)}) collective-permute-start(bf16[384,1536]{1,0:T(8,128)(2,1)S(1)} %copy-done.45), channel_id=1, source_target_pairs={{0,8},{1,9},{2,10},{3,11},{4,12},{5,13},{6,14},{7,15},{8,0},{9,1},... | collective-permute-start | bytes 3538952 | tf_op jit(solution)/shard_map/ppermute | solution.py:67
  771.6 63.8 %collective-permute-start.75 = (bf16[384,1536]{1,0:T(8,128)(2,1)S(1)}, bf16[384,1536]{1,0:T(8,128)(2,1)S(1)}, u32[]{:S(2)}, u32[]{:S(2)}) collective-permute-start(bf16[384,1536]{1,0:T(8,128)(2,1)S(1)} %copy-done.45), channel_id=1, source_target_pairs={{0,16},{1,17},{2,18},{3,19},{4,20},{5,21},{6,22},{7,23},{8,24},{9,... | collective-permute-start | bytes 3538952 | tf_op jit(solution)/shard_map/ppermute | solution.py:67
  776.5 58.9 %collective-permute-start.76 = (bf16[384,1536]{1,0:T(8,128)(2,1)S(1)}, bf16[384,1536]{1,0:T(8,128)(2,1)S(1)}, u32[]{:S(2)}, u32[]{:S(2)}) collective-permute-start(bf16[384,1536]{1,0:T(8,128)(2,1)S(1)} %copy-done.45), channel_id=1, source_target_pairs={{0,24},{1,25},{2,26},{3,27},{4,28},{5,29},{6,30},{7,31},{8,16},{9,... | collective-permute-start | bytes 3538952 | tf_op jit(solution)/shard_map/ppermute | solution.py:67
  777.9 56.3 %collective-permute-start.79 = (bf16[384,384]{0,1:T(8,128)(2,1)S(1)}, bf16[384,384]{0,1:T(8,128)(2,1)S(1)}, u32[]{:S(2)}, u32[]{:S(2)}) collective-permute-start(bf16[384,384]{0,1:T(8,128)(2,1)S(1)} %copy-done.62), channel_id=1, source_target_pairs={{0,24},{1,25},{2,26},{3,27},{4,28},{5,29},{6,30},{7,31},{8,16},{9,... | collective-permute-start | bytes 884744 | tf_op jit(solution)/shard_map/ppermute | solution.py:67
  779.0 76.9 %collective-permute-start.89 = (f32[16,1536]{1,0:T(8,128)S(1)}, f32[16,1536]{1,0:T(8,128)S(1)}, u32[]{:S(2)}, u32[]{:S(2)}) collective-permute-start(f32[16,1536]{1,0:T(8,128)S(1)} %add.336), channel_id=1, source_target_pairs={{0,2},{1,3},{2,0},{3,1},{4,6},{5,7},{6,4},{7,5},{8,10},{9,11},{10,... | collective-permute-start | bytes 294920 | tf_op jit(solution)/shard_map/ppermute | solution.py:67
  835.3 93.8 %collective-permute-start.99 = (bf16[4,192,2304]{2,1,0:T(8,128)(2,1)S(1)}, bf16[4,192,2304]{2,1,0:T(8,128)(2,1)}, u32[]{:S(2)}, u32[]{:S(2)}) collective-permute-start(bf16[4,192,2304]{2,1,0:T(8,128)(2,1)S(1)} %pad_maximum_fusion), channel_id=1, source_target_pairs={{0,16},{1,17},{2,18},{3,19},{4,20},{5,21},{6,22},{7,23},{8,24},{9,... | collective-permute-start | bytes 10616840 | tf_op jit(solution)/shard_map/ppermute | solution.py:67
  (181 other events, 3140.9 us)

commit v2 on v1

--- a/solution.py
+++ b/solution.py
@@ -52,81 +52,6 @@
 
 def matmul(left, right):
     return lax.dot_general(left, right, (((1,), (0,)), ((), ())), preferred_element_type=f32)
-
-
-class Links:
-    def __init__(self, n_rep, n_fsdp):
-        self.n_rep, self.n_fsdp = n_rep, n_fsdp
-
-    def swap(self, value, d_rep, d_fsdp):
-        pairs = [
-            (r * self.n_fsdp + f, (r ^ d_rep) * self.n_fsdp + (f ^ d_fsdp))
-            for r in range(self.n_rep)
-            for f in range(self.n_fsdp)
-        ]
-        return lax.ppermute(value, ("replica", "fsdp"), pairs)
-
-
-def place_kernel(n_src, rows, *refs):
-    out = refs[n_src]
-    sem = refs[n_src + 1]
-    me_f = lax.axis_index("fsdp")
-    me_r = lax.axis_index("replica")
-    copies = []
-    slot = 0
-    for n, (src, layout) in enumerate(zip(refs[:n_src], PIECES)):
-        for i, (j, k) in enumerate(layout):
-            owner = jnp.bitwise_xor(me_f, j)
-            if k is None:
-                start, size = owner * (4 * rows), 4 * rows
-            else:
-                start = owner * (4 * rows) + jnp.bitwise_xor(me_r, k) * rows
-                size = rows
-            copy = pltpu.make_async_copy(
-                src.at[pl.ds(i * rows, size)],
-                out.at[pl.ds(pl.multiple_of(start, rows), size)],
-                sem.at[slot],
-            )
-            copy.start()
-            copies.append(copy)
-            slot += 1
-    for copy in copies:
-        copy.wait()
-
-
-PIECES = [
-    [(0, None)],
-    [(2, 0), (4, 0), (6, 0)],
-    [(2, 2), (4, 2), (6, 2)],
-    [(2, 1), (4, 1), (6, 1), (2, 3), (4, 3), (6, 3)],
-    [(1, 0), (3, 0), (5, 0), (7, 0)],
-    [(1, 2), (3, 2), (5, 2), (7, 2)],
-    [(1, 1), (3, 1), (5, 1), (7, 1), (1, 3), (3, 3), (5, 3), (7, 3)],
-]
-
-
-def gather_dense(links, shard, me_r):
-    rows = shard.shape[0] // 4
-    quarter = lax.dynamic_slice_in_dim(shard, me_r * rows, rows, 0)
-    z = [links.swap(quarter, 0, j) for j in (2, 4, 6)]
-    zs = jnp.concatenate(z, 0)
-    ys = links.swap(jnp.concatenate([quarter] + z, 0), 0, 1)
-    zx = links.swap(zs, 2, 0)
-    yx = links.swap(ys, 2, 0)
-    zc = links.swap(jnp.concatenate([zs, zx], 0), 1, 0)
-    yc = links.swap(jnp.concatenate([ys, yx], 0), 1, 0)
-    pieces = [shard, zs, zx, zc, ys, yx, yc]
-    count = sum(len(p) for p in PIECES)
-    full = pl.pallas_call(
-        functools.partial(place_kernel, len(pieces), rows),
-        out_shape=jax.ShapeDtypeStruct((8 * shard.shape[0], shard.shape[1]), shard.dtype),
-        in_specs=[pl.BlockSpec(memory_space=pl.ANY)] * len(pieces),
-        out_specs=pl.BlockSpec(memory_space=pltpu.VMEM),
-        scratch_shapes=[pltpu.SemaphoreType.DMA((count,))],
-        compiler_params=pltpu.CompilerParams(vmem_limit_bytes=20 * MIB),
-        name="place",
-    )(*pieces)
-    return full
 
 
 def expert_kernel(nt, nw, length, width, hidden, rows, expert_of, offset_of, *refs):
@@ -310,64 +235,734 @@
     return result[:nt], result[nt : 2 * nt], result[2 * nt :]
 
 
+MESH_ID = pl.DeviceIdType.MESH
+
+
+def flip(index, bit):
+    return index + bit - 2 * bit * lax.rem(index // bit, 2)
+
+
+def flips(index, mask):
+    for bit in (1, 2, 4):
+        if mask & bit:
+            index = flip(index, bit)
+    return index
+
+
+class Wire:
+    def __init__(self, send_sem, recv_sem):
+        self.r, self.f = lax.axis_index("replica"), lax.axis_index("fsdp")
+        self.send_sem, self.recv_sem = send_sem, recv_sem
+        self.used, self.sent = 0, []
+
+    def meet(self, partners):
+        barrier = pltpu.get_barrier_semaphore()
+        for d_r, d_f in partners:
+            pl.semaphore_signal(
+                barrier, inc=1, device_id=self.at(d_r, d_f), device_id_type=MESH_ID
+            )
+        pl.semaphore_wait(barrier, len(partners))
+
+    def at(self, d_r, d_f):
+        return (flips(self.r, d_r), flips(self.f, d_f))
+
+    def send(self, src, dst, d_r, d_f):
+        copy = pltpu.make_async_remote_copy(
+            src_ref=src,
+            dst_ref=dst,
+            send_sem=self.send_sem.at[self.used],
+            recv_sem=self.recv_sem.at[self.used],
+            device_id=self.at(d_r, d_f),
+            device_id_type=MESH_ID,
+        )
+        copy.start()
+        self.used += 1
+        self.sent.append(copy)
+        return copy
+
+    def finish(self):
+        for copy in self.sent:
+            copy.wait_send()
+
+
+START_SENDS = 2 * 28 + 7 + 8 + 7
+PARTNERS = ((1, 0), (2, 0), (0, 1), (0, 2), (0, 4), (0, 6))
+
+
+def start_kernel(
+    in_ref, out_ref, tiny_ref, mine_ref, other_ref, g_ref,
+    in_all, out_all, tiny_all, w_all, g_all,
+    in_buf, out_buf, w_buf, tiny_buf, local_sem, send_sem, recv_sem,
+):
+    wire = Wire(send_sem, recv_sem)
+    r, f = wire.r, wire.f
+    shard = in_ref.shape[0]
+    quarter = shard // 4
+    local = []
+    for n, (src, buf) in enumerate(
+        ((in_ref, in_buf), (out_ref, out_buf), (mine_ref, w_buf), (tiny_ref, tiny_buf))
+    ):
+        copy = pltpu.make_async_copy(src, buf, local_sem.at[n])
+        copy.start()
+        local.append(copy)
+    wire.meet(PARTNERS)
+
+    def rows(j, k):
+        at = flips(f, j) * shard + flips(r, k) * quarter
+        return pl.ds(pl.multiple_of(at, quarter), quarter)
+
+    def shard_rows(j):
+        return pl.ds(pl.multiple_of(flips(f, j) * shard, shard), shard)
+
+    own = pl.ds(pl.multiple_of(r * quarter, quarter), quarter)
+    got_t = {}
+    for m in (2, 4, 6):
+        got_t[m] = wire.send(tiny_ref, tiny_all.at[f], 0, m)
+    got_t[1] = wire.send(tiny_ref, tiny_all.at[f], 0, 1)
+    got = {}
+    for name, src, dst in (("in", in_ref, in_all), ("out", out_ref, out_all)):
+        for m in (2, 4, 6):
+            got[name, m, 0] = wire.send(src.at[own], dst.at[rows(0, 0)], 0, m)
+        got[name, 1, 0] = wire.send(src.at[own], dst.at[rows(0, 0)], 0, 1)
+    for copy, (buf, dst) in zip(
+        local,
+        (
+            (in_buf, in_all.at[shard_rows(0)]),
+            (out_buf, out_all.at[shard_rows(0)]),
+            (w_buf, w_all.at[shard_rows(0)]),
+            (tiny_buf, tiny_all.at[f]),
+        ),
+    ):
+        copy.wait()
+    stores = []
+    for n, (buf, dst) in enumerate(
+        (
+            (in_buf, in_all.at[shard_rows(0)]),
+            (out_buf, out_all.at[shard_rows(0)]),
+            (w_buf, w_all.at[shard_rows(0)]),
+            (tiny_buf, tiny_all.at[f]),
+        )
+    ):
+        copy = pltpu.make_async_copy(buf, dst, local_sem.at[4 + n])
+        copy.start()
+        stores.append(copy)
+
+    for m in (2, 4, 6):
+        got_t[m].wait_recv()
+        at = tiny_all.at[flips(f, m)]
+        got_t[m + 1] = wire.send(at, at, 0, 1)
+
+    half = g_ref.shape[0] // 2
+    got_g = {}
+    got_g[2] = wire.send(g_ref, g_all.at[2], 2, 0)
+    got_g[4] = wire.send(g_ref, g_all.at[4], 0, 2)
+    got_g[1] = wire.send(g_ref, g_all.at[1], 1, 0)
+    got_w = {}
+    for m, src in ((2, other_ref), (4, mine_ref), (6, other_ref)):
+        got_w[m] = wire.send(src, w_all.at[shard_rows(0)], 0, m)
+    got_w[1] = wire.send(mine_ref, w_all.at[shard_rows(0)], 0, 1)
+
+    for name, dst in (("in", in_all), ("out", out_all)):
+
+        def pass_on(j, k, d_r, d_f):
+            at = dst.at[rows(j, k)]
+            return wire.send(at, at, d_r, d_f)
+
+        for m in (1, 2, 4, 6):
+            got[name, m, 0].wait_recv()
+            if m != 1:
+                got[name, m + 1, 0] = pass_on(m, 0, 0, 1)
+            got[name, m, 2] = pass_on(m, 0, 2, 0)
+            got[name, m, 1] = pass_on(m, 0, 1, 0)
+        for m in (3, 5, 7):
+            got[name, m, 0].wait_recv()
+            got[name, m, 2] = pass_on(m, 0, 2, 0)
+            got[name, m, 1] = pass_on(m, 0, 1, 0)
+        for m in (1, 2, 4, 6, 3, 5, 7):
+            got[name, m, 2].wait_recv()
+            got[name, m, 3] = pass_on(m, 2, 1, 0)
+
+    for m in (2, 4):
+        got_g[m].wait_recv()
+        got_g[m + 1] = wire.send(g_all.at[m], g_all.at[m + 1], 1, 0)
+    low, top = pl.ds(0, half), pl.ds(half, half)
+    far = [
+        wire.send(g_all.at[4, low], g_all.at[6, low], 2, 0),
+        wire.send(g_all.at[2, top], g_all.at[6, top], 0, 2),
+    ]
+    for m in (2, 4, 6):
+        got_w[m].wait_recv()
+        at = w_all.at[shard_rows(m)]
+        got_w[m + 1] = wire.send(at, at, 0, 1)
+    for copy in far:
+        copy.wait_recv()
+    got_g[7] = wire.send(g_all.at[6], g_all.at[7], 1, 0)
+
+    for m in (1, 3, 5, 7):
+        got_t[m].wait_recv()
+        got_w[m].wait_recv()
+        got_g[m].wait_recv()
+    for name in ("in", "out"):
+        for m in range(1, 8):
+            got[name, m, 1].wait_recv()
+            got[name, m, 3].wait_recv()
+    for copy in stores:
+        copy.wait()
+    wire.finish()
+
+
+def start(in_proj, out_proj, tiny, mine, other, grad, n_fsdp):
+    any_spec = pl.BlockSpec(memory_space=pl.ANY)
+    shard = in_proj.shape[0]
+    whole = n_fsdp * shard
+    return pl.pallas_call(
+        start_kernel,
+        out_shape=[
+            jax.ShapeDtypeStruct((whole, in_proj.shape[1]), bf16),
+            jax.ShapeDtypeStruct((whole, out_proj.shape[1]), bf16),
+            jax.ShapeDtypeStruct((n_fsdp,) + tiny.shape, bf16),
+            jax.ShapeDtypeStruct((whole, mine.shape[1]), bf16),
+            jax.ShapeDtypeStruct((8,) + grad.shape, bf16),
+        ],
+        in_specs=[any_spec] * 6,
+        out_specs=[any_spec] * 5,
+        scratch_shapes=[
+            pltpu.VMEM(in_proj.shape, bf16),
+            pltpu.VMEM(out_proj.shape, bf16),
+            pltpu.VMEM(mine.shape, bf16),
+            pltpu.VMEM(tiny.shape, bf16),
+            pltpu.SemaphoreType.DMA((8,)),
+            pltpu.SemaphoreType.DMA((START_SENDS,)),
+            pltpu.SemaphoreType.DMA((START_SENDS,)),
+        ],
+        compiler_params=pltpu.CompilerParams(
+            collective_id=1, has_side_effects=True, vmem_limit_bytes=16 * MIB
+        ),
+        name="start",
+    )(in_proj, out_proj, tiny, mine, other, grad)
+
+
+ORDER = (0, 1, 2, 3, 6, 7, 5, 4)
+GROUP_AT = {1: (1, 0), 2: (2, 0), 4: (0, 2), 6: (2, 2)}
+
+
+def pick(step, table):
+    value = jnp.int32(table[-1])
+    for i, item in enumerate(table[:-1]):
+        value = jnp.where(step == i, item, value)
+    return value
+
+
+def group_kernel(
+    v_ref, g_ref, g_all, w_ref,
+    xs, mix_all, dx_own, dx_in, grads,
+    wbuf, xbuf, gbuf, xt, gt_, hidg, dgu, mbuf, dbuf, rc, acc, stage,
+    sem_w, sem_x, sem_g, sem_m, sem_s, send_sem, recv_sem,
+):
+    wire = Wire(send_sem, recv_sem)
+    r, f = wire.r, wire.f
+    length, width = g_ref.shape
+    hidden = w_ref.shape[1] // 3
+    expert = 2 * r + lax.rem(f // 2, 2)
+    half = length // 2
+    low, top = pl.ds(0, half), pl.ds(half, half)
+    step_cols = 256
+
+    def plan(src, dst, d):
+        copy = pltpu.make_async_remote_copy(
+            src_ref=src,
+            dst_ref=dst,
+            send_sem=send_sem.at[wire.used],
+            recv_sem=recv_sem.at[wire.used],
+            device_id=wire.at(*d),
+            device_id_type=MESH_ID,
+        )
+        wire.used += 1
+        wire.sent.append(copy)
+        return copy
+
+    tok = {
+        1: plan(v_ref, xs.at[1], (1, 0)),
+        2: plan(v_ref, xs.at[2], (2, 0)),
+        4: plan(v_ref, xs.at[4], (0, 2)),
+        3: plan(xs.at[2], xs.at[3], (1, 0)),
+        5: plan(xs.at[4], xs.at[5], (1, 0)),
+        6: plan(xs.at[4, low], xs.at[6, low], (2, 0)),
+        8: plan(xs.at[2, top], xs.at[6, top], (0, 2)),
+        7: plan(xs.at[6], xs.at[7], (1, 0)),
+    }
+    to_core = {k: plan(dbuf.at[k + 1], rc.at[k // 2], (1, 0)) for k in (0, 2, 4, 6)}
+    back = {
+        k: plan(dbuf.at[k], dx_in.at[k // 2 - 1], GROUP_AT[k]) for k in (2, 4, 6)
+    }
+
+    load_w = pltpu.make_async_copy(w_ref, wbuf, sem_w.at[0])
+    load_w.start()
+
+    def load(step):
+        slot = lax.rem(step, 2)
+        k = pick(step, ORDER)
+
+        @pl.when(step == 0)
+        def _():
+            pltpu.make_async_copy(v_ref, xbuf.at[0], sem_x.at[0]).start()
+            pltpu.make_async_copy(g_ref, gbuf.at[0], sem_g.at[0]).start()
+
+        @pl.when(step > 0)
+        def _():
+            pltpu.make_async_copy(xs.at[k], xbuf.at[slot], sem_x.at[slot]).start()
+            pltpu.make_async_copy(g_all.at[k], gbuf.at[slot], sem_g.at[slot]).start()
+
+    load(jnp.int32(0))
+    wire.meet(PARTNERS_GROUP)
+    for k in (2, 4, 1):
+        tok[k].start()
+    acc[...] = jnp.zeros_like(acc)
+    lane = lax.broadcasted_iota(jnp.int32, (length, EXTRA), 1)
+    load_w.wait()
+
+    def total(k):
+        to_core[k].wait_recv()
+        dbuf[k] = (dbuf[k].astype(f32) + rc[k // 2].astype(f32)).astype(bf16)
+
+    def block(step, carry):
+        slot = lax.rem(step, 2)
+        k = pick(step, ORDER)
+        pltpu.make_async_copy(v_ref, xbuf.at[slot], sem_x.at[slot]).wait()
+        pltpu.make_async_copy(g_ref, gbuf.at[slot], sem_g.at[slot]).wait()
+
+        @pl.when(step >= 2)
+        def _():
+            pltpu.make_async_copy(mbuf.at[slot], mix_all.at[0], sem_m.at[slot]).wait()
+
+        extra = xbuf[slot, :, width:].astype(f32)
+        mine = (lane == expert) | (lane == expert + 8)
+        gate = jnp.sum(jnp.where(mine, extra, 0.0), axis=1, keepdims=True)
+        xt[...] = xbuf[slot, :, :width].T
+        gt_[...] = gbuf[slot].T
+
+        def first(c, dgate):
+            at = pl.multiple_of(c * step_cols, step_cols)
+            u = matmul(xbuf[slot, :, :width], wbuf[:, pl.ds(at, step_cols)])
+            up = matmul(xbuf[slot, :, :width], wbuf[:, pl.ds(hidden + at, step_cols)])
+            rev = matmul(gbuf[slot], wbuf[:, pl.ds(2 * hidden + at, step_cols)])
+            sig = 1.0 / (1.0 + jnp.exp(-u))
+            act = u * sig
+            hid = act * up
+            hidg[:, pl.ds(at, step_cols)] = (gate * hid).astype(bf16)
+            dgate = dgate + jnp.sum(rev * hid, axis=1, keepdims=True)
+            dhid = gate * rev
+            dgu[:, pl.ds(at, step_cols)] = (
+                dhid * up * sig * (1.0 + u * (1.0 - sig))
+            ).astype(bf16)
+            dgu[:, pl.ds(hidden + at, step_cols)] = (dhid * act).astype(bf16)
+            return dgate
+
+        dgate = lax.fori_loop(
+            0, hidden // step_cols, first, jnp.zeros((length, 1), f32)
+        )
+
+        def second(c, carry):
+            at = pl.multiple_of(c * step_cols, step_cols)
+            dbuf[k, :, pl.ds(at, step_cols)] = contract_cols(
+                dgu[...], wbuf[pl.ds(at, step_cols), pl.ds(0, 2 * hidden)]
+            ).astype(bf16)
+            mbuf[slot, :, pl.ds(at, step_cols)] = contract_cols(
+                hidg[...], wbuf[pl.ds(at, step_cols), pl.ds(2 * hidden, hidden)]
+            ).astype(bf16)
+            return carry
+
+        lax.fori_loop(0, width // step_cols, second, 0)
+        high = dgate.astype(bf16).astype(f32)
+        rest = dgate - high
+        dbuf[k, :, width:] = (
+            jnp.where(lane == expert, high, 0.0) + jnp.where(lane == expert + 8, rest, 0.0)
+        ).astype(bf16)
+        pltpu.make_async_copy(mbuf.at[slot], mix_all.at[k], sem_m.at[slot]).start()
+
+        @pl.when(step == 0)
+        def _():
+            tok[1].wait_recv()
+            load(step + 1)
+
+        @pl.when(step == 1)
+        def _():
+            to_core[0].start()
+
+        @pl.when(step == 2)
+        def _():
+            tok[3].wait_recv()
+            load(step + 1)
+
+        @pl.when(step == 3)
+        def _():
+            to_core[2].start()
+            total(0)
+            tok[6].wait_recv()
+            tok[8].wait_recv()
+            tok[7].start()
+            load(step + 1)
+
+        @pl.when(step == 4)
+        def _():
+            total(2)
+            back[2].start()
+            tok[7].wait_recv()
+            load(step + 1)
+
+        @pl.when(step == 5)
+        def _():
+            to_core[6].start()
+            tok[5].wait_recv()
+            load(step + 1)
+
+        @pl.when(step == 6)
+        def _():
+            to_core[4].start()
+            total(6)
+            back[6].start()
+            load(step + 1)
+
+        @pl.when(step == 7)
+        def _():
+            total(4)
+            back[4].start()
+
+        def third(c, carry):
+            at = pl.multiple_of(c * step_cols, step_cols)
+            acc[:, pl.ds(at, step_cols)] += matmul(xt[...], dgu[:, pl.ds(at, step_cols)])
+            return carry
+
+        lax.fori_loop(0, 2 * hidden // step_cols, third, 0)
+
+        def fourth(c, carry):
+            at = pl.multiple_of(c * step_cols, step_cols)
+            acc[:, pl.ds(2 * hidden + at, step_cols)] += matmul(
+                gt_[...], hidg[:, pl.ds(at, step_cols)]
+            )
+            return carry
+
+        lax.fori_loop(0, hidden // step_cols, fourth, 0)
+
+        @pl.when(step == 1)
+        def _():
+            tok[2].wait_recv()
+            tok[8].start()
+            tok[3].start()
+            load(step + 1)
+            tok[4].wait_recv()
+            tok[6].start()
+            tok[5].start()
+
+        return carry
+
+    lax.fori_loop(0, 8, block, 0)
+    keep = pltpu.make_async_copy(dbuf.at[0], dx_own, sem_w.at[0])
+    keep.start()
+    for slot in (0, 1):
+        pltpu.make_async_copy(mbuf.at[slot], mix_all.at[0], sem_m.at[slot]).wait()
+    parts = 8
+    rows = width // parts
+
+    def out(j, slot):
+        return pltpu.make_async_copy(
+            stage.at[slot], grads.at[pl.ds(j * rows, rows)], sem_s.at[slot]
+        )
+
+    for j in range(parts):
+        slot = j % 2
+        if j >= 2:
+            out(j - 2, slot).wait()
+        stage[slot] = acc[j * rows : (j + 1) * rows].astype(bf16)
+        out(j, slot).start()
+    for j in range(parts - 2, parts):
+        out(j, j % 2).wait()
+    keep.wait()
+    for k in (2, 4, 6):
+        back[k].wait_recv()
+    wire.finish()
+
+
+PARTNERS_GROUP = ((1, 0), (2, 0), (0, 2), (2, 2))
+GROUP_SENDS = 8 + 4 + 3
+
+
+def run_group(v, grad, g_all, w):
+    length, width = grad.shape
+    wide = v.shape[1]
+    cols = w.shape[1]
+    hidden = cols // 3
+    any_spec = pl.BlockSpec(memory_space=pl.ANY)
+    return pl.pallas_call(
+        group_kernel,
+        out_shape=[
+            jax.ShapeDtypeStruct((8, length, wide), bf16),
+            jax.ShapeDtypeStruct((8, length, width), bf16),
+            jax.ShapeDtypeStruct((length, wide), bf16),
+            jax.ShapeDtypeStruct((3, length, wide), bf16),
+            jax.ShapeDtypeStruct((width, cols), bf16),
+        ],
+        in_specs=[any_spec] * 4,
+        out_specs=[any_spec] * 5,
+        scratch_shapes=[
+            pltpu.VMEM((width, cols), bf16),
+            pltpu.VMEM((2, length, wide), bf16),
+            pltpu.VMEM((2, length, width), bf16),
+            pltpu.VMEM((width, length), bf16),
+            pltpu.VMEM((width, length), bf16),
+            pltpu.VMEM((length, hidden), bf16),
+            pltpu.VMEM((length, 2 * hidden), bf16),
+            pltpu.VMEM((2, length, width), bf16),
+            pltpu.VMEM((8, length, wide), bf16),
+            pltpu.VMEM((4, length, wide), bf16),
+            pltpu.VMEM((width, cols), f32),
+            pltpu.VMEM((2, width // 8, cols), bf16),
+            pltpu.SemaphoreType.DMA((1,)),
+            pltpu.SemaphoreType.DMA((2,)),
+            pltpu.SemaphoreType.DMA((2,)),
+            pltpu.SemaphoreType.DMA((2,)),
+            pltpu.SemaphoreType.DMA((2,)),
+            pltpu.SemaphoreType.DMA((GROUP_SENDS,)),
+            pltpu.SemaphoreType.DMA((GROUP_SENDS,)),
+        ],
+        compiler_params=pltpu.CompilerParams(
+            collective_id=2, has_side_effects=True, vmem_limit_bytes=60 * MIB
+        ),
+        cost_estimate=pl.CostEstimate(
+            flops=48 * length * width * cols,
+            bytes_accessed=64 * length * width + 4 * width * cols,
+            transcendentals=8 * length * hidden,
+        ),
+        name="group",
+    )(v, grad, g_all, w)
+
+
+PARTNERS_END = ((1, 0), (2, 0), (3, 0), (0, 1), (0, 2), (0, 4), (0, 6), (2, 2))
+END_SENDS = 4 + 3 + 4 + 6 + 4 + 3 + 3 * 4 + 4 + 3 + 3 + 5 + 8
+
+
+def end_kernel(
+    grads, mix_all, xn, attn, dres, dproj, terms,
+    g_out, mix_own, mix_in, d_out, terms_out,
+    gl, gy, gz, pair, ml, mrc, xq, aq, rq, pq, wq, wl, wy, wz, own_d, tbuf, tr,
+    local_sem, send_sem, recv_sem,
+):
+    wire = Wire(send_sem, recv_sem)
+    r, f = wire.r, wire.f
+    shard = gl.shape[1]
+    length = xn.shape[0]
+    low = lax.rem(f // 2, 2)
+    cols_p, cols_a = pq.shape[1], aq.shape[1]
+    used = [0]
+
+    def local(src, dst):
+        copy = pltpu.make_async_copy(src, dst, local_sem.at[used[0]])
+        copy.start()
+        used[0] += 1
+        return copy
+
+    def shard_rows(j):
+        return pl.ds(pl.multiple_of(flips(f, j) * shard, shard), shard)
+
+    def token_rows(k):
+        return pl.ds(k * length, length)
+
+    load_g = {j: local(grads.at[shard_rows(j)], gl.at[j // 2]) for j in (0, 2, 4, 6)}
+    load_m = {k: local(mix_all.at[k], ml.at[k // 2]) for k in (0, 2, 4, 6)}
+    loads = [
+        local(xn, xq.at[token_rows(0)]),
+        local(dres, rq.at[token_rows(0)]),
+        local(
+            attn.at[:, pl.ds(pl.multiple_of(r * cols_a, cols_a), cols_a)],
+            aq.at[token_rows(0)],
+        ),
+        local(
+            dproj.at[:, pl.ds(pl.multiple_of(r * cols_p, cols_p), cols_p)],
+            pq.at[token_rows(0)],
+        ),
+    ]
+    load_t = local(terms, tbuf.at[0])
+    wire.meet(PARTNERS_END)
+
+    act = {}
+    for k in (1, 2, 3):
+        to_p = flips(r, k) * cols_p
+        to_a = flips(r, k) * cols_a
+        act["p", k] = wire.send(
+            dproj.at[:, pl.ds(pl.multiple_of(to_p, cols_p), cols_p)],
+            pq.at[token_rows(k)], k, 0,
+        )
+        act["a", k] = wire.send(
+            attn.at[:, pl.ds(pl.multiple_of(to_a, cols_a), cols_a)],
+            aq.at[token_rows(k)], k, 0,
+        )
+    for k in (2, 1):
+        act["x", k] = wire.send(xn, xq.at[token_rows(k)], k, 0)
+        act["r", k] = wire.send(dres, rq.at[token_rows(k)], k, 0)
+    got_y = {
+        j: wire.send(grads.at[shard_rows(j + 1)], gy.at[j // 2], 0, 1) for j in (2, 4, 6, 0)
+    }
+    got_mc = {k: wire.send(mix_all.at[k + 1], mrc.at[k // 2], 1, 0) for k in (2, 4, 6, 0)}
+
+    load_t.wait()
+
+    for n, d in enumerate(((1, 0), (0, 1), (2, 0), (0, 2), (0, 4))):
+        copy = wire.send(tbuf.at[n], tr.at[n], *d)
+        copy.wait_recv()
+        tbuf[n + 1] = tbuf[n] + tr[n]
+    keep_t = local(tbuf.at[5], terms_out)
+
+    for k in ("x", "r"):
+        act[k, 2].wait_recv()
+        buf = xq if k == "x" else rq
+        act[k, 3] = wire.send(buf.at[token_rows(2)], buf.at[token_rows(3)], 1, 0)
+    for copy in loads:
+        copy.wait()
+    for k in (1, 2, 3):
+        for name in ("p", "a", "r", "x"):
+            if (name, k) != ("x", 2) and (name, k) != ("r", 2):
+                act[name, k].wait_recv()
+
+    part = 256
+
+    def dense(c, carry):
+        at = pl.multiple_of(c * part, part)
+        wq[pl.ds(at, part), pl.ds(0, cols_p)] = matmul(
+            xq[:, pl.ds(at, part)].T, pq[...]
+        ).astype(bf16)
+        wq[pl.ds(at, part), pl.ds(cols_p, cols_a)] = matmul(
+            rq[:, pl.ds(at, part)].T, aq[...]
+        ).astype(bf16)
+        return carry
+
+    lax.fori_loop(0, wq.shape[0] // part, dense, 0)
+    got_wy = {
+        j: wire.send(wq.at[shard_rows(j + 1)], wy.at[j // 2], 0, 1) for j in (2, 4, 6, 0)
+    }
+
+    def add(u, v):
+        return (u.astype(f32) + v.astype(f32)).astype(bf16)
+
+    got_m = {}
+    for k, d in ((2, (2, 0)), (4, (0, 2)), (6, (2, 2))):
+        load_m[k].wait()
+        got_mc[k].wait_recv()
+        ml[k // 2] = add(ml[k // 2], mrc[k // 2])
+        got_m[k] = wire.send(ml.at[k // 2], mix_in.at[k // 2 - 1], *d)
+    load_m[0].wait()
+    got_mc[0].wait_recv()
+    ml[0] = add(ml[0], mrc[0])
+    keep_m = local(ml.at[0], mix_own)
+
+    got_z = {}
+    for j in (2, 4, 6):
+        load_g[j].wait()
+        got_y[j].wait_recv()
+        gl[j // 2] = add(gl[j // 2], gy[j // 2])
+        got_z[j] = wire.send(gl.at[j // 2], gz.at[j // 2 - 1], 0, j)
+    load_g[0].wait()
+    got_y[0].wait_recv()
+
+    got_wz = {}
+    for j in (2, 4, 6):
+        wl[j // 2] = wq[shard_rows(j)]
+        got_wy[j].wait_recv()
+        wl[j // 2] = add(wl[j // 2], wy[j // 2])
+        got_wz[j] = wire.send(wl.at[j // 2], wz.at[j // 2 - 1], 0, j)
+    got_wy[0].wait_recv()
+    own = wq[shard_rows(0)].astype(f32) + wy[0].astype(f32)
+
+    got_z[4].wait_recv()
+    pair[0] = (
+        gl[0].astype(f32) + gy[0].astype(f32) + gz[1].astype(f32)
+    ).astype(bf16)
+    mine, other = 2 * r + low, 2 * r + 1 - low
+    kept = [local(pair.at[0], g_out.at[mine])]
+    got_e = {}
+    got_e[2, 0] = wire.send(pair.at[0], g_out.at[mine], 2, 0)
+    got_e[1, 0] = wire.send(pair.at[0], g_out.at[mine], 1, 0)
+    got_z[2].wait_recv()
+    got_z[6].wait_recv()
+    pair[1] = add(gz[0], gz[2])
+    kept.append(local(pair.at[1], g_out.at[other]))
+    got_e[2, 1] = wire.send(pair.at[1], g_out.at[other], 2, 0)
+    got_e[1, 1] = wire.send(pair.at[1], g_out.at[other], 1, 0)
+
+    for j in (2, 4, 6):
+        got_wz[j].wait_recv()
+        own = own + wz[j // 2 - 1].astype(f32)
+    own_d[...] = own.astype(bf16)
+    kept.append(local(own_d, d_out.at[r]))
+    got_d = [wire.send(own_d, d_out.at[r], k, 0) for k in (1, 2, 3)]
+
+    far = flips(r, 2)
+    for n, e in ((0, 2 * far + low), (1, 2 * far + 1 - low)):
+        got_e[2, n].wait_recv()
+        got_e[3, n] = wire.send(g_out.at[e], g_out.at[e], 1, 0)
+    for k in (1, 3):
+        for n in (0, 1):
+            got_e[k, n].wait_recv()
+    for copy in got_d:
+        copy.wait_recv()
+    for k in (2, 4, 6):
+        got_m[k].wait_recv()
+    for copy in kept + [keep_m, keep_t]:
+        copy.wait()
+    wire.finish()
+
+
+def run_end(grads, mix_all, xn, attn, dres, dproj, terms):
+    length, width = xn.shape
+    shard = width // 8
+    cols = grads.shape[1]
+    cols_p, cols_a = dproj.shape[1] // 4, attn.shape[1] // 4
+    dense = cols_p + cols_a
+    any_spec = pl.BlockSpec(memory_space=pl.ANY)
+    return pl.pallas_call(
+        end_kernel,
+        out_shape=[
+            jax.ShapeDtypeStruct((8, shard, cols), bf16),
+            jax.ShapeDtypeStruct((length, width), bf16),
+            jax.ShapeDtypeStruct((3, length, width), bf16),
+            jax.ShapeDtypeStruct((4, shard, dense), bf16),
+            jax.ShapeDtypeStruct(terms.shape, f32),
+        ],
+        in_specs=[any_spec] * 7,
+        out_specs=[any_spec] * 5,
+        scratch_shapes=[
+            pltpu.VMEM((4, shard, cols), bf16),
+            pltpu.VMEM((4, shard, cols), bf16),
+            pltpu.VMEM((3, shard, cols), bf16),
+            pltpu.VMEM((2, shard, cols), bf16),
+            pltpu.VMEM((4, length, width), bf16),
+            pltpu.VMEM((4, length, width), bf16),
+            pltpu.VMEM((4 * length, width), bf16),
+            pltpu.VMEM((4 * length, cols_a), bf16),
+            pltpu.VMEM((4 * length, width), bf16),
+            pltpu.VMEM((4 * length, cols_p), bf16),
+            pltpu.VMEM((width, dense), bf16),
+            pltpu.VMEM((4, shard, dense), bf16),
+            pltpu.VMEM((4, shard, dense), bf16),
+            pltpu.VMEM((3, shard, dense), bf16),
+            pltpu.VMEM((shard, dense), bf16),
+            pltpu.VMEM((6,) + terms.shape, f32),
+            pltpu.VMEM((5,) + terms.shape, f32),
+            pltpu.SemaphoreType.DMA((24,)),
+            pltpu.SemaphoreType.DMA((END_SENDS,)),
+            pltpu.SemaphoreType.DMA((END_SENDS,)),
+        ],
+        compiler_params=pltpu.CompilerParams(
+            collective_id=3, has_side_effects=True, vmem_limit_bytes=60 * MIB
+        ),
+        name="end",
+    )(grads, mix_all, xn, attn, dres, dproj, terms)
+
+
 class Near:
-    group = ((0, 0), (1, 0), (2, 0), (3, 0), (0, 2), (1, 2), (2, 2), (3, 2))
-
     def __init__(self, n_rep, n_fsdp):
-        self.links = Links(n_rep, n_fsdp)
-        self.swap = self.links.swap
-
-    def dense(self, shard):
-        return gather_dense(self.links, shard, lax.axis_index("replica"))
-
-    def small(self, shard):
-        f = lax.axis_index("fsdp")
-        got = shard[None]
-        for bit in (1, 2, 4):
-            other = self.swap(got, 0, bit)
-            up = (f & bit) != 0
-            got = jnp.concatenate(
-                [jnp.where(up, other, got), jnp.where(up, got, other)], axis=0
-            )
-        return got
-
-    def sum_all(self, value):
-        for d in ((1, 0), (0, 1), (2, 0), (0, 2), (0, 4)):
-            value = value + self.swap(value, *d)
-        return value
-
-    def spread(self, value):
-        half = value.shape[0] // 2
-        over_x = self.swap(value, 2, 0)
-        over_z = self.swap(value, 0, 2)
-        far = jnp.concatenate(
-            [self.swap(over_z[:half], 2, 0), self.swap(over_x[half:], 0, 2)], axis=0
-        )
-        near = [value, over_x, over_z, far]
-        cores = [self.swap(v, 1, 0) for v in near]
-        return [near[0], cores[0], near[1], cores[1], near[2], cores[2], near[3], cores[3]]
-
-    def collect(self, parts):
-        sums = [
-            (parts[k].astype(f32) + self.swap(parts[k + 1], 1, 0).astype(f32)).astype(bf16)
-            for k in (0, 2, 4, 6)
-        ]
-        cut = sums[0].shape[0] // 2
-        a = [s[:cut] for s in sums]
-        b = [s[cut:] for s in sums]
-
-        def add(u, v):
-            return u.astype(f32) + v.astype(f32)
-
-        a0 = add(a[0], self.swap(a[1], 2, 0))
-        a2 = add(a[2], self.swap(a[3], 2, 0)).astype(bf16)
-        b0 = add(b[0], self.swap(b[2], 0, 2))
-        b1 = add(b[1], self.swap(b[3], 0, 2)).astype(bf16)
-        a0 = a0 + self.swap(a2, 0, 2).astype(f32)
-        b0 = b0 + self.swap(b1, 2, 0).astype(f32)
-        return jnp.concatenate([a0, b0], axis=0)
-
-    def expert_weights(self, expert_in, expert_out):
+        self.n_fsdp = n_fsdp
+
+    def start(self, in_proj, out_proj, tiny, expert_in, expert_out, grad):
         r, f = lax.axis_index("replica"), lax.axis_index("fsdp")
         low = (f >> 1) & 1
         mine, other = [
@@ -380,98 +975,39 @@
             )
             for e in (2 * r + low, 2 * r + 1 - low)
         ]
-        blocks = {0: mine}
-        blocks[2] = self.swap(other, 0, 2)
-        blocks[4] = self.swap(mine, 0, 4)
-        blocks[6] = self.swap(other, 0, 6)
-        for j in (0, 2, 4, 6):
-            blocks[j + 1] = self.swap(blocks[j], 0, 1)
-        return [blocks[j] for j in range(8)]
-
-    def experts(self, xs, gs, weights):
-        rows = weights[0].shape[0]
-
-        def expert_of():
-            return 2 * lax.axis_index("replica") + lax.rem(lax.axis_index("fsdp") // 2, 2)
-
-        def offset_of(j):
-            return jnp.bitwise_xor(lax.axis_index("fsdp"), j) * rows
-
-        return run_expert(xs, gs, weights, expert_of, offset_of)
-
-    def expert_sums(self, grads):
-        f = lax.axis_index("fsdp")
-        r = lax.axis_index("replica")
-
-        def add(u, v):
-            return (u.astype(f32) + v.astype(f32)).astype(bf16)
-
-        held = {j: add(grads[j], self.swap(grads[j + 1], 0, 1)) for j in (0, 2, 4, 6)}
-        mine = add(held[0], self.swap(held[4], 0, 4))
-        other = add(self.swap(held[2], 0, 2), self.swap(held[6], 0, 6))
-        low = ((f >> 1) & 1) == 0
-        pair = jnp.stack([jnp.where(low, mine, other), jnp.where(low, other, mine)])
-        core = (r & 1) == 0
-        peer = self.swap(pair, 1, 0)
-        four = jnp.concatenate([jnp.where(core, pair, peer), jnp.where(core, peer, pair)])
-        side = (r & 2) == 0
-        far = self.swap(four, 2, 0)
-        return jnp.concatenate([jnp.where(side, four, far), jnp.where(side, far, four)])
-
-    def spread_quad(self, value):
-        return [value] + [self.swap(value, k, 0) for k in (1, 2, 3)]
-
-    def trade_quad(self, value):
-        r = lax.axis_index("replica")
-        width = value.shape[1] // 4
-        return [
-            (lambda part: part if k == 0 else self.swap(part, k, 0))(
-                lax.dynamic_slice_in_dim(value, (r ^ k) * width, width, 1)
-            )
-            for k in range(4)
-        ]
-
-    def dense_sum(self, quarter):
-        f = lax.axis_index("fsdp")
-        r = lax.axis_index("replica")
-        rows = quarter.shape[0] // 8
-        blocks = [
-            lax.dynamic_slice_in_dim(quarter, (f ^ j) * rows, rows, 0).astype(bf16)
-            for j in range(8)
-        ]
-
-        def add(u, v):
-            return (u.astype(f32) + v.astype(f32)).astype(bf16)
-
-        got = self.swap(jnp.stack([blocks[j + 1] for j in (0, 2, 4, 6)]), 0, 1)
-        held = {j: add(blocks[j], got[j // 2]) for j in (0, 2, 4, 6)}
-        total = held[0].astype(f32)
-        for j in (2, 4, 6):
-            total = total + self.swap(held[j], 0, j).astype(f32)
-        total = total.astype(bf16)
-        core = (r & 1) == 0
-        peer = self.swap(total, 1, 0)
-        two = jnp.concatenate(
-            [jnp.where(core, total, peer), jnp.where(core, peer, total)], axis=1
+        pad = jnp.pad(tiny, ((0, 0), (0, -tiny.shape[1] % 128)))
+        proj_in, proj_out, tiny_all, weights, gs = start(
+            in_proj, out_proj, pad, mine, other, grad, self.n_fsdp
         )
-        side = (r & 2) == 0
-        far = self.swap(two, 2, 0)
-        return jnp.concatenate([jnp.where(side, two, far), jnp.where(side, far, two)], axis=1)
+        tiny_all = tiny_all[:, :, : tiny.shape[1]].transpose(1, 0, 2).reshape(16, -1)
+        return proj_in, proj_out, tiny_all, (weights, gs, grad)
+
+    def experts(self, payload, held):
+        weights, gs, grad = held
+        _, mix_all, dx_own, dx_in, grads = run_group(payload, grad, gs, weights)
+        dx = dx_own.astype(f32)
+        for k in range(3):
+            dx = dx + dx_in[k].astype(f32)
+        return dx, (mix_all, grads)
+
+    def end(self, held, first, normed, attn, dres, dproj, terms):
+        mix_all, grads = held
+        expert_sum, mix_own, mix_in, dense, terms = run_end(
+            grads, mix_all, normed, attn, dres, dproj, terms
+        )
+        mixed = first + mix_own.astype(f32)
+        for k in range(3):
+            mixed = mixed + mix_in[k].astype(f32)
+        cut = dproj.shape[1] // 4
+        in_grad = dense[:, :, :cut].transpose(1, 0, 2).reshape(dense.shape[1], -1)
+        out_grad = dense[:, :, cut:].transpose(1, 0, 2).reshape(dense.shape[1], -1)
+        return mixed, in_grad, out_grad, expert_sum.transpose(1, 0, 2), terms
 
 
 class Wide:
     def __init__(self, n_rep, n_fsdp):
         self.n_rep, self.n_fsdp = n_rep, n_fsdp
 
-    def dense(self, shard):
-        return lax.all_gather(shard, "fsdp", axis=0, tiled=True)
-
-    def small(self, shard):
-        return lax.all_gather(shard, "fsdp", axis=0)
-
-    def sum_all(self, value):
-        return lax.psum(value, ("replica", "fsdp"))
-
     def spread(self, value):
         every = lax.all_gather(value, "replica", axis=0)
         return [every[k] for k in range(self.n_rep)]
@@ -479,10 +1015,10 @@
     def collect(self, parts):
         return lax.psum_scatter(jnp.stack(parts), "replica", scatter_dimension=0).astype(f32)
 
-    def expert_weights(self, expert_in, expert_out):
+    def start(self, in_proj, out_proj, tiny, expert_in, expert_out, grad):
         r = lax.axis_index("replica")
         per = expert_in.shape[1] // self.n_rep
-        out = []
+        weights = []
         for i in range(per):
             both = jnp.concatenate(
                 [
@@ -491,10 +1027,17 @@
                 ],
                 axis=1,
             )
-            out.append(lax.all_gather(both, "fsdp", axis=0, tiled=True))
-        return out
-
-    def experts(self, xs, gs, weights):
+            weights.append(lax.all_gather(both, "fsdp", axis=0, tiled=True))
+        return (
+            lax.all_gather(in_proj, "fsdp", axis=0, tiled=True),
+            lax.all_gather(out_proj, "fsdp", axis=0, tiled=True),
+            lax.all_gather(tiny, "fsdp", axis=1, tiled=True),
+            (weights, self.spread(grad)),
+        )
+
+    def experts(self, payload, held):
+        weights, gs = held
+        xs = self.spread(payload)
         per = len(weights)
         mixes, dxs, grads = None, None, []
         for i, w in enumerate(weights):
@@ -506,26 +1049,27 @@
             mixes = mix if mixes is None else [a + b for a, b in zip(mixes, mix)]
             dxs = dx if dxs is None else [a + b for a, b in zip(dxs, dx)]
             grads.append(grad[0])
-        return mixes, dxs, grads
-
-    def expert_sums(self, grads):
+        return self.collect(dxs), (mixes, grads)
+
+    def trade(self, value):
+        cut = value.reshape(value.shape[0], self.n_rep, -1).transpose(1, 0, 2)
+        got = lax.all_to_all(cut, "replica", 0, 0)
+        return got.reshape(-1, got.shape[2])
+
+    def end(self, held, first, normed, attn, dres, dproj, terms):
+        mixes, grads = held
+        mixed = first + self.collect(mixes)
         own = jnp.stack(
             [lax.psum_scatter(g, "fsdp", scatter_dimension=0, tiled=True) for g in grads]
         )
-        return lax.all_gather(own, "replica", axis=0, tiled=True)
-
-    def spread_quad(self, value):
-        every = lax.all_gather(value, "replica", axis=0)
-        return [every[k] for k in range(self.n_rep)]
-
-    def trade_quad(self, value):
-        cut = value.reshape(value.shape[0], self.n_rep, -1).transpose(1, 0, 2)
-        got = lax.all_to_all(cut, "replica", 0, 0)
-        return [got[k] for k in range(self.n_rep)]
-
-    def dense_sum(self, quarter):
-        own = lax.psum_scatter(quarter.astype(bf16), "fsdp", scatter_dimension=0, tiled=True)
-        return lax.all_gather(own, "replica", axis=1, tiled=True)
+        expert_sum = lax.all_gather(own, "replica", axis=0, tiled=True).transpose(1, 0, 2)
+        dense = []
+        for left, right in ((normed, dproj), (dres, attn)):
+            left = lax.all_gather(left, "replica", axis=0, tiled=True)
+            part = contract_rows(left, self.trade(right)).astype(bf16)
+            own = lax.psum_scatter(part, "fsdp", scatter_dimension=0, tiled=True)
+            dense.append(lax.all_gather(own, "replica", axis=1, tiled=True))
+        return mixed, dense[0], dense[1], expert_sum, lax.psum(terms, ("replica", "fsdp"))
 
 
 def layer(
@@ -546,18 +1090,12 @@
     tiny = jnp.concatenate(
         [router.T, norm_gains.T, jnp.zeros((16 - experts - 2, shard), bf16)], axis=0
     )
-    tiny = net.small(tiny).transpose(1, 0, 2).reshape(16, width)
+    proj_in, proj_out, tiny, held = net.start(
+        in_proj, out_proj, tiny, expert_in, expert_out, out_grad
+    )
     router_rows = tiny[:experts]
     gain_one = tiny[experts].astype(f32)
     gain_two = tiny[experts + 1].astype(f32)
-    proj_in = net.dense(in_proj)
-    out_proj, proj_in = lax.optimization_barrier((out_proj, proj_in))
-    proj_out = net.dense(out_proj)
-    expert_in, expert_out, out_grad_sent, _ = lax.optimization_barrier(
-        (expert_in, expert_out, out_grad, proj_out)
-    )
-    weights = net.expert_weights(expert_in, expert_out)
-    gs = net.spread(out_grad_sent)
 
     inputs = tokens.astype(f32)
     scale_one = rms_scale(inputs)
@@ -594,10 +1132,7 @@
     payload = jnp.concatenate(
         [normed_two, high, low, jnp.zeros((length, EXTRA - 2 * experts), bf16)], axis=1
     )
-    xs = net.spread(payload)
-    mixes, dxs, grads = net.experts(xs, gs, weights)
-    dx = net.collect(dxs)
-    mixed = (first + net.collect(mixes)).astype(bf16)
+    dx, held = net.experts(payload, held)
 
     grad_out = out_grad.astype(f32)
     dgate_all = dx[:, width : width + experts] + dx[:, width + experts : width + 2 * experts]
@@ -632,14 +1167,6 @@
         * (dunit_one - unit_one * jnp.mean(dunit_one * unit_one, axis=-1, keepdims=True))
     ).astype(bf16)
 
-    expert_sum = net.expert_sums(grads).transpose(1, 0, 2)
-    all_normed = jnp.concatenate(net.spread_quad(normed), axis=0)
-    part_attn = jnp.concatenate(net.trade_quad(attn), axis=0)
-    all_dres = jnp.concatenate(net.spread_quad(dres), axis=0)
-    out_proj_grad = net.dense_sum(contract_rows(all_dres, part_attn)).astype(f32)
-    part_dproj = jnp.concatenate(net.trade_quad(dproj), axis=0)
-    in_proj_grad = net.dense_sum(contract_rows(all_normed, part_dproj)).astype(f32)
-
     terms = jnp.concatenate(
         [
             contract_rows(dlogits, normed_two),
@@ -649,14 +1176,15 @@
         ],
         axis=0,
     )
-    terms = lax.dynamic_slice_in_dim(
-        net.sum_all(terms), lax.axis_index("fsdp") * shard, shard, 1
-    ).T
+    mixed, in_proj_grad, out_proj_grad, expert_sum, terms = net.end(
+        held, first, normed, attn, dres, dproj, terms
+    )
+    terms = lax.dynamic_slice_in_dim(terms, lax.axis_index("fsdp") * shard, shard, 1).T
     return (
-        mixed,
+        mixed.astype(bf16),
         tokens_grad,
-        in_proj_grad,
-        out_proj_grad,
+        in_proj_grad.astype(f32),
+        out_proj_grad.astype(f32),
         terms[:, :experts],
         terms[:, experts : experts + 2],
         expert_sum[..., : 2 * hidden].astype(f32),

time: 964 us -> 746 us (0.77)
  waiting for transfers between devices: 474 us -> 0 us
  Pallas kernels: 129 us -> 557 us
  starting transfers between devices: 167 us -> 0 us
  other arithmetic: 70.5 us -> 41.2 us
  local copies, waits for them, and re-layouts: 67.4 us -> 81.4 us
    ppermute x100 -> x0, waiting for transfers between devices: 474 us -> none  [swap(): return lax.ppermute(value, ('replica', 'fsdp'), pairs)]
    pallas_call x3, Pallas kernels: 129 us -> 557 us  [the longest x1 253 us: run_end(): pl.pallas_call(end_kernel, out_shape=[jax.ShapeDtypeStruct((8, shard, col...]
    ppermute x100 -> x0, starting transfers between devices: 167 us -> none  [swap(): return lax.ppermute(value, ('replica', 'fsdp'), pairs)]
    convert_element_type x21 -> x0, other arithmetic: 12.8 us -> none  [the longest x8 3.62 us: collect(): (parts[k].astype(f32) + self.swap(parts[k + 1], 1, 0).astype(f32)).astype...]
    unnamed x234 -> x128, local copies, waits for them, and re-layouts: 28.9 us -> 36.6 us
  transfers between devices with their start and end apart: 100 -> 0, of which waited for: 39 -> 0; matrix products, arithmetic and copies ran while one was open for 14% -> 0% of each run, Pallas kernels for 0% -> 0%
where the time goes in v2:
time: 746 us; the launch traced here: 736 us
  Pallas kernels  557 us (75%)
  local copies, waits for them, and re-layouts  81.4 us (11%)
  matrix products  54.5 us (7%)
  other arithmetic  41.2 us (6%)
    pallas_call x1, Pallas kernels, run_end(): pl.pallas_call(end_kernel, out_shape=[jax.ShapeDtypeStruct((8, shard, col...  253 us
    pallas_call x1, Pallas kernels, start(): pl.pallas_call(start_kernel, out_shape=[jax.ShapeDtypeStruct((whole, in_p...  152 us
    pallas_call x1, Pallas kernels, run_group(): pl.pallas_call(group_kernel, out_shape=[jax.ShapeDtypeStruct((8, length,...  151 us
    unnamed x128, local copies, waits for them, and re-layouts  36.6 us

profile of v2, /device:TPU:1, one launch (start us, length us, event | category | flops | bytes accessed | tf_op | source)
XLA Modules:
  0.0 735.6 jit_solution(15689177437228990488)
XLA Ops:
  0.6 6.2 constant_dynamic-slice_fusion.1
  11.4 151.7 %start.1 = (bf16[1536,2048]{1,0:T(8,128)(2,1)S(1)}, bf16[1536,1536]{1,0:T(8,128)(2,1)S(1)}, bf16[8,16,256]{2,1,0:T(8,128)(2,1)S(1)}, bf16[1536,2304]{1,0:T(8,128)(2,1)S(1)}, bf16[8,384,1536]{2,1,0:T(8,128)(2,1)S(1)}) custom-call(bf16[192,2048]{1,0:T(8,128)(2,1)S(1)} %copy-done.2, bf16[192,1536]{1,0:T(8,128)(2,1)S(1)} %copy-done.3, ...), custom_call_target="tpu_custom_call" | custom-call | tf_op jit(solution)/shard_map/start/pallas_call | solution.py:418
  163.2 3.7 copy-done.4
  166.9 2.8 copy-done.5
  169.7 2.7 copy-done.6
  172.4 2.2 copy-done.7
  176.9 5.1 fusion.52
  187.6 2.0 subtract_convert_fusion.3
  191.3 2.0 copy.119
  196.5 3.3 fusion.51
  203.9 4.6 fusion.22
  208.6 2.2 multiply_reduce_fusion.2
  223.4 2.6 concatenate.47.v_ref
  226.0 151.3 %group.1 = (bf16[8,384,1664]{2,1,0:T(8,128)(2,1)}, bf16[8,384,1536]{2,1,0:T(8,128)(2,1)}, bf16[384,1664]{1,0:T(8,128)(2,1)}, bf16[3,384,1664]{2,1,0:T(8,128)(2,1)}, bf16[1536,2304]{1,0:T(8,128)(2,1)}) custom-call(bf16[384,1664]{1,0:T(8,128)(2,1)} %concatenate.47.v_ref, bf16[384,1536]{1,0:T(8,128)(2,1)} %g_ref.3, bf16[8,384,1536]{2,1,0:T(8,128)(2,1)} %copy-done.4, ...), custom_call_target="tpu_custom_call" | custom-call | flops 65229815808 | bytes 51904512 | tf_op jit(solution)/shard_map/group/pallas_call | solution.py:696
  377.3 3.0 convert_add_fusion.1
  389.4 3.3 multiply_reduce_fusion
  395.0 5.3 convolution_convert_fusion
  400.4 2.5 copy.128
  402.9 7.8 %fusion = (f32[2,6,384]{2,1,0:T(8,128)S(1)}, f32[2,384,384,6]{2,1,3,0:T(8,128)}) fusion(f32[2,6,384,384]{2,3,1,0:T(8,128)} %copy-done.8, f32[2,6,384]{2,1,0:T(8,128)} %log_add_fusion, bf16[384,2,6,128]{0,3,2,1:T(8,128)(2,1)} %bitcast.118, bf16[384,2,128,1]{2,1,0,3:T(2,128)(2,1)} %bitcast.134), kind=kOutput, calls=%fused_computation.2 | convolution fusion | flops 458288640 | bytes 15568896 | tf_op jit(solution)/shard_map/qkgd,tkd->kgqt/dot_general | solution.py:1152
  410.8 6.3 fusion.2
  417.1 2.9 convolution_multiply_fusion
  421.6 2.4 copy.140
  423.9 4.6 fusion.27
  432.6 4.8 fusion.28
  439.2 8.5 %fusion.15 = (f32[384]{0:T(512)}, f32[1536]{0:T(1024)S(1)}, f32[384,1536]{1,0:T(8,128)}) fusion(bf16[384,1536]{1,0:T(8,128)(2,1)} %param.10, f32[1536]{0:T(1024)S(1)} %copy-done.44, f32[384]{0:T(512)} %copy-done.51, bf16[1536,2048]{1,0:T(8,128)(2,1)} %copy-done.6, bf16[384,256]{1,0:T(8,128)(2,1)} %copy.165, bf16[384,256]{1,0:T(8,128)(2,1)} %copy_bitcast_fusion.4, ...), kind=kOutput, calls=%fused_computation.29 | convolution fusion | flops 2424764416 | bytes 11418624 | tf_op jit(solution)/shard_map/dot_general | solution.py:50
  449.9 2.4 copy.141.attn
  452.3 253.5 %end.1 = (bf16[8,192,2304]{2,1,0:T(8,128)(2,1)}, bf16[384,1536]{1,0:T(8,128)(2,1)}, bf16[3,384,1536]{2,1,0:T(8,128)(2,1)}, bf16[4,192,896]{2,1,0:T(8,128)(2,1)}, f32[16,1536]{1,0:T(8,128)}) custom-call(bf16[1536,2304]{1,0:T(8,128)(2,1)} %get-tuple-element.27.grads, bf16[8,384,1536]{2,1,0:T(8,128)(2,1)} %get-tuple-element.28.mix_all, ...), custom_call_target="tpu_custom_call" | custom-call | tf_op jit(solution)/shard_map/end/pallas_call | solution.py:921
  705.8 3.6 slice_convert_fusion
  709.4 9.2 %copy.144 = f32[192,8,1536]{2,1,0:T(8,128)} copy(f32[192,8,1536]{2,0,1:T(8,128)S(1)} %slice_convert_fusion) | data formatting | bytes 18874368
  718.6 2.1 slice_convert_fusion.1
  720.7 5.2 copy.145
  728.8 3.1 fusion.19
  (201 shorter events, 60.6 us)
Async XLA Ops:
  10.0 165.9 %copy-start.13 = (bf16[384,1536]{1,0:T(8,128)(2,1)S(1)}, bf16[384,1536]{1,0:T(8,128)(2,1)}, u32[]{:S(2)}) copy-start(bf16[384,1536]{1,0:T(8,128)(2,1)} %param.10) | copy-start | bytes 3538948
  163.2 3.7 copy-start.4
  176.9 5.1 copy-start.19
  182.0 7.7 %copy-start.22 = (f32[384,2048]{1,0:T(8,128)}, f32[384,2048]{1,0:T(8,128)S(1)}, u32[]{:S(2)}) copy-start(f32[384,2048]{1,0:T(8,128)S(1)} %fusion.52) | copy-start | bytes 9437188
  186.7 3.0 copy-start.27
  186.7 3.0 copy-start.33
  195.4 4.5 copy-start.16
  196.4 3.5 copy-start.17
  199.9 4.0 copy-start.39
  199.9 8.7 %slice-start = ((s8[4718592]{0:T(1024)(128)(4,1)}), s8[524288]{0:T(1024)(128)(4,1)S(1)}, s32[]{:S(2)}) async-start(s8[4718592]{0:T(1024)(128)(4,1)} %bitcast.114), calls=%async_computation | async-start | bytes 1048576
  202.8 5.7 copy-start.42
  203.9 4.6 copy-start.34
  203.9 4.7 slice-start.1
  203.9 4.7 copy-start.14
  210.8 3.2 copy-start.45
  389.4 3.3 copy-start.1
  389.4 3.3 copy-start.46
  402.9 7.8 %slice-start.2 = ((s8[7077888]{0:T(1024)(128)(4,1)}), s8[4194304]{0:T(1024)(128)(4,1)S(1)}, s32[]{:S(2)}) async-start(s8[7077888]{0:T(1024)(128)(4,1)} %bitcast.116), calls=%async_computation.2 | async-start | bytes 8388608
  402.9 7.8 %slice-start.3 = ((s8[7077888]{0:T(1024)(128)(4,1)}), s8[2883584]{0:T(1024)(128)(4,1)S(1)}, s32[]{:S(2)}) async-start(s8[7077888]{0:T(1024)(128)(4,1)} %bitcast.116), calls=%async_computation.3 | async-start | bytes 5767168
  402.9 7.8 %copy-start.38 = (f32[2,6,384]{2,1,0:T(8,128)S(1)}, f32[2,6,384]{2,1,0:T(8,128)}, u32[]{:S(2)}) copy-start(f32[2,6,384]{2,1,0:T(8,128)} %log_add_fusion) | copy-start | bytes 55300
  410.8 6.3 copy-start.25
  410.8 6.3 copy-start.26
  417.1 3.0 copy-start.32
  432.6 6.6 copy-start.44
  439.1 8.6 %copy-start.50 = (f32[1536]{0:T(1024)S(1)}, f32[1536]{0:T(1024)}, u32[]{:S(2)}) copy-start(f32[1536]{0:T(1024)} %get-tuple-element.68) | copy-start | bytes 18436
  439.1 8.7 %copy-start.41 = (f32[8,1536]{1,0:T(8,128)S(1)}, f32[8,1536]{1,0:T(8,128)}, u32[]{:S(2)}) copy-start(f32[8,1536]{1,0:T(8,128)} %fusion.54) | copy-start | bytes 147460
  439.1 9.4 %copy-start.18 = (bf16[384,1536]{1,0:T(8,128)(2,1)S(1)}, bf16[384,1536]{1,0:T(8,128)(2,1)}, u32[]{:S(2)}) copy-start(bf16[384,1536]{1,0:T(8,128)(2,1)} %copy.140) | copy-start | bytes 3538948
  439.1 9.4 %copy-start.35 = (bf16[384,256]{1,0:T(8,128)(2,1)S(1)}, bf16[384,256]{1,0:T(8,128)(2,1)}, u32[]{:S(2)}) copy-start(bf16[384,256]{1,0:T(8,128)(2,1)} %copy.165) | copy-start | bytes 589828
  439.1 9.4 %copy-start.36 = (bf16[384,256]{1,0:T(8,128)(2,1)S(1)}, bf16[384,256]{1,0:T(8,128)(2,1)}, u32[]{:S(2)}) copy-start(bf16[384,256]{1,0:T(8,128)(2,1)} %copy_bitcast_fusion.4) | copy-start | bytes 589828
  720.7 5.2 copy-start.29
  720.7 6.8 copy-start.21
  720.7 6.8 copy-start.23
  (31 other events, 58.1 us)

commit v3 on v2

--- a/solution.py
+++ b/solution.py
@@ -266,7 +266,7 @@
     def at(self, d_r, d_f):
         return (flips(self.r, d_r), flips(self.f, d_f))
 
-    def send(self, src, dst, d_r, d_f):
+    def plan(self, src, dst, d_r, d_f):
         copy = pltpu.make_async_remote_copy(
             src_ref=src,
             dst_ref=dst,
@@ -275,37 +275,46 @@
             device_id=self.at(d_r, d_f),
             device_id_type=MESH_ID,
         )
+        self.used += 1
+        return copy
+
+    def send(self, src, dst, d_r, d_f):
+        copy = self.plan(src, dst, d_r, d_f)
         copy.start()
-        self.used += 1
         self.sent.append(copy)
         return copy
 
-    def finish(self):
+    def finish(self, waited=()):
         for copy in self.sent:
-            copy.wait_send()
-
-
-START_SENDS = 2 * 28 + 7 + 8 + 7
+            if all(copy is not other for other in waited):
+                copy.wait_send()
+
+
+FRONT_SENDS = 2 * 28 + 7 + 7 + 8 + 8
 PARTNERS = ((1, 0), (2, 0), (0, 1), (0, 2), (0, 4), (0, 6))
-
-
-def start_kernel(
+ROWS = 64
+
+
+def turn(v, cosine, sine):
+    return v * cosine + pltpu.roll(v, HD // 2, 1) * sine
+
+
+def front_kernel(
+    tokens, seg_col, seg_row, routes, cos, sin,
     in_ref, out_ref, tiny_ref, mine_ref, other_ref, g_ref,
-    in_all, out_all, tiny_all, w_all, g_all,
-    in_buf, out_buf, w_buf, tiny_buf, local_sem, send_sem, recv_sem,
+    qkv, attn, xn, first, lse, table, tiny_out, v,
+    in_all, out_all, w_all, g_all, xs,
+    in_v, out_v, tiny_v, rt, bias, w_buf, local_sem, send_sem, recv_sem,
 ):
     wire = Wire(send_sem, recv_sem)
     r, f = wire.r, wire.f
     shard = in_ref.shape[0]
     quarter = shard // 4
-    local = []
-    for n, (src, buf) in enumerate(
-        ((in_ref, in_buf), (out_ref, out_buf), (mine_ref, w_buf), (tiny_ref, tiny_buf))
-    ):
-        copy = pltpu.make_async_copy(src, buf, local_sem.at[n])
-        copy.start()
-        local.append(copy)
-    wire.meet(PARTNERS)
+    length, width = tokens.shape
+    half = length // 2
+    low, top = pl.ds(0, half), pl.ds(half, half)
+    experts = 8
+    scale = HD ** (-0.5)
 
     def rows(j, k):
         at = flips(f, j) * shard + flips(r, k) * quarter
@@ -314,136 +323,252 @@
     def shard_rows(j):
         return pl.ds(pl.multiple_of(flips(f, j) * shard, shard), shard)
 
+    def local(n, src, dst):
+        copy = pltpu.make_async_copy(src, dst, local_sem.at[n])
+        copy.start()
+        return copy
+
+    own_in = local(0, in_ref, in_v.at[shard_rows(0)])
+    own_out = local(1, out_ref, out_v.at[shard_rows(0)])
+    own_tiny = local(2, tiny_ref, tiny_v.at[f])
+    own_w = local(3, mine_ref, w_buf)
+    wire.meet(PARTNERS)
+
     own = pl.ds(pl.multiple_of(r * quarter, quarter), quarter)
-    got_t = {}
-    for m in (2, 4, 6):
-        got_t[m] = wire.send(tiny_ref, tiny_all.at[f], 0, m)
-    got_t[1] = wire.send(tiny_ref, tiny_all.at[f], 0, 1)
-    got = {}
-    for name, src, dst in (("in", in_ref, in_all), ("out", out_ref, out_all)):
-        for m in (2, 4, 6):
-            got[name, m, 0] = wire.send(src.at[own], dst.at[rows(0, 0)], 0, m)
-        got[name, 1, 0] = wire.send(src.at[own], dst.at[rows(0, 0)], 0, 1)
-    for copy, (buf, dst) in zip(
-        local,
-        (
-            (in_buf, in_all.at[shard_rows(0)]),
-            (out_buf, out_all.at[shard_rows(0)]),
-            (w_buf, w_all.at[shard_rows(0)]),
-            (tiny_buf, tiny_all.at[f]),
-        ),
-    ):
-        copy.wait()
-    stores = []
-    for n, (buf, dst) in enumerate(
-        (
-            (in_buf, in_all.at[shard_rows(0)]),
-            (out_buf, out_all.at[shard_rows(0)]),
-            (w_buf, w_all.at[shard_rows(0)]),
-            (tiny_buf, tiny_all.at[f]),
-        )
-    ):
-        copy = pltpu.make_async_copy(buf, dst, local_sem.at[4 + n])
-        copy.start()
-        stores.append(copy)
+    land = {"in": in_v, "out": out_v}
+    source = {"in": in_ref, "out": out_ref}
+    got, got_t, got_w, got_g, got_x = {}, {}, {}, {}, {}
+
+    for m in (2, 4, 6, 1):
+        got_t[m] = wire.send(tiny_ref, tiny_v.at[f], 0, m)
+
+    def own_pieces(name):
+        for m in (2, 4, 6, 1):
+            got[name, m, 0] = wire.send(
+                source[name].at[own], land[name].at[rows(0, 0)], 0, m
+            )
+
+    def pass_on(name, j, k, d_r, d_f):
+        at = land[name].at[rows(j, k)]
+        return wire.send(at, at, d_r, d_f)
+
+    def near_pieces(name):
+        for m in (1, 2, 4, 6):
+            got[name, m, 0].wait_recv()
+            if m != 1:
+                got[name, m + 1, 0] = pass_on(name, m, 0, 0, 1)
+            got[name, m, 2] = pass_on(name, m, 0, 2, 0)
+            got[name, m, 1] = pass_on(name, m, 0, 1, 0)
+
+    def far_pieces(name):
+        for m in (3, 5, 7):
+            got[name, m, 0].wait_recv()
+            got[name, m, 2] = pass_on(name, m, 0, 2, 0)
+            got[name, m, 1] = pass_on(name, m, 0, 1, 0)
+
+    def side_pieces(name):
+        for m in (1, 2, 4, 6, 3, 5, 7):
+            got[name, m, 2].wait_recv()
+            got[name, m, 3] = pass_on(name, m, 2, 1, 0)
+
+    def all_pieces(name):
+        for m in range(1, 8):
+            got[name, m, 1].wait_recv()
+            got[name, m, 3].wait_recv()
+
+    own_pieces("in")
+    own_w.wait()
+    kept = [local(4, w_buf, w_all.at[shard_rows(0)])]
 
     for m in (2, 4, 6):
         got_t[m].wait_recv()
-        at = tiny_all.at[flips(f, m)]
+        at = tiny_v.at[flips(f, m)]
         got_t[m + 1] = wire.send(at, at, 0, 1)
-
-    half = g_ref.shape[0] // 2
-    got_g = {}
+    for m in (1, 3, 5, 7):
+        got_t[m].wait_recv()
+    own_tiny.wait()
+    lanes = tiny_v.shape[2]
+    rt[...] = jnp.zeros_like(rt)
+    for z in range(4):
+        both = tiny_v[2 * z].astype(f32) + tiny_v[2 * z + 1].astype(f32)
+        tiny_out[:, z * lanes : (z + 1) * lanes] = both
+        row = lax.broadcasted_iota(jnp.int32, both.shape, 0)
+        rt[0:16, z * lanes : (z + 1) * lanes] = jnp.where(row < experts, both, 0.0).astype(bf16)
+
+    def norm_one(c, carry):
+        at = pl.ds(pl.multiple_of(c * ROWS, ROWS), ROWS)
+        x = tokens[at, :].astype(f32)
+        unit = x * lax.rsqrt(jnp.mean(x * x, axis=-1, keepdims=True) + epsilon)
+        xn[at, :] = (unit * tiny_out[experts : experts + 1, :]).astype(bf16)
+        return carry
+
+    lax.fori_loop(0, length // ROWS, norm_one, 0)
+    spot = lax.broadcasted_iota(jnp.int32, bias.shape, 0)
+    keys_at = lax.broadcasted_iota(jnp.int32, bias.shape, 1)
+    bias[...] = jnp.where((spot >= keys_at) & (seg_col[...] == seg_row[...]), 0.0, -1e30)
+
+    near_pieces("in")
+    own_pieces("out")
+    far_pieces("in")
+    side_pieces("in")
+    near_pieces("out")
+    for m, src in ((2, other_ref), (4, mine_ref), (6, other_ref)):
+        got_w[m] = wire.send(src, w_all.at[shard_rows(0)], 0, m)
+    got_w[1] = wire.send(mine_ref, w_all.at[shard_rows(0)], 0, 1)
+    own_in.wait()
+    all_pieces("in")
+
+    def project(c, carry):
+        at = pl.multiple_of(c * 256, 256)
+        t = matmul(xn[...], in_v[:, pl.ds(at, 256)])
+        turned = c < 7
+        for n in (0, 1):
+            part = t[:, n * HD : (n + 1) * HD]
+            part = turn(
+                part, jnp.where(turned, cos[...], 1.0), jnp.where(turned, sin[...], 0.0)
+            )
+            qkv[:, pl.ds(at + n * HD, HD)] = part.astype(bf16)
+        return carry
+
+    lax.fori_loop(0, 8, project, 0)
+    far_pieces("out")
+    side_pieces("out")
     got_g[2] = wire.send(g_ref, g_all.at[2], 2, 0)
     got_g[4] = wire.send(g_ref, g_all.at[4], 0, 2)
     got_g[1] = wire.send(g_ref, g_all.at[1], 1, 0)
-    got_w = {}
-    for m, src in ((2, other_ref), (4, mine_ref), (6, other_ref)):
-        got_w[m] = wire.send(src, w_all.at[shard_rows(0)], 0, m)
-    got_w[1] = wire.send(mine_ref, w_all.at[shard_rows(0)], 0, 1)
-
-    for name, dst in (("in", in_all), ("out", out_all)):
-
-        def pass_on(j, k, d_r, d_f):
-            at = dst.at[rows(j, k)]
-            return wire.send(at, at, d_r, d_f)
-
-        for m in (1, 2, 4, 6):
-            got[name, m, 0].wait_recv()
-            if m != 1:
-                got[name, m + 1, 0] = pass_on(m, 0, 0, 1)
-            got[name, m, 2] = pass_on(m, 0, 2, 0)
-            got[name, m, 1] = pass_on(m, 0, 1, 0)
-        for m in (3, 5, 7):
-            got[name, m, 0].wait_recv()
-            got[name, m, 2] = pass_on(m, 0, 2, 0)
-            got[name, m, 1] = pass_on(m, 0, 1, 0)
-        for m in (1, 2, 4, 6, 3, 5, 7):
-            got[name, m, 2].wait_recv()
-            got[name, m, 3] = pass_on(m, 2, 1, 0)
-
-    for m in (2, 4):
-        got_g[m].wait_recv()
-        got_g[m + 1] = wire.send(g_all.at[m], g_all.at[m + 1], 1, 0)
-    low, top = pl.ds(0, half), pl.ds(half, half)
-    far = [
-        wire.send(g_all.at[4, low], g_all.at[6, low], 2, 0),
-        wire.send(g_all.at[2, top], g_all.at[6, top], 0, 2),
-    ]
+    lane = lax.broadcasted_iota(jnp.int32, (length, HD), 1)
+    lse[...] = jnp.zeros_like(lse)
+
+    def head(h, carry):
+        at = pl.ds(pl.multiple_of(h * HD, HD), HD)
+        group = h // GROUP
+        k_at = pl.ds(pl.multiple_of(WQ + group * HD, HD), HD)
+        v_at = pl.ds(pl.multiple_of(WQ + WK + group * HD, HD), HD)
+        s = contract_cols(qkv[:, at], qkv[:, k_at]) * scale + bias[...]
+        highest = jnp.max(s, axis=-1, keepdims=True)
+        expo = jnp.exp(s - highest)
+        total = jnp.sum(expo, axis=-1, keepdims=True)
+        p = (expo * (1.0 / total)).astype(bf16)
+        attn[:, at] = matmul(p, qkv[:, v_at]).astype(bf16)
+        lse[...] = jnp.where(lane == h, highest + jnp.log(total), lse[...])
+        return carry
+
+    lax.fori_loop(0, HQ, head, 0)
+    own_out.wait()
+    all_pieces("out")
+    kept.append(local(5, in_v, in_all))
+    kept.append(local(6, out_v, out_all))
+
+    def add_out(c, carry):
+        at = pl.ds(pl.multiple_of(c * 256, 256), 256)
+        first[:, at] = tokens[:, at].astype(f32) + contract_cols(attn[...], out_v[at, :])
+        return carry
+
+    lax.fori_loop(0, width // 256, add_out, 0)
+
+    def norm_two(c, carry):
+        at = pl.ds(pl.multiple_of(c * ROWS, ROWS), ROWS)
+        h = first[at, :]
+        unit = h * lax.rsqrt(jnp.mean(h * h, axis=-1, keepdims=True) + epsilon)
+        v[at, 0:width] = (unit * tiny_out[experts + 1 : experts + 2, :]).astype(bf16)
+        return carry
+
+    lax.fori_loop(0, length // ROWS, norm_two, 0)
+    logits = contract_cols(v[:, 0:width], rt[...])
+    chosen = lane == routes[:, 0:1]
+    for j in range(1, routes.shape[1]):
+        chosen = chosen | (lane == routes[:, j : j + 1])
+    logits = jnp.where(chosen, logits, -1e30)
+    expo = jnp.exp(logits - jnp.max(logits, axis=-1, keepdims=True))
+    expo = jnp.where(chosen, expo, 0.0)
+    gates = expo / jnp.sum(expo, axis=-1, keepdims=True)
+    table[...] = gates
+    high = gates.astype(bf16).astype(f32)
+    v[:, width:] = (high + pltpu.roll(gates - high, experts, 1)).astype(bf16)
+
+    got_x[2] = wire.send(v, xs.at[2], 2, 0)
+    got_x[4] = wire.send(v, xs.at[4], 0, 2)
+    got_x[1] = wire.send(v, xs.at[1], 1, 0)
+
+    def onward(got_some, buf):
+        for m in (2, 4):
+            got_some[m].wait_recv()
+            got_some[m + 1] = wire.send(buf.at[m], buf.at[m + 1], 1, 0)
+        return [
+            wire.send(buf.at[4, low], buf.at[6, low], 2, 0),
+            wire.send(buf.at[2, top], buf.at[6, top], 0, 2),
+        ]
+
+    far_g = onward(got_g, g_all)
     for m in (2, 4, 6):
         got_w[m].wait_recv()
         at = w_all.at[shard_rows(m)]
         got_w[m + 1] = wire.send(at, at, 0, 1)
-    for copy in far:
+    far_x = onward(got_x, xs)
+    for copy in far_g:
         copy.wait_recv()
     got_g[7] = wire.send(g_all.at[6], g_all.at[7], 1, 0)
-
+    for copy in far_x:
+        copy.wait_recv()
+    got_x[7] = wire.send(xs.at[6], xs.at[7], 1, 0)
     for m in (1, 3, 5, 7):
-        got_t[m].wait_recv()
         got_w[m].wait_recv()
         got_g[m].wait_recv()
-    for name in ("in", "out"):
-        for m in range(1, 8):
-            got[name, m, 1].wait_recv()
-            got[name, m, 3].wait_recv()
-    for copy in stores:
+        got_x[m].wait_recv()
+    for copy in kept:
         copy.wait()
     wire.finish()
 
 
-def start(in_proj, out_proj, tiny, mine, other, grad, n_fsdp):
+def front(tokens, seg_ids, routes, cos, sin, in_proj, out_proj, tiny, mine, other, grad):
     any_spec = pl.BlockSpec(memory_space=pl.ANY)
-    shard = in_proj.shape[0]
-    whole = n_fsdp * shard
+    vmem = pl.BlockSpec(memory_space=pltpu.VMEM)
+    length, width = tokens.shape
+    shard, cols = in_proj.shape
+    whole = 8 * shard
+    wide = width + EXTRA
     return pl.pallas_call(
-        start_kernel,
+        front_kernel,
         out_shape=[
-            jax.ShapeDtypeStruct((whole, in_proj.shape[1]), bf16),
+            jax.ShapeDtypeStruct((length, cols), bf16),
+            jax.ShapeDtypeStruct((length, WQ), bf16),
+            jax.ShapeDtypeStruct((length, width), bf16),
+            jax.ShapeDtypeStruct((length, width), f32),
+            jax.ShapeDtypeStruct((length, HD), f32),
+            jax.ShapeDtypeStruct((length, EXTRA), f32),
+            jax.ShapeDtypeStruct((16, width), f32),
+            jax.ShapeDtypeStruct((length, wide), bf16),
+            jax.ShapeDtypeStruct((whole, cols), bf16),
             jax.ShapeDtypeStruct((whole, out_proj.shape[1]), bf16),
-            jax.ShapeDtypeStruct((n_fsdp,) + tiny.shape, bf16),
             jax.ShapeDtypeStruct((whole, mine.shape[1]), bf16),
             jax.ShapeDtypeStruct((8,) + grad.shape, bf16),
+            jax.ShapeDtypeStruct((8, length, wide), bf16),
         ],
-        in_specs=[any_spec] * 6,
-        out_specs=[any_spec] * 5,
+        in_specs=[vmem] * 6 + [any_spec] * 6,
+        out_specs=[vmem] * 8 + [any_spec] * 5,
         scratch_shapes=[
-            pltpu.VMEM(in_proj.shape, bf16),
-            pltpu.VMEM(out_proj.shape, bf16),
+            pltpu.VMEM((whole, cols), bf16),
+            pltpu.VMEM((whole, out_proj.shape[1]), bf16),
+            pltpu.VMEM((8,) + tiny.shape, bf16),
+            pltpu.VMEM((EXTRA, width), bf16),
+            pltpu.VMEM((length, length), f32),
             pltpu.VMEM(mine.shape, bf16),
-            pltpu.VMEM(tiny.shape, bf16),
             pltpu.SemaphoreType.DMA((8,)),
-            pltpu.SemaphoreType.DMA((START_SENDS,)),
-            pltpu.SemaphoreType.DMA((START_SENDS,)),
+            pltpu.SemaphoreType.DMA((FRONT_SENDS,)),
+            pltpu.SemaphoreType.DMA((FRONT_SENDS,)),
         ],
         compiler_params=pltpu.CompilerParams(
-            collective_id=1, has_side_effects=True, vmem_limit_bytes=16 * MIB
+            collective_id=1, has_side_effects=True, vmem_limit_bytes=56 * MIB
         ),
-        name="start",
-    )(in_proj, out_proj, tiny, mine, other, grad)
-
-
-ORDER = (0, 1, 2, 3, 6, 7, 5, 4)
-GROUP_AT = {1: (1, 0), 2: (2, 0), 4: (0, 2), 6: (2, 2)}
+        name="front",
+    )(
+        tokens, seg_ids.reshape(length, 1), seg_ids, routes, cos, sin,
+        in_proj, out_proj, tiny, mine, other, grad,
+    )
+
+
+ORDER = (7, 6, 3, 2, 5, 4, 1, 0)
+GROUP_AT = {2: (2, 0), 4: (0, 2), 6: (2, 2)}
 
 
 def pick(step, table):
@@ -454,47 +579,18 @@
 
 
 def group_kernel(
-    v_ref, g_ref, g_all, w_ref,
-    xs, mix_all, dx_own, dx_in, grads,
-    wbuf, xbuf, gbuf, xt, gt_, hidg, dgu, mbuf, dbuf, rc, acc, stage,
+    v_ref, g_ref, xs, g_all, w_ref, xn, attn,
+    mix_sum, dx_own, dx_in, grads, xq, aq,
+    wbuf, xbuf, gbuf, xt, gt_, hidg, dgu, deven, dodd, rc, meven, modd, mrc, acc, stage,
     sem_w, sem_x, sem_g, sem_m, sem_s, send_sem, recv_sem,
 ):
     wire = Wire(send_sem, recv_sem)
     r, f = wire.r, wire.f
     length, width = g_ref.shape
     hidden = w_ref.shape[1] // 3
+    cols_a = aq.shape[2]
     expert = 2 * r + lax.rem(f // 2, 2)
-    half = length // 2
-    low, top = pl.ds(0, half), pl.ds(half, half)
     step_cols = 256
-
-    def plan(src, dst, d):
-        copy = pltpu.make_async_remote_copy(
-            src_ref=src,
-            dst_ref=dst,
-            send_sem=send_sem.at[wire.used],
-            recv_sem=recv_sem.at[wire.used],
-            device_id=wire.at(*d),
-            device_id_type=MESH_ID,
-        )
-        wire.used += 1
-        wire.sent.append(copy)
-        return copy
-
-    tok = {
-        1: plan(v_ref, xs.at[1], (1, 0)),
-        2: plan(v_ref, xs.at[2], (2, 0)),
-        4: plan(v_ref, xs.at[4], (0, 2)),
-        3: plan(xs.at[2], xs.at[3], (1, 0)),
-        5: plan(xs.at[4], xs.at[5], (1, 0)),
-        6: plan(xs.at[4, low], xs.at[6, low], (2, 0)),
-        8: plan(xs.at[2, top], xs.at[6, top], (0, 2)),
-        7: plan(xs.at[6], xs.at[7], (1, 0)),
-    }
-    to_core = {k: plan(dbuf.at[k + 1], rc.at[k // 2], (1, 0)) for k in (0, 2, 4, 6)}
-    back = {
-        k: plan(dbuf.at[k], dx_in.at[k // 2 - 1], GROUP_AT[k]) for k in (2, 4, 6)
-    }
 
     load_w = pltpu.make_async_copy(w_ref, wbuf, sem_w.at[0])
     load_w.start()
@@ -503,38 +599,46 @@
         slot = lax.rem(step, 2)
         k = pick(step, ORDER)
 
-        @pl.when(step == 0)
+        @pl.when(k == 0)
         def _():
-            pltpu.make_async_copy(v_ref, xbuf.at[0], sem_x.at[0]).start()
-            pltpu.make_async_copy(g_ref, gbuf.at[0], sem_g.at[0]).start()
-
-        @pl.when(step > 0)
+            pltpu.make_async_copy(v_ref, xbuf.at[slot], sem_x.at[slot]).start()
+            pltpu.make_async_copy(g_ref, gbuf.at[slot], sem_g.at[slot]).start()
+
+        @pl.when(k > 0)
         def _():
             pltpu.make_async_copy(xs.at[k], xbuf.at[slot], sem_x.at[slot]).start()
             pltpu.make_async_copy(g_all.at[k], gbuf.at[slot], sem_g.at[slot]).start()
 
     load(jnp.int32(0))
     wire.meet(PARTNERS_GROUP)
-    for k in (2, 4, 1):
-        tok[k].start()
+    act = {}
+    for k in (2, 3, 1):
+        to_a = flips(r, k) * cols_a
+        act["a", k] = wire.send(
+            attn.at[:, pl.ds(pl.multiple_of(to_a, cols_a), cols_a)], aq.at[k], k, 0
+        )
+    act["x", 2] = wire.send(xn, xq.at[2], 2, 0)
+    act["x", 1] = wire.send(xn, xq.at[1], 1, 0)
+    act["x", 3] = wire.plan(xq.at[2], xq.at[3], 1, 0)
+    to_core = {k: wire.plan(dodd.at[n % 2], rc.at[n], 1, 0) for n, k in enumerate((6, 2, 4, 0))}
+    mix_core = {k: wire.plan(modd.at[n % 2], mrc.at[n], 1, 0) for n, k in enumerate((6, 2, 4, 0))}
+    back = {k: wire.plan(deven.at[k // 2], dx_in.at[k // 2 - 1], *GROUP_AT[k]) for k in (2, 4, 6)}
     acc[...] = jnp.zeros_like(acc)
     lane = lax.broadcasted_iota(jnp.int32, (length, EXTRA), 1)
     load_w.wait()
 
-    def total(k):
-        to_core[k].wait_recv()
-        dbuf[k] = (dbuf[k].astype(f32) + rc[k // 2].astype(f32)).astype(bf16)
+    def keep_mix(n, k):
+        return pltpu.make_async_copy(meven.at[n % 2], mix_sum.at[k // 2], sem_m.at[n % 2])
 
     def block(step, carry):
         slot = lax.rem(step, 2)
-        k = pick(step, ORDER)
+
+        @pl.when(step < 7)
+        def _():
+            load(step + 1)
+
         pltpu.make_async_copy(v_ref, xbuf.at[slot], sem_x.at[slot]).wait()
         pltpu.make_async_copy(g_ref, gbuf.at[slot], sem_g.at[slot]).wait()
-
-        @pl.when(step >= 2)
-        def _():
-            pltpu.make_async_copy(mbuf.at[slot], mix_all.at[0], sem_m.at[slot]).wait()
-
         extra = xbuf[slot, :, width:].astype(f32)
         mine = (lane == expert) | (lane == expert + 8)
         gate = jnp.sum(jnp.where(mine, extra, 0.0), axis=1, keepdims=True)
@@ -561,72 +665,74 @@
         dgate = lax.fori_loop(
             0, hidden // step_cols, first, jnp.zeros((length, 1), f32)
         )
-
-        def second(c, carry):
-            at = pl.multiple_of(c * step_cols, step_cols)
-            dbuf[k, :, pl.ds(at, step_cols)] = contract_cols(
-                dgu[...], wbuf[pl.ds(at, step_cols), pl.ds(0, 2 * hidden)]
-            ).astype(bf16)
-            mbuf[slot, :, pl.ds(at, step_cols)] = contract_cols(
-                hidg[...], wbuf[pl.ds(at, step_cols), pl.ds(2 * hidden, hidden)]
-            ).astype(bf16)
-            return carry
-
-        lax.fori_loop(0, width // step_cols, second, 0)
         high = dgate.astype(bf16).astype(f32)
         rest = dgate - high
-        dbuf[k, :, width:] = (
+        tail = (
             jnp.where(lane == expert, high, 0.0) + jnp.where(lane == expert + 8, rest, 0.0)
         ).astype(bf16)
-        pltpu.make_async_copy(mbuf.at[slot], mix_all.at[k], sem_m.at[slot]).start()
-
-        @pl.when(step == 0)
+
+        def out_parts(dst_d, n_d, dst_m, n_m):
+            def second(c, carry):
+                at = pl.multiple_of(c * step_cols, step_cols)
+                dst_d[n_d, :, pl.ds(at, step_cols)] = contract_cols(
+                    dgu[...], wbuf[pl.ds(at, step_cols), pl.ds(0, 2 * hidden)]
+                ).astype(bf16)
+                dst_m[n_m, :, pl.ds(at, step_cols)] = contract_cols(
+                    hidg[...], wbuf[pl.ds(at, step_cols), pl.ds(2 * hidden, hidden)]
+                ).astype(bf16)
+                return carry
+
+            lax.fori_loop(0, width // step_cols, second, 0)
+            dst_d[n_d, :, width:] = tail
+
+        pair = step // 2
+
+        @pl.when(slot == 0)
         def _():
-            tok[1].wait_recv()
-            load(step + 1)
-
-        @pl.when(step == 1)
+            for n, k in enumerate((6, 2, 4, 0)):
+                if n >= 2:
+
+                    @pl.when(pair == n)
+                    def _():
+                        to_core[(6, 2, 4, 0)[n - 2]].wait_send()
+                        mix_core[(6, 2, 4, 0)[n - 2]].wait_send()
+
+            out_parts(dodd, lax.rem(pair, 2), modd, lax.rem(pair, 2))
+            for n, k in enumerate((6, 2, 4, 0)):
+
+                @pl.when(pair == n)
+                def _():
+                    to_core[k].start()
+                    mix_core[k].start()
+                    if n == 2:
+                        act["x", 2].wait_recv()
+                        act["x", 3].start()
+
+        @pl.when(slot == 1)
         def _():
-            to_core[0].start()
-
-        @pl.when(step == 2)
-        def _():
-            tok[3].wait_recv()
-            load(step + 1)
-
-        @pl.when(step == 3)
-        def _():
-            to_core[2].start()
-            total(0)
-            tok[6].wait_recv()
-            tok[8].wait_recv()
-            tok[7].start()
-            load(step + 1)
-
-        @pl.when(step == 4)
-        def _():
-            total(2)
-            back[2].start()
-            tok[7].wait_recv()
-            load(step + 1)
-
-        @pl.when(step == 5)
-        def _():
-            to_core[6].start()
-            tok[5].wait_recv()
-            load(step + 1)
-
-        @pl.when(step == 6)
-        def _():
-            to_core[4].start()
-            total(6)
-            back[6].start()
-            load(step + 1)
-
-        @pl.when(step == 7)
-        def _():
-            total(4)
-            back[4].start()
+            for n, k in enumerate((6, 2, 4, 0)):
+                if n >= 2:
+
+                    @pl.when(pair == n)
+                    def _():
+                        keep_mix(n - 2, (6, 2, 4, 0)[n - 2]).wait()
+
+            out_parts(deven, pick(pair, (3, 1, 2, 0)), meven, lax.rem(pair, 2))
+            for n, k in enumerate((6, 2, 4, 0)):
+
+                @pl.when(pair == n)
+                def _():
+                    to_core[k].wait_recv()
+                    deven[k // 2] = (
+                        deven[k // 2].astype(f32) + rc[n].astype(f32)
+                    ).astype(bf16)
+                    if k:
+                        back[k].start()
+                    mix_core[k].wait_recv()
+                    meven[n % 2] = (
+                        meven[n % 2].astype(f32) + mrc[n].astype(f32)
+                    ).astype(bf16)
+                    keep_mix(n, k).start()
 
         def third(c, carry):
             at = pl.multiple_of(c * step_cols, step_cols)
@@ -643,24 +749,11 @@
             return carry
 
         lax.fori_loop(0, hidden // step_cols, fourth, 0)
-
-        @pl.when(step == 1)
-        def _():
-            tok[2].wait_recv()
-            tok[8].start()
-            tok[3].start()
-            load(step + 1)
-            tok[4].wait_recv()
-            tok[6].start()
-            tok[5].start()
-
         return carry
 
     lax.fori_loop(0, 8, block, 0)
-    keep = pltpu.make_async_copy(dbuf.at[0], dx_own, sem_w.at[0])
+    keep = pltpu.make_async_copy(deven.at[0], dx_own, sem_w.at[0])
     keep.start()
-    for slot in (0, 1):
-        pltpu.make_async_copy(mbuf.at[slot], mix_all.at[0], sem_m.at[slot]).wait()
     parts = 8
     rows = width // parts
 
@@ -678,16 +771,27 @@
     for j in range(parts - 2, parts):
         out(j, j % 2).wait()
     keep.wait()
+    keep_mix(2, 4).wait()
+    keep_mix(3, 0).wait()
     for k in (2, 4, 6):
         back[k].wait_recv()
+        back[k].wait_send()
+    for k in (4, 0):
+        to_core[k].wait_send()
+        mix_core[k].wait_send()
+    act["x", 1].wait_recv()
+    act["x", 3].wait_recv()
+    act["x", 3].wait_send()
+    for k in (1, 2, 3):
+        act["a", k].wait_recv()
     wire.finish()
 
 
-PARTNERS_GROUP = ((1, 0), (2, 0), (0, 2), (2, 2))
-GROUP_SENDS = 8 + 4 + 3
-
-
-def run_group(v, grad, g_all, w):
+PARTNERS_GROUP = ((1, 0), (2, 0), (3, 0), (0, 2), (2, 2))
+GROUP_SENDS = 6 + 8 + 3
+
+
+def run_group(v, grad, xs, g_all, w, xn, attn):
     length, width = grad.shape
     wide = v.shape[1]
     cols = w.shape[1]
@@ -696,14 +800,15 @@
     return pl.pallas_call(
         group_kernel,
         out_shape=[
-            jax.ShapeDtypeStruct((8, length, wide), bf16),
-            jax.ShapeDtypeStruct((8, length, width), bf16),
+            jax.ShapeDtypeStruct((4, length, width), bf16),
             jax.ShapeDtypeStruct((length, wide), bf16),
             jax.ShapeDtypeStruct((3, length, wide), bf16),
             jax.ShapeDtypeStruct((width, cols), bf16),
+            jax.ShapeDtypeStruct((4, length, width), bf16),
+            jax.ShapeDtypeStruct((4, length, attn.shape[1] // 4), bf16),
         ],
-        in_specs=[any_spec] * 4,
-        out_specs=[any_spec] * 5,
+        in_specs=[any_spec] * 7,
+        out_specs=[any_spec] * 6,
         scratch_shapes=[
             pltpu.VMEM((width, cols), bf16),
             pltpu.VMEM((2, length, wide), bf16),
@@ -712,9 +817,12 @@
             pltpu.VMEM((width, length), bf16),
             pltpu.VMEM((length, hidden), bf16),
             pltpu.VMEM((length, 2 * hidden), bf16),
+            pltpu.VMEM((4, length, wide), bf16),
+            pltpu.VMEM((2, length, wide), bf16),
+            pltpu.VMEM((4, length, wide), bf16),
             pltpu.VMEM((2, length, width), bf16),
-            pltpu.VMEM((8, length, wide), bf16),
-            pltpu.VMEM((4, length, wide), bf16),
+            pltpu.VMEM((2, length, width), bf16),
+            pltpu.VMEM((4, length, width), bf16),
             pltpu.VMEM((width, cols), f32),
             pltpu.VMEM((2, width // 8, cols), bf16),
             pltpu.SemaphoreType.DMA((1,)),
@@ -726,7 +834,7 @@
             pltpu.SemaphoreType.DMA((GROUP_SENDS,)),
         ],
         compiler_params=pltpu.CompilerParams(
-            collective_id=2, has_side_effects=True, vmem_limit_bytes=60 * MIB
+            collective_id=2, has_side_effects=True, vmem_limit_bytes=62 * MIB
         ),
         cost_estimate=pl.CostEstimate(
             flops=48 * length * width * cols,
@@ -734,25 +842,30 @@
             transcendentals=8 * length * hidden,
         ),
         name="group",
-    )(v, grad, g_all, w)
-
-
-PARTNERS_END = ((1, 0), (2, 0), (3, 0), (0, 1), (0, 2), (0, 4), (0, 6), (2, 2))
-END_SENDS = 4 + 3 + 4 + 6 + 4 + 3 + 3 * 4 + 4 + 3 + 3 + 5 + 8
-
-
-def end_kernel(
-    grads, mix_all, xn, attn, dres, dproj, terms,
-    g_out, mix_own, mix_in, d_out, terms_out,
-    gl, gy, gz, pair, ml, mrc, xq, aq, rq, pq, wq, wl, wy, wz, own_d, tbuf, tr,
+    )(v, grad, xs, g_all, w, xn, attn)
+
+
+PARTNERS_BACK = ((1, 0), (2, 0), (3, 0), (0, 1), (0, 2), (0, 4), (0, 6), (2, 2))
+BACK_SENDS = 4 + 3 + 3 + 3 + 2 * 4 + 3 + 2 * 3 + 6 + 3 + 5
+
+
+def back_kernel(
+    dx_own, g_ref, first, table, tiny, v, tokens, qkv, lse, cos, sin, seg_col, seg_row,
+    dx_in, grads, mix_sum, attn, xq, aq, xn, in_all, out_all,
+    tokens_grad, terms_out,
+    g_out, mix_in, d_out,
+    in_v, out_v, din_v, gl, gy, gz, act_v, aq_v, pq, wo, wi, wyo, wyi, wzo, wzi, own_d,
+    dn, dxn, dl, dattn, dproj, dkv, bias, tbuf, tr,
     local_sem, send_sem, recv_sem,
 ):
     wire = Wire(send_sem, recv_sem)
     r, f = wire.r, wire.f
     shard = gl.shape[1]
-    length = xn.shape[0]
+    length, width = tokens.shape
+    experts = 8
     low = lax.rem(f // 2, 2)
-    cols_p, cols_a = pq.shape[1], aq.shape[1]
+    cols_p, cols_a = pq.shape[1], aq_v.shape[1]
+    scale = HD ** (-0.5)
     used = [0]
 
     def local(src, dst):
@@ -767,133 +880,235 @@
     def token_rows(k):
         return pl.ds(k * length, length)
 
-    load_g = {j: local(grads.at[shard_rows(j)], gl.at[j // 2]) for j in (0, 2, 4, 6)}
-    load_m = {k: local(mix_all.at[k], ml.at[k // 2]) for k in (0, 2, 4, 6)}
-    loads = [
-        local(xn, xq.at[token_rows(0)]),
-        local(dres, rq.at[token_rows(0)]),
-        local(
-            attn.at[:, pl.ds(pl.multiple_of(r * cols_a, cols_a), cols_a)],
-            aq.at[token_rows(0)],
-        ),
-        local(
-            dproj.at[:, pl.ds(pl.multiple_of(r * cols_p, cols_p), cols_p)],
-            pq.at[token_rows(0)],
-        ),
-    ]
-    load_t = local(terms, tbuf.at[0])
-    wire.meet(PARTNERS_END)
-
-    act = {}
+    def part_of(k, cols):
+        return pl.ds(pl.multiple_of(flips(r, k) * cols, cols), cols)
+
+    def add(u, w):
+        return (u.astype(f32) + w.astype(f32)).astype(bf16)
+
+    load_dx = local(dx_in, din_v)
+    load_out = local(out_all, out_v)
+    load_g = {j: local(grads.at[shard_rows(j)], gl.at[j // 2]) for j in (2, 6, 4, 0)}
+    load_in = local(in_all, in_v)
+    load_a = [local(attn.at[:, part_of(0, cols_a)], aq_v.at[token_rows(0)])]
+    load_a += [local(aq.at[k], aq_v.at[token_rows(k)]) for k in (1, 2, 3)]
+    wire.meet(PARTNERS_BACK)
+    got_y, got_m = {}, {}
+    for j in (2, 6, 4, 0):
+        got_y[j] = wire.send(grads.at[shard_rows(j + 1)], gy.at[j // 2], 0, 1)
+    got_m[4] = wire.send(mix_sum.at[2], mix_in.at[1], 0, 2)
+
+    spot = lax.broadcasted_iota(jnp.int32, bias.shape, 0)
+    keys_at = lax.broadcasted_iota(jnp.int32, bias.shape, 1)
+    bias[...] = jnp.where((spot >= keys_at) & (seg_col[...] == seg_row[...]), 0.0, -1e30)
+    tbuf[0] = jnp.zeros_like(tbuf[0])
+    load_dx.wait()
+
+    def sum_dx(c, carry):
+        at = pl.ds(pl.multiple_of(c * ROWS, ROWS), ROWS)
+        d = dx_own[at, :].astype(f32)
+        for n in range(3):
+            d = d + din_v[n, at, :].astype(f32)
+        dn[at, :] = d[:, :width]
+        dgate = d[:, width:]
+        dgate = dgate + pltpu.roll(dgate, EXTRA - experts, 1)
+        gates = table[at, :]
+        mean = jnp.sum(gates * dgate, axis=-1, keepdims=True)
+        dl[at, :] = (gates * (dgate - mean)).astype(bf16)
+        return carry
+
+    lax.fori_loop(0, length // ROWS, sum_dx, 0)
+    dlt = dl[...].T[0:16]
+
+    def add_router(c, carry):
+        at = pl.ds(pl.multiple_of(c * 256, 256), 256)
+        row = lax.broadcasted_iota(jnp.int32, (16, 256), 0)
+        router = jnp.where(row < experts, tiny[:, at], 0.0).astype(bf16)
+        dn[:, at] = dn[:, at] + matmul(dl[:, 0:16], router)
+        tbuf[0, :, at] = matmul(dlt, v[:, at])
+        return carry
+
+    lax.fori_loop(0, width // 256, add_router, 0)
+
+    def norm_two(c, gain):
+        at = pl.ds(pl.multiple_of(c * ROWS, ROWS), ROWS)
+        h = first[at, :]
+        r2 = lax.rsqrt(jnp.mean(h * h, axis=-1, keepdims=True) + epsilon)
+        unit = h * r2
+        d = dn[at, :]
+        gain = gain + jnp.sum(d * unit, axis=0, keepdims=True)
+        d = d * tiny[experts + 1 : experts + 2, :]
+        d = g_ref[at, :].astype(f32) + r2 * (
+            d - unit * jnp.mean(d * unit, axis=-1, keepdims=True)
+        )
+        dn[at, :] = d
+        act_v[at, :] = d.astype(bf16)
+        return gain
+
+    gain_two = lax.fori_loop(0, length // ROWS, norm_two, jnp.zeros((1, width), f32))
+    tbuf[0, experts + 1 : experts + 2, :] = gain_two
+    got_r = {}
+    got_r[2] = wire.send(act_v.at[token_rows(0)], act_v.at[token_rows(2)], 2, 0)
+    got_r[1] = wire.send(act_v.at[token_rows(0)], act_v.at[token_rows(1)], 1, 0)
+    load_out.wait()
+
+    def to_attn(c, carry):
+        at = pl.ds(pl.multiple_of(c * 256, 256), 256)
+        dattn[:, at] = matmul(act_v[0:length, :], out_v[:, at]).astype(bf16)
+        return carry
+
+    lax.fori_loop(0, WQ // 256, to_attn, 0)
+    lane = lax.broadcasted_iota(jnp.int32, (length, HD), 1)
+
+    def turn_back(w):
+        return w * cos[...] - pltpu.roll(w, HD // 2, 1) * sin[...]
+
+    got_z = {}
+
+    def pass_y(j):
+        load_g[j].wait()
+        got_y[j].wait_recv()
+        gl[j // 2] = add(gl[j // 2], gy[j // 2])
+        got_z[j] = wire.send(gl.at[j // 2], gz.at[j // 2 - 1], 0, j)
+
+    for group in range(KV):
+        k_at = pl.ds(WQ + group * HD, HD)
+        v_at = pl.ds(WQ + WK + group * HD, HD)
+        dkv[...] = jnp.zeros_like(dkv)
+
+        def head(i, carry):
+            h = group * GROUP + i
+            at = pl.ds(pl.multiple_of(h * HD, HD), HD)
+            s = contract_cols(qkv[:, at], qkv[:, k_at]) * scale + bias[...]
+            level = jnp.sum(jnp.where(lane == h, lse[...], 0.0), axis=1, keepdims=True)
+            p = jnp.exp(s - level)
+            da = dattn[:, at]
+            dp = contract_cols(da, qkv[:, v_at])
+            delta = jnp.sum(p * dp, axis=-1, keepdims=True)
+            ds = (p * (dp - delta)).astype(bf16)
+            dkv[1] += contract_rows(p.astype(bf16), da)
+            dkv[0] += contract_rows(ds, qkv[:, at])
+            dproj[:, at] = turn_back(matmul(ds, qkv[:, k_at]) * scale).astype(bf16)
+            return carry
+
+        lax.fori_loop(0, GROUP, head, 0)
+        dproj[:, k_at] = turn_back(dkv[0] * scale).astype(bf16)
+        dproj[:, v_at] = dkv[1].astype(bf16)
+        if group == 0:
+            got_r[2].wait_recv()
+            got_r[3] = wire.send(act_v.at[token_rows(2)], act_v.at[token_rows(3)], 1, 0)
+
+    keep_p = local(dproj.at[:, part_of(0, cols_p)], pq.at[token_rows(0)])
+    got_p = {}
+    for k in (2, 3, 1):
+        got_p[k] = wire.send(dproj.at[:, part_of(k, cols_p)], pq.at[token_rows(k)], k, 0)
+    got_m[2] = wire.send(mix_sum.at[1], mix_in.at[0], 2, 0)
+    got_m[6] = wire.send(mix_sum.at[3], mix_in.at[2], 2, 2)
+
+    for copy in load_a:
+        copy.wait()
+    got_r[1].wait_recv()
+    got_r[3].wait_recv()
+
+    def dense_out(c, carry):
+        at = pl.ds(pl.multiple_of(c * 256, 256), 256)
+        wo[at, :] = matmul(act_v[:, at].T, aq_v[...]).astype(bf16)
+        return carry
+
+    lax.fori_loop(0, width // 256, dense_out, 0)
+    for copy in (got_r[2], got_r[1], got_r[3]):
+        copy.wait_send()
+    load_x = [local(xn, act_v.at[token_rows(0)])]
+    load_x += [local(xq.at[k], act_v.at[token_rows(k)]) for k in (1, 2, 3)]
+    got_wo, got_wi, got_wzo, got_wzi = {}, {}, {}, {}
+    for j in (2, 6, 4, 0):
+        got_wo[j] = wire.send(wo.at[shard_rows(j + 1)], wyo.at[j // 2], 0, 1)
+    pass_y(2)
+
+    keep_p.wait()
+    for copy in load_x:
+        copy.wait()
     for k in (1, 2, 3):
-        to_p = flips(r, k) * cols_p
-        to_a = flips(r, k) * cols_a
-        act["p", k] = wire.send(
-            dproj.at[:, pl.ds(pl.multiple_of(to_p, cols_p), cols_p)],
-            pq.at[token_rows(k)], k, 0,
-        )
-        act["a", k] = wire.send(
-            attn.at[:, pl.ds(pl.multiple_of(to_a, cols_a), cols_a)],
-            aq.at[token_rows(k)], k, 0,
-        )
-    for k in (2, 1):
-        act["x", k] = wire.send(xn, xq.at[token_rows(k)], k, 0)
-        act["r", k] = wire.send(dres, rq.at[token_rows(k)], k, 0)
-    got_y = {
-        j: wire.send(grads.at[shard_rows(j + 1)], gy.at[j // 2], 0, 1) for j in (2, 4, 6, 0)
-    }
-    got_mc = {k: wire.send(mix_all.at[k + 1], mrc.at[k // 2], 1, 0) for k in (2, 4, 6, 0)}
-
-    load_t.wait()
-
+        got_p[k].wait_recv()
+
+    def dense_in(c, carry):
+        at = pl.ds(pl.multiple_of(c * 256, 256), 256)
+        wi[at, :] = matmul(act_v[:, at].T, pq[...]).astype(bf16)
+        return carry
+
+    lax.fori_loop(0, width // 256, dense_in, 0)
+    for j in (2, 6, 4, 0):
+        got_wi[j] = wire.send(wi.at[shard_rows(j + 1)], wyi.at[j // 2], 0, 1)
+    pass_y(6)
+
+    load_in.wait()
+
+    def to_norm(c, carry):
+        at = pl.ds(pl.multiple_of(c * 256, 256), 256)
+        dxn[:, at] = contract_cols(dproj[...], in_v[at, :])
+        return carry
+
+    lax.fori_loop(0, width // 256, to_norm, 0)
+
+    def norm_one(c, gain):
+        at = pl.ds(pl.multiple_of(c * ROWS, ROWS), ROWS)
+        x = tokens[at, :].astype(f32)
+        r1 = lax.rsqrt(jnp.mean(x * x, axis=-1, keepdims=True) + epsilon)
+        unit = x * r1
+        d = dxn[at, :]
+        gain = gain + jnp.sum(d * unit, axis=0, keepdims=True)
+        d = d * tiny[experts : experts + 1, :]
+        d = dn[at, :] + r1 * (d - unit * jnp.mean(d * unit, axis=-1, keepdims=True))
+        tokens_grad[at, :] = d.astype(bf16)
+        return gain
+
+    gain_one = lax.fori_loop(0, length // ROWS, norm_one, jnp.zeros((1, width), f32))
+    tbuf[0, experts : experts + 1, :] = gain_one
+    pass_y(4)
     for n, d in enumerate(((1, 0), (0, 1), (2, 0), (0, 2), (0, 4))):
         copy = wire.send(tbuf.at[n], tr.at[n], *d)
         copy.wait_recv()
         tbuf[n + 1] = tbuf[n] + tr[n]
-    keep_t = local(tbuf.at[5], terms_out)
-
-    for k in ("x", "r"):
-        act[k, 2].wait_recv()
-        buf = xq if k == "x" else rq
-        act[k, 3] = wire.send(buf.at[token_rows(2)], buf.at[token_rows(3)], 1, 0)
-    for copy in loads:
-        copy.wait()
-    for k in (1, 2, 3):
-        for name in ("p", "a", "r", "x"):
-            if (name, k) != ("x", 2) and (name, k) != ("r", 2):
-                act[name, k].wait_recv()
-
-    part = 256
-
-    def dense(c, carry):
-        at = pl.multiple_of(c * part, part)
-        wq[pl.ds(at, part), pl.ds(0, cols_p)] = matmul(
-            xq[:, pl.ds(at, part)].T, pq[...]
-        ).astype(bf16)
-        wq[pl.ds(at, part), pl.ds(cols_p, cols_a)] = matmul(
-            rq[:, pl.ds(at, part)].T, aq[...]
-        ).astype(bf16)
-        return carry
-
-    lax.fori_loop(0, wq.shape[0] // part, dense, 0)
-    got_wy = {
-        j: wire.send(wq.at[shard_rows(j + 1)], wy.at[j // 2], 0, 1) for j in (2, 4, 6, 0)
-    }
-
-    def add(u, v):
-        return (u.astype(f32) + v.astype(f32)).astype(bf16)
-
-    got_m = {}
-    for k, d in ((2, (2, 0)), (4, (0, 2)), (6, (2, 2))):
-        load_m[k].wait()
-        got_mc[k].wait_recv()
-        ml[k // 2] = add(ml[k // 2], mrc[k // 2])
-        got_m[k] = wire.send(ml.at[k // 2], mix_in.at[k // 2 - 1], *d)
-    load_m[0].wait()
-    got_mc[0].wait_recv()
-    ml[0] = add(ml[0], mrc[0])
-    keep_m = local(ml.at[0], mix_own)
-
-    got_z = {}
-    for j in (2, 4, 6):
-        load_g[j].wait()
-        got_y[j].wait_recv()
-        gl[j // 2] = add(gl[j // 2], gy[j // 2])
-        got_z[j] = wire.send(gl.at[j // 2], gz.at[j // 2 - 1], 0, j)
+    terms_out[...] = tbuf[5]
+
+    for j in (2, 6, 4):
+        got_wo[j].wait_recv()
+        wyo[j // 2] = add(wo[shard_rows(j), :], wyo[j // 2])
+        got_wzo[j] = wire.send(wyo.at[j // 2], wzo.at[j // 2 - 1], 0, j)
+    for j in (2, 6, 4):
+        got_wi[j].wait_recv()
+        wyi[j // 2] = add(wi[shard_rows(j), :], wyi[j // 2])
+        got_wzi[j] = wire.send(wyi.at[j // 2], wzi.at[j // 2 - 1], 0, j)
+
+    mine, other = 2 * r + low, 2 * r + 1 - low
     load_g[0].wait()
     got_y[0].wait_recv()
-
-    got_wz = {}
-    for j in (2, 4, 6):
-        wl[j // 2] = wq[shard_rows(j)]
-        got_wy[j].wait_recv()
-        wl[j // 2] = add(wl[j // 2], wy[j // 2])
-        got_wz[j] = wire.send(wl.at[j // 2], wz.at[j // 2 - 1], 0, j)
-    got_wy[0].wait_recv()
-    own = wq[shard_rows(0)].astype(f32) + wy[0].astype(f32)
-
     got_z[4].wait_recv()
-    pair[0] = (
-        gl[0].astype(f32) + gy[0].astype(f32) + gz[1].astype(f32)
-    ).astype(bf16)
-    mine, other = 2 * r + low, 2 * r + 1 - low
-    kept = [local(pair.at[0], g_out.at[mine])]
+    got_z[2].wait_send()
+    gl[0] = (gl[0].astype(f32) + gy[0].astype(f32) + gz[1].astype(f32)).astype(bf16)
+    kept = [local(gl.at[0], g_out.at[mine])]
     got_e = {}
-    got_e[2, 0] = wire.send(pair.at[0], g_out.at[mine], 2, 0)
-    got_e[1, 0] = wire.send(pair.at[0], g_out.at[mine], 1, 0)
+    got_e[2, 0] = wire.send(gl.at[0], g_out.at[mine], 2, 0)
+    got_e[1, 0] = wire.send(gl.at[0], g_out.at[mine], 1, 0)
     got_z[2].wait_recv()
     got_z[6].wait_recv()
-    pair[1] = add(gz[0], gz[2])
-    kept.append(local(pair.at[1], g_out.at[other]))
-    got_e[2, 1] = wire.send(pair.at[1], g_out.at[other], 2, 0)
-    got_e[1, 1] = wire.send(pair.at[1], g_out.at[other], 1, 0)
-
-    for j in (2, 4, 6):
-        got_wz[j].wait_recv()
-        own = own + wz[j // 2 - 1].astype(f32)
-    own_d[...] = own.astype(bf16)
+    gz[0] = add(gz[0], gz[2])
+    kept.append(local(gz.at[0], g_out.at[other]))
+    got_e[2, 1] = wire.send(gz.at[0], g_out.at[other], 2, 0)
+    got_e[1, 1] = wire.send(gz.at[0], g_out.at[other], 1, 0)
+
+    def own_rows(w, y, z, got_w, got_zs, cols):
+        got_w[0].wait_recv()
+        total = w[shard_rows(0), :].astype(f32) + y[0].astype(f32)
+        for j in (2, 4, 6):
+            got_zs[j].wait_recv()
+            total = total + z[j // 2 - 1].astype(f32)
+        own_d[:, cols] = total.astype(bf16)
+
+    own_rows(wo, wyo, wzo, got_wo, got_wzo, pl.ds(cols_p, cols_a))
+    own_rows(wi, wyi, wzi, got_wi, got_wzi, pl.ds(0, cols_p))
     kept.append(local(own_d, d_out.at[r]))
-    got_d = [wire.send(own_d, d_out.at[r], k, 0) for k in (1, 2, 3)]
+    got_d = [wire.send(own_d, d_out.at[r], k, 0) for k in (2, 3, 1)]
 
     far = flips(r, 2)
     for n, e in ((0, 2 * far + low), (1, 2 * far + 1 - low)):
@@ -906,102 +1121,131 @@
         copy.wait_recv()
     for k in (2, 4, 6):
         got_m[k].wait_recv()
-    for copy in kept + [keep_m, keep_t]:
+    for copy in kept:
         copy.wait()
-    wire.finish()
-
-
-def run_end(grads, mix_all, xn, attn, dres, dproj, terms):
-    length, width = xn.shape
+    wire.finish((got_r[2], got_r[1], got_r[3], got_z[2]))
+
+
+def run_back(
+    dx_own, grad, first, table, tiny, v, tokens, qkv, lse, cos, sin, seg_ids,
+    dx_in, grads, mix_sum, attn, xq, aq, xn, in_all, out_all,
+):
+    any_spec = pl.BlockSpec(memory_space=pl.ANY)
+    vmem = pl.BlockSpec(memory_space=pltpu.VMEM)
+    length, width = tokens.shape
     shard = width // 8
     cols = grads.shape[1]
-    cols_p, cols_a = dproj.shape[1] // 4, attn.shape[1] // 4
-    dense = cols_p + cols_a
-    any_spec = pl.BlockSpec(memory_space=pl.ANY)
+    cols_p, cols_a = qkv.shape[1] // 4, attn.shape[1] // 4
     return pl.pallas_call(
-        end_kernel,
+        back_kernel,
         out_shape=[
+            jax.ShapeDtypeStruct((length, width), bf16),
+            jax.ShapeDtypeStruct((16, width), f32),
             jax.ShapeDtypeStruct((8, shard, cols), bf16),
-            jax.ShapeDtypeStruct((length, width), bf16),
             jax.ShapeDtypeStruct((3, length, width), bf16),
-            jax.ShapeDtypeStruct((4, shard, dense), bf16),
-            jax.ShapeDtypeStruct(terms.shape, f32),
+            jax.ShapeDtypeStruct((4, shard, cols_p + cols_a), bf16),
         ],
-        in_specs=[any_spec] * 7,
-        out_specs=[any_spec] * 5,
+        in_specs=[vmem] * 13 + [any_spec] * 9,
+        out_specs=[vmem] * 2 + [any_spec] * 3,
         scratch_shapes=[
+            pltpu.VMEM(in_all.shape, bf16),
+            pltpu.VMEM(out_all.shape, bf16),
+            pltpu.VMEM(dx_in.shape, bf16),
             pltpu.VMEM((4, shard, cols), bf16),
             pltpu.VMEM((4, shard, cols), bf16),
             pltpu.VMEM((3, shard, cols), bf16),
-            pltpu.VMEM((2, shard, cols), bf16),
-            pltpu.VMEM((4, length, width), bf16),
-            pltpu.VMEM((4, length, width), bf16),
             pltpu.VMEM((4 * length, width), bf16),
             pltpu.VMEM((4 * length, cols_a), bf16),
-            pltpu.VMEM((4 * length, width), bf16),
             pltpu.VMEM((4 * length, cols_p), bf16),
-            pltpu.VMEM((width, dense), bf16),
-            pltpu.VMEM((4, shard, dense), bf16),
-            pltpu.VMEM((4, shard, dense), bf16),
-            pltpu.VMEM((3, shard, dense), bf16),
-            pltpu.VMEM((shard, dense), bf16),
-            pltpu.VMEM((6,) + terms.shape, f32),
-            pltpu.VMEM((5,) + terms.shape, f32),
-            pltpu.SemaphoreType.DMA((24,)),
-            pltpu.SemaphoreType.DMA((END_SENDS,)),
-            pltpu.SemaphoreType.DMA((END_SENDS,)),
+            pltpu.VMEM((width, cols_a), bf16),
+            pltpu.VMEM((width, cols_p), bf16),
+            pltpu.VMEM((4, shard, cols_a), bf16),
+            pltpu.VMEM((4, shard, cols_p), bf16),
+            pltpu.VMEM((3, shard, cols_a), bf16),
+            pltpu.VMEM((3, shard, cols_p), bf16),
+            pltpu.VMEM((shard, cols_p + cols_a), bf16),
+            pltpu.VMEM((length, width), f32),
+            pltpu.VMEM((length, width), f32),
+            pltpu.VMEM((length, EXTRA), bf16),
+            pltpu.VMEM((length, WQ), bf16),
+            pltpu.VMEM(qkv.shape, bf16),
+            pltpu.VMEM((2, length, HD), f32),
+            pltpu.VMEM((length, length), f32),
+            pltpu.VMEM((6, 16, width), f32),
+            pltpu.VMEM((5, 16, width), f32),
+            pltpu.SemaphoreType.DMA((20,)),
+            pltpu.SemaphoreType.DMA((BACK_SENDS,)),
+            pltpu.SemaphoreType.DMA((BACK_SENDS,)),
         ],
         compiler_params=pltpu.CompilerParams(
-            collective_id=3, has_side_effects=True, vmem_limit_bytes=60 * MIB
+            collective_id=3, has_side_effects=True, vmem_limit_bytes=62 * MIB
         ),
-        name="end",
-    )(grads, mix_all, xn, attn, dres, dproj, terms)
-
-
-class Near:
-    def __init__(self, n_rep, n_fsdp):
-        self.n_fsdp = n_fsdp
-
-    def start(self, in_proj, out_proj, tiny, expert_in, expert_out, grad):
-        r, f = lax.axis_index("replica"), lax.axis_index("fsdp")
-        low = (f >> 1) & 1
-        mine, other = [
-            jnp.concatenate(
-                [
-                    lax.dynamic_index_in_dim(expert_in, e, 1, keepdims=False),
-                    lax.dynamic_index_in_dim(expert_out, e, 1, keepdims=False),
-                ],
-                axis=1,
-            )
-            for e in (2 * r + low, 2 * r + 1 - low)
-        ]
-        pad = jnp.pad(tiny, ((0, 0), (0, -tiny.shape[1] % 128)))
-        proj_in, proj_out, tiny_all, weights, gs = start(
-            in_proj, out_proj, pad, mine, other, grad, self.n_fsdp
+        name="back",
+    )(
+        dx_own, grad, first, table, tiny, v, tokens, qkv, lse, cos, sin,
+        seg_ids.reshape(length, 1), seg_ids,
+        dx_in, grads, mix_sum, attn, xq, aq, xn, in_all, out_all,
+    )
+
+
+def near_layer(
+    tokens, seg_ids, routes, in_proj, out_proj, router, norm_gains, expert_in, expert_out,
+    out_grad,
+):
+    length, width = tokens.shape
+    experts = router.shape[1]
+    hidden = expert_out.shape[2]
+    shard = router.shape[0]
+    r, f = lax.axis_index("replica"), lax.axis_index("fsdp")
+    cosine, sine = [t[:, 0] for t in tables(length)]
+    cos = jnp.concatenate([cosine, cosine], axis=1)
+    sin = jnp.concatenate([-sine, sine], axis=1)
+    tiny = jnp.concatenate(
+        [router.T, norm_gains.T, jnp.zeros((16 - experts - 2, shard), bf16)], axis=0
+    )
+    none = jnp.zeros_like(tiny)
+    tiny = jnp.where(
+        f % 2 == 0,
+        jnp.concatenate([tiny, none], axis=1),
+        jnp.concatenate([none, tiny], axis=1),
+    )
+    low = (f >> 1) & 1
+    mine, other = [
+        jnp.concatenate(
+            [
+                lax.dynamic_index_in_dim(expert_in, e, 1, keepdims=False),
+                lax.dynamic_index_in_dim(expert_out, e, 1, keepdims=False),
+            ],
+            axis=1,
         )
-        tiny_all = tiny_all[:, :, : tiny.shape[1]].transpose(1, 0, 2).reshape(16, -1)
-        return proj_in, proj_out, tiny_all, (weights, gs, grad)
-
-    def experts(self, payload, held):
-        weights, gs, grad = held
-        _, mix_all, dx_own, dx_in, grads = run_group(payload, grad, gs, weights)
-        dx = dx_own.astype(f32)
-        for k in range(3):
-            dx = dx + dx_in[k].astype(f32)
-        return dx, (mix_all, grads)
-
-    def end(self, held, first, normed, attn, dres, dproj, terms):
-        mix_all, grads = held
-        expert_sum, mix_own, mix_in, dense, terms = run_end(
-            grads, mix_all, normed, attn, dres, dproj, terms
-        )
-        mixed = first + mix_own.astype(f32)
-        for k in range(3):
-            mixed = mixed + mix_in[k].astype(f32)
-        cut = dproj.shape[1] // 4
-        in_grad = dense[:, :, :cut].transpose(1, 0, 2).reshape(dense.shape[1], -1)
-        out_grad = dense[:, :, cut:].transpose(1, 0, 2).reshape(dense.shape[1], -1)
-        return mixed, in_grad, out_grad, expert_sum.transpose(1, 0, 2), terms
+        for e in (2 * r + low, 2 * r + 1 - low)
+    ]
+    qkv, attn, xn, first, lse, table, small, v, in_all, out_all, w_all, g_all, xs = front(
+        tokens, seg_ids, routes, cos, sin, in_proj, out_proj, tiny, mine, other, out_grad
+    )
+    mix_sum, dx_own, dx_in, grads, xq, aq = run_group(v, out_grad, xs, g_all, w_all, xn, attn)
+    tokens_grad, terms, expert_sum, mix_in, dense = run_back(
+        dx_own, out_grad, first, table, small, v, tokens, qkv, lse, cos, sin, seg_ids,
+        dx_in, grads, mix_sum, attn, xq, aq, xn, in_all, out_all,
+    )
+    mixed = first + mix_sum[0].astype(f32)
+    for k in range(3):
+        mixed = mixed + mix_in[k].astype(f32)
+    cut = in_proj.shape[1] // 4
+    in_grad = dense[:, :, :cut].transpose(1, 0, 2).reshape(shard, -1)
+    out_proj_grad = dense[:, :, cut:].transpose(1, 0, 2).reshape(shard, -1)
+    expert_sum = expert_sum.transpose(1, 0, 2)
+    terms = lax.dynamic_slice_in_dim(terms, f * shard, shard, 1).T
+    return (
+        mixed.astype(bf16),
+        tokens_grad,
+        in_grad.astype(f32),
+        out_proj_grad.astype(f32),
+        terms[:, :experts],
+        terms[:, experts : experts + 2],
+        expert_sum[..., : 2 * hidden].astype(f32),
+        expert_sum[..., 2 * hidden :].astype(f32),
+    )
 
 
 class Wide:
@@ -1194,11 +1438,14 @@
 
 def solution(mesh):
     n_rep, n_fsdp = mesh.shape["replica"], mesh.shape["fsdp"]
-    net = Near(n_rep, n_fsdp) if (n_rep, n_fsdp) == (4, 8) else Wide(n_rep, n_fsdp)
+    if (n_rep, n_fsdp) == (4, 8):
+        body = near_layer
+    else:
+        body = functools.partial(layer, Wide(n_rep, n_fsdp))
     both = P(("replica", "fsdp"), None)
     fsdp, deep = P("fsdp", None), P("fsdp", None, None)
     return jax.shard_map(
-        functools.partial(layer, net),
+        body,
         mesh=mesh,
         in_specs=(both, both, both, fsdp, fsdp, fsdp, fsdp, deep, deep, both),
         out_specs=(both, both, fsdp, fsdp, fsdp, fsdp, deep, deep),

time: 746 us -> 582 us (0.78); the launches traced: 736 us -> 580 us
  matrix products: 54.5 us -> 0 us
  local copies, waits for them, and re-layouts: 81.4 us -> 29.6 us
  other arithmetic: 41.2 us -> 12 us
  Pallas kernels: 557 us -> 537 us
    dot_general x13 -> x0, matrix products: 54.5 us -> none  [the longest x3 13.7 us: matmul(): lax.dot_general(left, right, (((1,), (0,)), ((), ())), preferred_element_...]
    unnamed x128 -> x14, local copies, waits for them, and re-layouts: 36.6 us -> 16.7 us
    pallas_call x3, Pallas kernels: 557 us -> 537 us  [the longest x1 226 us: run_back(): pl.pallas_call(back_kernel, out_shape=[jax.ShapeDtypeStruct((length, widt...]
    convert_element_type x9 -> x3, other arithmetic: 17.6 us -> 6.69 us  [the longest x1 4.98 us: near_layer(): mixed.astype(bf16)]
    slice x10 -> x2, local copies, waits for them, and re-layouts: 10.8 us -> 1.18 us  [the longest x1 0.6 us: near_layer(): terms[:, :experts]]
where the time goes in v3:
time: 582 us; the launch traced here: 580 us
  Pallas kernels  537 us (92%)
  local copies, waits for them, and re-layouts  29.6 us (5%)
  other arithmetic  12 us (2%)
    pallas_call x1, Pallas kernels, run_back(): pl.pallas_call(back_kernel, out_shape=[jax.ShapeDtypeStruct((length, widt...  226 us
    pallas_call x1, Pallas kernels, front(): pl.pallas_call(front_kernel, out_shape=[jax.ShapeDtypeStruct((length, col...  190 us
    pallas_call x1, Pallas kernels, run_group(): pl.pallas_call(group_kernel, out_shape=[jax.ShapeDtypeStruct((4, length,...  122 us
    unnamed x14, local copies, waits for them, and re-layouts  16.7 us

profile of v3, /device:TPU:1, one launch (start us, length us, event | category | flops | bytes accessed | tf_op | source)
XLA Modules:
  0.0 579.6 jit_solution(16528924863322862055)
XLA Ops:
  0.7 0.1 pad.8.clone
  0.8 0.8 maximum_maximum_fusion
  1.5 0.7 pad_select_fusion.tiny_ref
  2.2 1.5 copy.25.seg_col
  3.7 1.5 copy.26.routes
  5.2 0.7 fusion.3
  6.0 0.0 copy-start.1
  6.0 0.9 pad_maximum_fusion.2
  6.9 4.2 constant_dynamic-slice_fusion
  11.1 0.1 copy_bitcast_fusion.2
  11.2 2.4 constant_dynamic-slice_fusion.1
  13.6 0.2 copy_bitcast_fusion
  13.8 1.0 pad_maximum_fusion.1.other_ref
  14.7 1.0 pad_maximum_fusion.mine_ref
  15.7 190.0 %front.1 = (bf16[384,2048]{1,0:T(8,128)(2,1)}, bf16[384,1536]{1,0:T(8,128)(2,1)}, bf16[384,1536]{1,0:T(8,128)(2,1)}, f32[384,1536]{1,0:T(8,128)}, f32[384,128]{1...) custom-call(bf16[384,1536]{1,0:T(8,128)(2,1)} %tokens.3, ...), custom_call_target="tpu_custom_call" | custom-call | tf_op jit(solution)/shard_map/front/pallas_call | solution.py:530
  205.7 121.7 %group.1 = (bf16[4,384,1536]{2,1,0:T(8,128)(2,1)}, bf16[384,1664]{1,0:T(8,128)(2,1)}, bf16[3,384,1664]{2,1,0:T(8,128)(2,1)}, bf16[1536,2304]{1,0:T(8,128)(2,1)},...) custom-call(bf16[384,1664]{1,0:T(8,128)(2,1)} %get-tuple-element.33.v_ref.v, bf16[384,1536]{1,0:T(8,128)(2,1)} %g_ref.5, ...), custom_call_target="tpu_custom_call" | custom-call | flops 65229815808 | bytes 51904512 | tf_op jit(solution)/shard_map/group/pallas_call | solution.py:800
  327.4 225.6 %back.1 = (bf16[384,1536]{1,0:T(8,128)(2,1)}, f32[16,1536]{1,0:T(8,128)}, bf16[8,192,2304]{2,1,0:T(8,128)(2,1)}, bf16[3,384,1536]{2,1,0:T(8,128)(2,1)}, bf16[4,192,896]{2,1,0:T(8,128)(2,1)}) custom-call(bf16[384,1664]{1,0:T(8,128)(2,1)} %get-tuple-element.40.dx_own, bf16[384,1536]{1,0:T(8,128)(2,1)} %g_ref.5, f32[384,1536]{1,0:T(8,128)} %get-tuple-element.32.first, ...), custom_call_target="tpu_custom_call" | custom-call | tf_op jit(solution)/shard_map/back/pallas_call | solution.py:1139
  553.0 0.0 slice-start
  553.0 5.0 fusion
  558.0 0.8 dynamic-slice_bitcast_fusion
  558.8 0.6 slice.41
  559.4 0.6 slice.40
  560.0 0.1 convert_bitcast_fusion.1
  560.0 1.2 copy.37
  561.2 0.2 convert_bitcast_fusion
  561.4 1.3 copy.36
  562.7 0.0 slice-done.1
  562.7 0.4 slice_convert_fusion.1
  563.2 4.9 copy.31
  568.1 1.3 slice_convert_fusion
  569.4 9.2 %copy.30 = f32[192,8,1536]{2,1,0:T(8,128)} copy(f32[192,8,1536]{2,0,1:T(8,128)S(1)} %slice_convert_fusion) | data formatting | bytes 18874368
  578.6 1.0 copy.43
  (10 shorter events, 0.0 us)
Async XLA Ops:
  6.0 5.2 copy-start.1
  553.0 7.0 %copy-start = (bf16[4,192,896]{2,1,0:T(8,128)(2,1)S(1)}, bf16[4,192,896]{2,1,0:T(8,128)(2,1)}, u32[]{:S(2)}) copy-start(bf16[4,192,896]{2,1,0:T(8,128)(2,1)} %get-tuple-element.53) | copy-start | bytes 4128772
  553.0 9.7 %slice-start = ((s8[7077888]{0:T(1024)(128)(4,1)}), s8[4194304]{0:T(1024)(128)(4,1)S(1)}, s32[]{:S(2)}) async-start(s8[7077888]{0:T(1024)(128)(4,1)} %bitcast.34), calls=%async_computation | async-start | bytes 8388608
  560.0 2.8 slice-start.1
  569.4 9.2 %copy-start.2 = (bf16[384,1536]{1,0:T(8,128)(2,1)S(1)}, bf16[384,1536]{1,0:T(8,128)(2,1)}, u32[]{:S(2)}) copy-start(bf16[384,1536]{1,0:T(8,128)(2,1)} %get-tuple-element.94) | copy-start | bytes 3538948

commit v4 on v3

--- a/solution.py
+++ b/solution.py
@@ -276,6 +276,7 @@
             device_id_type=MESH_ID,
         )
         self.used += 1
+        assert self.used <= self.send_sem.shape[0]
         return copy
 
     def send(self, src, dst, d_r, d_f):
@@ -290,7 +291,8 @@
                 copy.wait_send()
 
 
-FRONT_SENDS = 2 * 28 + 7 + 7 + 8 + 8
+CUTS = 2
+FRONT_SENDS = 2 * 28 + 7 + 7 * CUTS + 4 + 3
 PARTNERS = ((1, 0), (2, 0), (0, 1), (0, 2), (0, 4), (0, 6))
 ROWS = 64
 
@@ -311,8 +313,6 @@
     shard = in_ref.shape[0]
     quarter = shard // 4
     length, width = tokens.shape
-    half = length // 2
-    low, top = pl.ds(0, half), pl.ds(half, half)
     experts = 8
     scale = HD ** (-0.5)
 
@@ -377,6 +377,7 @@
             got[name, m, 3].wait_recv()
 
     own_pieces("in")
+    own_pieces("out")
     own_w.wait()
     kept = [local(4, w_buf, w_all.at[shard_rows(0)])]
 
@@ -407,14 +408,31 @@
     keys_at = lax.broadcasted_iota(jnp.int32, bias.shape, 1)
     bias[...] = jnp.where((spot >= keys_at) & (seg_col[...] == seg_row[...]), 0.0, -1e30)
 
+    cut = shard // CUTS
+
+    def send_w(n, src, d_f):
+        at = pl.ds(n * cut, cut)
+        to = pl.ds(pl.multiple_of(f * shard + n * cut, cut), cut)
+        return wire.send(src.at[at], w_all.at[to], 0, d_f)
+
+    def pass_w(n, m):
+        got_w[m, n].wait_recv()
+        at = w_all.at[pl.ds(pl.multiple_of(flips(f, m) * shard + n * cut, cut), cut)]
+        got_w[m + 1, n] = wire.send(at, at, 0, 1)
+
     near_pieces("in")
-    own_pieces("out")
+    for n in range(CUTS):
+        for m, src in ((2, other_ref), (4, mine_ref), (6, other_ref)):
+            got_w[m, n] = send_w(n, src, m)
+    got_g[4] = wire.send(g_ref, g_all.at[4], 0, 2)
+    got_g[1] = wire.send(g_ref, g_all.at[1], 1, 0)
     far_pieces("in")
+    near_pieces("out")
+    far_pieces("out")
+    for n in range(CUTS):
+        got_w[1, n] = send_w(n, mine_ref, 1)
+    got_g[2] = wire.send(g_ref, g_all.at[2], 2, 0)
     side_pieces("in")
-    near_pieces("out")
-    for m, src in ((2, other_ref), (4, mine_ref), (6, other_ref)):
-        got_w[m] = wire.send(src, w_all.at[shard_rows(0)], 0, m)
-    got_w[1] = wire.send(mine_ref, w_all.at[shard_rows(0)], 0, 1)
     own_in.wait()
     all_pieces("in")
 
@@ -431,11 +449,7 @@
         return carry
 
     lax.fori_loop(0, 8, project, 0)
-    far_pieces("out")
-    side_pieces("out")
-    got_g[2] = wire.send(g_ref, g_all.at[2], 2, 0)
-    got_g[4] = wire.send(g_ref, g_all.at[4], 0, 2)
-    got_g[1] = wire.send(g_ref, g_all.at[1], 1, 0)
+    pass_w(0, 2)
     lane = lax.broadcasted_iota(jnp.int32, (length, HD), 1)
     lse[...] = jnp.zeros_like(lse)
 
@@ -453,7 +467,11 @@
         lse[...] = jnp.where(lane == h, highest + jnp.log(total), lse[...])
         return carry
 
-    lax.fori_loop(0, HQ, head, 0)
+    lax.fori_loop(0, HQ // 2, head, 0)
+    side_pieces("out")
+    pass_w(0, 4)
+    lax.fori_loop(HQ // 2, HQ, head, 0)
+    pass_w(0, 6)
     own_out.wait()
     all_pieces("out")
     kept.append(local(5, in_v, in_all))
@@ -487,33 +505,20 @@
     v[:, width:] = (high + pltpu.roll(gates - high, experts, 1)).astype(bf16)
 
     got_x[2] = wire.send(v, xs.at[2], 2, 0)
-    got_x[4] = wire.send(v, xs.at[4], 0, 2)
     got_x[1] = wire.send(v, xs.at[1], 1, 0)
-
-    def onward(got_some, buf):
-        for m in (2, 4):
-            got_some[m].wait_recv()
-            got_some[m + 1] = wire.send(buf.at[m], buf.at[m + 1], 1, 0)
-        return [
-            wire.send(buf.at[4, low], buf.at[6, low], 2, 0),
-            wire.send(buf.at[2, top], buf.at[6, top], 0, 2),
-        ]
-
-    far_g = onward(got_g, g_all)
-    for m in (2, 4, 6):
-        got_w[m].wait_recv()
-        at = w_all.at[shard_rows(m)]
-        got_w[m + 1] = wire.send(at, at, 0, 1)
-    far_x = onward(got_x, xs)
-    for copy in far_g:
-        copy.wait_recv()
-    got_g[7] = wire.send(g_all.at[6], g_all.at[7], 1, 0)
-    for copy in far_x:
-        copy.wait_recv()
-    got_x[7] = wire.send(xs.at[6], xs.at[7], 1, 0)
-    for m in (1, 3, 5, 7):
-        got_w[m].wait_recv()
+    for n in range(1, CUTS):
+        for m in (2, 4, 6):
+            pass_w(n, m)
+    got_g[2].wait_recv()
+    got_g[3] = wire.send(g_all.at[2], g_all.at[3], 1, 0)
+    got_x[2].wait_recv()
+    got_x[3] = wire.send(xs.at[2], xs.at[3], 1, 0)
+    for n in range(CUTS):
+        for m in (1, 3, 5, 7):
+            got_w[m, n].wait_recv()
+    for m in (1, 3, 4):
         got_g[m].wait_recv()
+    for m in (1, 3):
         got_x[m].wait_recv()
     for copy in kept:
         copy.wait()
@@ -541,8 +546,8 @@
             jax.ShapeDtypeStruct((whole, cols), bf16),
             jax.ShapeDtypeStruct((whole, out_proj.shape[1]), bf16),
             jax.ShapeDtypeStruct((whole, mine.shape[1]), bf16),
-            jax.ShapeDtypeStruct((8,) + grad.shape, bf16),
-            jax.ShapeDtypeStruct((8, length, wide), bf16),
+            jax.ShapeDtypeStruct((5,) + grad.shape, bf16),
+            jax.ShapeDtypeStruct((4, length, wide), bf16),
         ],
         in_specs=[vmem] * 6 + [any_spec] * 6,
         out_specs=[vmem] * 8 + [any_spec] * 5,
@@ -567,7 +572,7 @@
     )
 
 
-ORDER = (7, 6, 3, 2, 5, 4, 1, 0)
+ORDER = (3, 2, 4, 5, 7, 6, 1, 0)
 GROUP_AT = {2: (2, 0), 4: (0, 2), 6: (2, 2)}
 
 
@@ -579,8 +584,8 @@
 
 
 def group_kernel(
-    v_ref, g_ref, xs, g_all, w_ref, xn, attn,
-    mix_sum, dx_own, dx_in, grads, xq, aq,
+    v_ref, g_ref, xs, g_all, w_ref, xn,
+    mix_sum, dx_own, dx_in, grads, xq, x_late, g_late,
     wbuf, xbuf, gbuf, xt, gt_, hidg, dgu, deven, dodd, rc, meven, modd, mrc, acc, stage,
     sem_w, sem_x, sem_g, sem_m, sem_s, send_sem, recv_sem,
 ):
@@ -588,7 +593,8 @@
     r, f = wire.r, wire.f
     length, width = g_ref.shape
     hidden = w_ref.shape[1] // 3
-    cols_a = aq.shape[2]
+    half = length // 2
+    low, top = pl.ds(0, half), pl.ds(half, half)
     expert = 2 * r + lax.rem(f // 2, 2)
     step_cols = 256
 
@@ -604,36 +610,64 @@
             pltpu.make_async_copy(v_ref, xbuf.at[slot], sem_x.at[slot]).start()
             pltpu.make_async_copy(g_ref, gbuf.at[slot], sem_g.at[slot]).start()
 
-        @pl.when(k > 0)
-        def _():
-            pltpu.make_async_copy(xs.at[k], xbuf.at[slot], sem_x.at[slot]).start()
-            pltpu.make_async_copy(g_all.at[k], gbuf.at[slot], sem_g.at[slot]).start()
+        for table, src_x, src_g in (
+            ((1, 2, 3), xs, g_all), ((4,), x_late, g_all), ((5, 6, 7), x_late, g_late)
+        ):
+
+            @pl.when((k >= table[0]) & (k <= table[-1]))
+            def _():
+                pltpu.make_async_copy(src_x.at[k], xbuf.at[slot], sem_x.at[slot]).start()
+                pltpu.make_async_copy(src_g.at[k], gbuf.at[slot], sem_g.at[slot]).start()
 
     load(jnp.int32(0))
     wire.meet(PARTNERS_GROUP)
-    act = {}
-    for k in (2, 3, 1):
-        to_a = flips(r, k) * cols_a
-        act["a", k] = wire.send(
-            attn.at[:, pl.ds(pl.multiple_of(to_a, cols_a), cols_a)], aq.at[k], k, 0
-        )
-    act["x", 2] = wire.send(xn, xq.at[2], 2, 0)
-    act["x", 1] = wire.send(xn, xq.at[1], 1, 0)
-    act["x", 3] = wire.plan(xq.at[2], xq.at[3], 1, 0)
-    to_core = {k: wire.plan(dodd.at[n % 2], rc.at[n], 1, 0) for n, k in enumerate((6, 2, 4, 0))}
-    mix_core = {k: wire.plan(modd.at[n % 2], mrc.at[n], 1, 0) for n, k in enumerate((6, 2, 4, 0))}
+    late_x = {4: wire.send(v_ref, x_late.at[4], 0, 2)}
+    far = [
+        wire.send(g_all.at[4, low], g_late.at[6, low], 2, 0),
+        wire.send(xs.at[2, top], x_late.at[6, top], 0, 2),
+        wire.send(g_all.at[2, top], g_late.at[6, top], 0, 2),
+    ]
+    late_g = {5: wire.send(g_all.at[4], g_late.at[5], 1, 0)}
+    act = {2: wire.send(xn, xq.at[2], 2, 0), 1: wire.send(xn, xq.at[1], 1, 0)}
+    act[3] = wire.plan(xq.at[2], xq.at[3], 1, 0)
+    far.append(wire.plan(x_late.at[4, low], x_late.at[6, low], 2, 0))
+    late_x[5] = wire.plan(x_late.at[4], x_late.at[5], 1, 0)
+    late_x[7] = wire.plan(x_late.at[6], x_late.at[7], 1, 0)
+    late_g[7] = wire.plan(g_late.at[6], g_late.at[7], 1, 0)
+    slots = {2: 0, 4: 1, 6: 2, 0: 3}
+    to_core = {k: wire.plan(dodd.at[n % 2], rc.at[n], 1, 0) for k, n in slots.items()}
+    mix_core = {k: wire.plan(modd.at[n % 2], mrc.at[n], 1, 0) for k, n in slots.items()}
     back = {k: wire.plan(deven.at[k // 2], dx_in.at[k // 2 - 1], *GROUP_AT[k]) for k in (2, 4, 6)}
     acc[...] = jnp.zeros_like(acc)
     lane = lax.broadcasted_iota(jnp.int32, (length, EXTRA), 1)
     load_w.wait()
 
-    def keep_mix(n, k):
-        return pltpu.make_async_copy(meven.at[n % 2], mix_sum.at[k // 2], sem_m.at[n % 2])
+    def keep_mix(k):
+        n = slots[k] % 2
+        return pltpu.make_async_copy(meven.at[n], mix_sum.at[k // 2], sem_m.at[n])
+
+    def send_core(k):
+        to_core[k].start()
+        mix_core[k].start()
+
+    def sent_core(k):
+        to_core[k].wait_send()
+        mix_core[k].wait_send()
+
+    def complete(k):
+        n = slots[k]
+        to_core[k].wait_recv()
+        deven[k // 2] = (deven[k // 2].astype(f32) + rc[n].astype(f32)).astype(bf16)
+        if k in (4, 6):
+            back[k].start()
+        mix_core[k].wait_recv()
+        meven[n % 2] = (meven[n % 2].astype(f32) + mrc[n].astype(f32)).astype(bf16)
+        keep_mix(k).start()
 
     def block(step, carry):
         slot = lax.rem(step, 2)
 
-        @pl.when(step < 7)
+        @pl.when((step == 0) | (step >= 4) & (step < 7))
         def _():
             load(step + 1)
 
@@ -685,54 +719,61 @@
             lax.fori_loop(0, width // step_cols, second, 0)
             dst_d[n_d, :, width:] = tail
 
-        pair = step // 2
-
-        @pl.when(slot == 0)
+        slot_two = pick(step, (0, 0, 1, 1, 0, 0, 1, 1))
+        k = pick(step, ORDER)
+
+        @pl.when(step == 4)
         def _():
-            for n, k in enumerate((6, 2, 4, 0)):
-                if n >= 2:
-
-                    @pl.when(pair == n)
-                    def _():
-                        to_core[(6, 2, 4, 0)[n - 2]].wait_send()
-                        mix_core[(6, 2, 4, 0)[n - 2]].wait_send()
-
-            out_parts(dodd, lax.rem(pair, 2), modd, lax.rem(pair, 2))
-            for n, k in enumerate((6, 2, 4, 0)):
-
-                @pl.when(pair == n)
-                def _():
-                    to_core[k].start()
-                    mix_core[k].start()
-                    if n == 2:
-                        act["x", 2].wait_recv()
-                        act["x", 3].start()
-
-        @pl.when(slot == 1)
+            sent_core(2)
+
+        @pl.when(step == 6)
         def _():
-            for n, k in enumerate((6, 2, 4, 0)):
-                if n >= 2:
-
-                    @pl.when(pair == n)
-                    def _():
-                        keep_mix(n - 2, (6, 2, 4, 0)[n - 2]).wait()
-
-            out_parts(deven, pick(pair, (3, 1, 2, 0)), meven, lax.rem(pair, 2))
-            for n, k in enumerate((6, 2, 4, 0)):
-
-                @pl.when(pair == n)
-                def _():
-                    to_core[k].wait_recv()
-                    deven[k // 2] = (
-                        deven[k // 2].astype(f32) + rc[n].astype(f32)
-                    ).astype(bf16)
-                    if k:
-                        back[k].start()
-                    mix_core[k].wait_recv()
-                    meven[n % 2] = (
-                        meven[n % 2].astype(f32) + mrc[n].astype(f32)
-                    ).astype(bf16)
-                    keep_mix(n, k).start()
+            sent_core(4)
+
+        @pl.when(step == 5)
+        def _():
+            keep_mix(2).wait()
+
+        @pl.when(step == 7)
+        def _():
+            keep_mix(4).wait()
+
+        @pl.when(lax.rem(k, 2) == 1)
+        def _():
+            out_parts(dodd, slot_two, modd, slot_two)
+
+        @pl.when(lax.rem(k, 2) == 0)
+        def _():
+            out_parts(deven, k // 2, meven, slot_two)
+
+        def come_5():
+            late_x[5].wait_recv()
+            late_g[5].wait_recv()
+            load(step + 1)
+
+        def come_6():
+            for copy in far:
+                copy.wait_recv()
+            late_x[7].start()
+            late_g[7].start()
+            act[2].wait_recv()
+            act[3].start()
+
+        for at_step, todo in (
+            (0, (lambda: send_core(2),)),
+            (1, (lambda: complete(2),)),
+            (2, (come_5,)),
+            (3, (lambda: send_core(4), come_6)),
+            (4, (lambda: complete(4), lambda: send_core(6))),
+            (5, (lambda: complete(6),)),
+            (6, (lambda: send_core(0),)),
+            (7, (lambda: complete(0),)),
+        ):
+
+            @pl.when(step == at_step)
+            def _():
+                for do in todo:
+                    do()
 
         def third(c, carry):
             at = pl.multiple_of(c * step_cols, step_cols)
@@ -749,6 +790,21 @@
             return carry
 
         lax.fori_loop(0, hidden // step_cols, fourth, 0)
+
+        @pl.when(step == 1)
+        def _():
+            late_x[4].wait_recv()
+            late_x[5].start()
+            far[3].start()
+            back[2].start()
+            load(step + 1)
+
+        @pl.when(step == 3)
+        def _():
+            late_x[7].wait_recv()
+            late_g[7].wait_recv()
+            load(step + 1)
+
         return carry
 
     lax.fori_loop(0, 8, block, 0)
@@ -771,27 +827,25 @@
     for j in range(parts - 2, parts):
         out(j, j % 2).wait()
     keep.wait()
-    keep_mix(2, 4).wait()
-    keep_mix(3, 0).wait()
+    keep_mix(6).wait()
+    keep_mix(0).wait()
     for k in (2, 4, 6):
         back[k].wait_recv()
         back[k].wait_send()
-    for k in (4, 0):
-        to_core[k].wait_send()
-        mix_core[k].wait_send()
-    act["x", 1].wait_recv()
-    act["x", 3].wait_recv()
-    act["x", 3].wait_send()
-    for k in (1, 2, 3):
-        act["a", k].wait_recv()
+    sent_core(6)
+    sent_core(0)
+    act[1].wait_recv()
+    act[3].wait_recv()
+    for copy in (act[3], far[3], late_x[5], late_x[7], late_g[7]):
+        copy.wait_send()
     wire.finish()
 
 
-PARTNERS_GROUP = ((1, 0), (2, 0), (3, 0), (0, 2), (2, 2))
-GROUP_SENDS = 6 + 8 + 3
-
-
-def run_group(v, grad, xs, g_all, w, xn, attn):
+PARTNERS_GROUP = ((1, 0), (2, 0), (0, 2), (2, 2))
+GROUP_SENDS = 12 + 8 + 3
+
+
+def run_group(v, grad, xs, g_all, w, xn):
     length, width = grad.shape
     wide = v.shape[1]
     cols = w.shape[1]
@@ -805,10 +859,11 @@
             jax.ShapeDtypeStruct((3, length, wide), bf16),
             jax.ShapeDtypeStruct((width, cols), bf16),
             jax.ShapeDtypeStruct((4, length, width), bf16),
-            jax.ShapeDtypeStruct((4, length, attn.shape[1] // 4), bf16),
+            jax.ShapeDtypeStruct((8, length, wide), bf16),
+            jax.ShapeDtypeStruct((8, length, width), bf16),
         ],
-        in_specs=[any_spec] * 7,
-        out_specs=[any_spec] * 6,
+        in_specs=[any_spec] * 6,
+        out_specs=[any_spec] * 7,
         scratch_shapes=[
             pltpu.VMEM((width, cols), bf16),
             pltpu.VMEM((2, length, wide), bf16),
@@ -842,20 +897,21 @@
             transcendentals=8 * length * hidden,
         ),
         name="group",
-    )(v, grad, xs, g_all, w, xn, attn)
-
-
-PARTNERS_BACK = ((1, 0), (2, 0), (3, 0), (0, 1), (0, 2), (0, 4), (0, 6), (2, 2))
-BACK_SENDS = 4 + 3 + 3 + 3 + 2 * 4 + 3 + 2 * 3 + 6 + 3 + 5
+    )(v, grad, xs, g_all, w, xn)
+
+
+PARTNERS_BACK = ((1, 0), (2, 0), (3, 0), (0, 1), (0, 2), (0, 4), (0, 6))
+TERMS = 16
+BACK_SENDS = 4 + 3 + 3 + 2 + 3 + 2 * 4 + 2 * 3 + 1 + 6 + 3
 
 
 def back_kernel(
     dx_own, g_ref, first, table, tiny, v, tokens, qkv, lse, cos, sin, seg_col, seg_row,
-    dx_in, grads, mix_sum, attn, xq, aq, xn, in_all, out_all,
-    tokens_grad, terms_out,
+    dx_in, grads, mix_sum, attn, xq, xn, in_all, out_all,
+    tokens_grad,
     g_out, mix_in, d_out,
-    in_v, out_v, din_v, gl, gy, gz, act_v, aq_v, pq, wo, wi, wyo, wyi, wzo, wzi, own_d,
-    dn, dxn, dl, dattn, dproj, dkv, bias, tbuf, tr,
+    in_v, out_v, mix_v, gl, gy, gz, act_v, aq_v, pq, wo, wi, wyo, wyi, wzo, wzi, wxo, own_d,
+    dn, dxn, dl, dattn, dproj, dkv, bias, tbuf,
     local_sem, send_sem, recv_sem,
 ):
     wire = Wire(send_sem, recv_sem)
@@ -886,29 +942,40 @@
     def add(u, w):
         return (u.astype(f32) + w.astype(f32)).astype(bf16)
 
-    load_dx = local(dx_in, din_v)
+    half = lax.rem(r, 2)
+    side = r // 2
+
+    def half_of(index):
+        return pl.ds(pl.multiple_of(index * cols_a, cols_a), cols_a)
+
+    load_dx = [
+        local(dx_in.at[n], in_v.at[token_rows(n), pl.ds(0, dx_in.shape[2])]) for n in range(3)
+    ]
     load_out = local(out_all, out_v)
-    load_g = {j: local(grads.at[shard_rows(j)], gl.at[j // 2]) for j in (2, 6, 4, 0)}
-    load_in = local(in_all, in_v)
-    load_a = [local(attn.at[:, part_of(0, cols_a)], aq_v.at[token_rows(0)])]
-    load_a += [local(aq.at[k], aq_v.at[token_rows(k)]) for k in (1, 2, 3)]
+    load_g = {j: local(grads.at[shard_rows(j)], gl.at[j // 2]) for j in (4, 0, 2, 6)}
+    load_a = local(attn.at[:, half_of(half)], aq_v.at[token_rows(0)])
+    load_mix = local(mix_sum.at[2], mix_v.at[0])
     wire.meet(PARTNERS_BACK)
     got_y, got_m = {}, {}
-    for j in (2, 6, 4, 0):
+    for j in (4, 0, 2, 6):
         got_y[j] = wire.send(grads.at[shard_rows(j + 1)], gy.at[j // 2], 0, 1)
-    got_m[4] = wire.send(mix_sum.at[2], mix_in.at[1], 0, 2)
+    got_a = wire.send(attn.at[:, half_of(1 - half)], aq_v.at[token_rows(1)], 1, 0)
+    got_m[2] = wire.send(mix_sum.at[1], mix_in.at[0], 2, 0)
+    got_m[6] = wire.send(mix_sum.at[3], mix_v.at[1], 2, 0)
 
     spot = lax.broadcasted_iota(jnp.int32, bias.shape, 0)
     keys_at = lax.broadcasted_iota(jnp.int32, bias.shape, 1)
     bias[...] = jnp.where((spot >= keys_at) & (seg_col[...] == seg_row[...]), 0.0, -1e30)
-    tbuf[0] = jnp.zeros_like(tbuf[0])
-    load_dx.wait()
+    tbuf[...] = jnp.zeros_like(tbuf)
+    for copy in load_dx:
+        copy.wait()
 
     def sum_dx(c, carry):
         at = pl.ds(pl.multiple_of(c * ROWS, ROWS), ROWS)
         d = dx_own[at, :].astype(f32)
         for n in range(3):
-            d = d + din_v[n, at, :].astype(f32)
+            here = pl.ds(pl.multiple_of(n * length + c * ROWS, ROWS), ROWS)
+            d = d + in_v[here, 0 : dx_own.shape[1]].astype(f32)
         dn[at, :] = d[:, :width]
         dgate = d[:, width:]
         dgate = dgate + pltpu.roll(dgate, EXTRA - experts, 1)
@@ -918,6 +985,7 @@
         return carry
 
     lax.fori_loop(0, length // ROWS, sum_dx, 0)
+    load_in = local(in_all, in_v)
     dlt = dl[...].T[0:16]
 
     def add_router(c, carry):
@@ -925,7 +993,7 @@
         row = lax.broadcasted_iota(jnp.int32, (16, 256), 0)
         router = jnp.where(row < experts, tiny[:, at], 0.0).astype(bf16)
         dn[:, at] = dn[:, at] + matmul(dl[:, 0:16], router)
-        tbuf[0, :, at] = matmul(dlt, v[:, at])
+        tbuf[:, at] = matmul(dlt, v[:, at])
         return carry
 
     lax.fori_loop(0, width // 256, add_router, 0)
@@ -946,10 +1014,8 @@
         return gain
 
     gain_two = lax.fori_loop(0, length // ROWS, norm_two, jnp.zeros((1, width), f32))
-    tbuf[0, experts + 1 : experts + 2, :] = gain_two
-    got_r = {}
-    got_r[2] = wire.send(act_v.at[token_rows(0)], act_v.at[token_rows(2)], 2, 0)
-    got_r[1] = wire.send(act_v.at[token_rows(0)], act_v.at[token_rows(1)], 1, 0)
+    tbuf[experts + 1 : experts + 2, :] = gain_two
+    got_r = wire.send(act_v.at[token_rows(0)], act_v.at[token_rows(1)], 1, 0)
     load_out.wait()
 
     def to_attn(c, carry):
@@ -971,6 +1037,7 @@
         gl[j // 2] = add(gl[j // 2], gy[j // 2])
         got_z[j] = wire.send(gl.at[j // 2], gz.at[j // 2 - 1], 0, j)
 
+    pass_y(4)
     for group in range(KV):
         k_at = pl.ds(WQ + group * HD, HD)
         v_at = pl.ds(WQ + WK + group * HD, HD)
@@ -994,52 +1061,28 @@
         lax.fori_loop(0, GROUP, head, 0)
         dproj[:, k_at] = turn_back(dkv[0] * scale).astype(bf16)
         dproj[:, v_at] = dkv[1].astype(bf16)
-        if group == 0:
-            got_r[2].wait_recv()
-            got_r[3] = wire.send(act_v.at[token_rows(2)], act_v.at[token_rows(3)], 1, 0)
 
     keep_p = local(dproj.at[:, part_of(0, cols_p)], pq.at[token_rows(0)])
     got_p = {}
     for k in (2, 3, 1):
         got_p[k] = wire.send(dproj.at[:, part_of(k, cols_p)], pq.at[token_rows(k)], k, 0)
-    got_m[2] = wire.send(mix_sum.at[1], mix_in.at[0], 2, 0)
-    got_m[6] = wire.send(mix_sum.at[3], mix_in.at[2], 2, 2)
-
-    for copy in load_a:
-        copy.wait()
-    got_r[1].wait_recv()
-    got_r[3].wait_recv()
+
+    load_a.wait()
+    got_a.wait_recv()
+    got_r.wait_recv()
 
     def dense_out(c, carry):
         at = pl.ds(pl.multiple_of(c * 256, 256), 256)
-        wo[at, :] = matmul(act_v[:, at].T, aq_v[...]).astype(bf16)
+        wo[at, :] = matmul(act_v[0 : 2 * length, at].T, aq_v[...]).astype(bf16)
         return carry
 
     lax.fori_loop(0, width // 256, dense_out, 0)
-    for copy in (got_r[2], got_r[1], got_r[3]):
-        copy.wait_send()
+    got_r.wait_send()
     load_x = [local(xn, act_v.at[token_rows(0)])]
     load_x += [local(xq.at[k], act_v.at[token_rows(k)]) for k in (1, 2, 3)]
     got_wo, got_wi, got_wzo, got_wzi = {}, {}, {}, {}
     for j in (2, 6, 4, 0):
         got_wo[j] = wire.send(wo.at[shard_rows(j + 1)], wyo.at[j // 2], 0, 1)
-    pass_y(2)
-
-    keep_p.wait()
-    for copy in load_x:
-        copy.wait()
-    for k in (1, 2, 3):
-        got_p[k].wait_recv()
-
-    def dense_in(c, carry):
-        at = pl.ds(pl.multiple_of(c * 256, 256), 256)
-        wi[at, :] = matmul(act_v[:, at].T, pq[...]).astype(bf16)
-        return carry
-
-    lax.fori_loop(0, width // 256, dense_in, 0)
-    for j in (2, 6, 4, 0):
-        got_wi[j] = wire.send(wi.at[shard_rows(j + 1)], wyi.at[j // 2], 0, 1)
-    pass_y(6)
 
     load_in.wait()
 
@@ -1063,13 +1106,45 @@
         return gain
 
     gain_one = lax.fori_loop(0, length // ROWS, norm_one, jnp.zeros((1, width), f32))
-    tbuf[0, experts : experts + 1, :] = gain_one
-    pass_y(4)
-    for n, d in enumerate(((1, 0), (0, 1), (2, 0), (0, 2), (0, 4))):
-        copy = wire.send(tbuf.at[n], tr.at[n], *d)
-        copy.wait_recv()
-        tbuf[n + 1] = tbuf[n] + tr[n]
-    terms_out[...] = tbuf[5]
+    tbuf[experts : experts + 1, :] = gain_one
+    load_mix.wait()
+    got_m[6].wait_recv()
+    mix_v[0] = add(mix_v[0], mix_v[1])
+    got_m[4] = wire.send(mix_v.at[0], mix_in.at[1], 0, 2)
+    pass_y(2)
+
+    mine, other = 2 * r + low, 2 * r + 1 - low
+    load_g[0].wait()
+    got_y[0].wait_recv()
+    got_z[4].wait_recv()
+    gl[0] = (gl[0].astype(f32) + gy[0].astype(f32) + gz[1].astype(f32)).astype(bf16)
+    kept = [local(gl.at[0], g_out.at[mine])]
+    got_e = {}
+
+    keep_p.wait()
+    for copy in load_x:
+        copy.wait()
+    for k in (1, 2, 3):
+        got_p[k].wait_recv()
+    got_e[2, 0] = wire.send(gl.at[0], g_out.at[mine], 2, 0)
+    got_e[1, 0] = wire.send(gl.at[0], g_out.at[mine], 1, 0)
+
+    tall = shard + TERMS
+
+    def tall_rows(j):
+        return pl.ds(pl.multiple_of(flips(f, j) * tall, TERMS), tall)
+
+    for z in range(4):
+        lanes = slice(2 * z * shard, 2 * (z + 1) * shard)
+        both = matmul(act_v[:, lanes].T, pq[...]).astype(bf16)
+        for y in (0, 1):
+            top = (2 * z + y) * tall
+            wi[top : top + shard, :] = both[y * shard : (y + 1) * shard]
+            wi[top + shard : top + tall, :] = jnp.zeros((TERMS, cols_p), bf16)
+            wi[top + shard : top + tall, 0 : 2 * shard] = tbuf[:, lanes].astype(bf16)
+    for j in (2, 6, 4, 0):
+        got_wi[j] = wire.send(wi.at[tall_rows(j + 1)], wyi.at[j // 2], 0, 1)
+    pass_y(6)
 
     for j in (2, 6, 4):
         got_wo[j].wait_recv()
@@ -1077,19 +1152,9 @@
         got_wzo[j] = wire.send(wyo.at[j // 2], wzo.at[j // 2 - 1], 0, j)
     for j in (2, 6, 4):
         got_wi[j].wait_recv()
-        wyi[j // 2] = add(wi[shard_rows(j), :], wyi[j // 2])
+        wyi[j // 2] = add(wi[tall_rows(j), :], wyi[j // 2])
         got_wzi[j] = wire.send(wyi.at[j // 2], wzi.at[j // 2 - 1], 0, j)
 
-    mine, other = 2 * r + low, 2 * r + 1 - low
-    load_g[0].wait()
-    got_y[0].wait_recv()
-    got_z[4].wait_recv()
-    got_z[2].wait_send()
-    gl[0] = (gl[0].astype(f32) + gy[0].astype(f32) + gz[1].astype(f32)).astype(bf16)
-    kept = [local(gl.at[0], g_out.at[mine])]
-    got_e = {}
-    got_e[2, 0] = wire.send(gl.at[0], g_out.at[mine], 2, 0)
-    got_e[1, 0] = wire.send(gl.at[0], g_out.at[mine], 1, 0)
     got_z[2].wait_recv()
     got_z[6].wait_recv()
     gz[0] = add(gz[0], gz[2])
@@ -1097,16 +1162,27 @@
     got_e[2, 1] = wire.send(gz.at[0], g_out.at[other], 2, 0)
     got_e[1, 1] = wire.send(gz.at[0], g_out.at[other], 1, 0)
 
-    def own_rows(w, y, z, got_w, got_zs, cols):
+    def own_rows(w, rows, y, z, got_w, got_zs):
         got_w[0].wait_recv()
-        total = w[shard_rows(0), :].astype(f32) + y[0].astype(f32)
+        total = w[rows, :].astype(f32) + y[0].astype(f32)
         for j in (2, 4, 6):
             got_zs[j].wait_recv()
             total = total + z[j // 2 - 1].astype(f32)
-        own_d[:, cols] = total.astype(bf16)
-
-    own_rows(wo, wyo, wzo, got_wo, got_wzo, pl.ds(cols_p, cols_a))
-    own_rows(wi, wyi, wzi, got_wi, got_wzi, pl.ds(0, cols_p))
+        return total
+
+    wxo[0] = own_rows(wo, shard_rows(0), wyo, wzo, got_wo, got_wzo).astype(bf16)
+    quarter = cols_a // 2
+
+    def quarter_of(index):
+        return pl.ds(pl.multiple_of(index * quarter, quarter), quarter)
+
+    got_x = wire.send(
+        wxo.at[0, :, quarter_of(1 - side)], wxo.at[1, :, pl.ds(0, quarter)], 2, 0
+    )
+    own_d[:, 0:cols_p] = own_rows(wi, tall_rows(0), wyi, wzi, got_wi, got_wzi).astype(bf16)
+    got_x.wait_recv()
+    own_d[shard:, cols_p:] = jnp.zeros((TERMS, quarter), bf16)
+    own_d[0:shard, cols_p:] = add(wxo[0, :, quarter_of(side)], wxo[1, :, 0:quarter])
     kept.append(local(own_d, d_out.at[r]))
     got_d = [wire.send(own_d, d_out.at[r], k, 0) for k in (2, 3, 1)]
 
@@ -1119,51 +1195,51 @@
             got_e[k, n].wait_recv()
     for copy in got_d:
         copy.wait_recv()
-    for k in (2, 4, 6):
+    for k in (2, 4):
         got_m[k].wait_recv()
     for copy in kept:
         copy.wait()
-    wire.finish((got_r[2], got_r[1], got_r[3], got_z[2]))
+    wire.finish((got_r,))
 
 
 def run_back(
     dx_own, grad, first, table, tiny, v, tokens, qkv, lse, cos, sin, seg_ids,
-    dx_in, grads, mix_sum, attn, xq, aq, xn, in_all, out_all,
+    dx_in, grads, mix_sum, attn, xq, xn, in_all, out_all,
 ):
     any_spec = pl.BlockSpec(memory_space=pl.ANY)
     vmem = pl.BlockSpec(memory_space=pltpu.VMEM)
     length, width = tokens.shape
     shard = width // 8
     cols = grads.shape[1]
-    cols_p, cols_a = qkv.shape[1] // 4, attn.shape[1] // 4
+    cols_p, cols_a = qkv.shape[1] // 4, attn.shape[1] // 2
     return pl.pallas_call(
         back_kernel,
         out_shape=[
             jax.ShapeDtypeStruct((length, width), bf16),
-            jax.ShapeDtypeStruct((16, width), f32),
             jax.ShapeDtypeStruct((8, shard, cols), bf16),
-            jax.ShapeDtypeStruct((3, length, width), bf16),
-            jax.ShapeDtypeStruct((4, shard, cols_p + cols_a), bf16),
+            jax.ShapeDtypeStruct((2, length, width), bf16),
+            jax.ShapeDtypeStruct((4, shard + TERMS, cols_p + cols_a // 2), bf16),
         ],
-        in_specs=[vmem] * 13 + [any_spec] * 9,
-        out_specs=[vmem] * 2 + [any_spec] * 3,
+        in_specs=[vmem] * 13 + [any_spec] * 8,
+        out_specs=[vmem] + [any_spec] * 3,
         scratch_shapes=[
             pltpu.VMEM(in_all.shape, bf16),
             pltpu.VMEM(out_all.shape, bf16),
-            pltpu.VMEM(dx_in.shape, bf16),
+            pltpu.VMEM((2, length, width), bf16),
             pltpu.VMEM((4, shard, cols), bf16),
             pltpu.VMEM((4, shard, cols), bf16),
             pltpu.VMEM((3, shard, cols), bf16),
             pltpu.VMEM((4 * length, width), bf16),
-            pltpu.VMEM((4 * length, cols_a), bf16),
+            pltpu.VMEM((2 * length, cols_a), bf16),
             pltpu.VMEM((4 * length, cols_p), bf16),
             pltpu.VMEM((width, cols_a), bf16),
-            pltpu.VMEM((width, cols_p), bf16),
+            pltpu.VMEM((width + 8 * TERMS, cols_p), bf16),
             pltpu.VMEM((4, shard, cols_a), bf16),
-            pltpu.VMEM((4, shard, cols_p), bf16),
+            pltpu.VMEM((4, shard + TERMS, cols_p), bf16),
             pltpu.VMEM((3, shard, cols_a), bf16),
-            pltpu.VMEM((3, shard, cols_p), bf16),
-            pltpu.VMEM((shard, cols_p + cols_a), bf16),
+            pltpu.VMEM((3, shard + TERMS, cols_p), bf16),
+            pltpu.VMEM((2, shard, cols_a), bf16),
+            pltpu.VMEM((shard + TERMS, cols_p + cols_a // 2), bf16),
             pltpu.VMEM((length, width), f32),
             pltpu.VMEM((length, width), f32),
             pltpu.VMEM((length, EXTRA), bf16),
@@ -1171,8 +1247,7 @@
             pltpu.VMEM(qkv.shape, bf16),
             pltpu.VMEM((2, length, HD), f32),
             pltpu.VMEM((length, length), f32),
-            pltpu.VMEM((6, 16, width), f32),
-            pltpu.VMEM((5, 16, width), f32),
+            pltpu.VMEM((TERMS, width), f32),
             pltpu.SemaphoreType.DMA((20,)),
             pltpu.SemaphoreType.DMA((BACK_SENDS,)),
             pltpu.SemaphoreType.DMA((BACK_SENDS,)),
@@ -1184,7 +1259,7 @@
     )(
         dx_own, grad, first, table, tiny, v, tokens, qkv, lse, cos, sin,
         seg_ids.reshape(length, 1), seg_ids,
-        dx_in, grads, mix_sum, attn, xq, aq, xn, in_all, out_all,
+        dx_in, grads, mix_sum, attn, xq, xn, in_all, out_all,
     )
 
 
@@ -1223,19 +1298,20 @@
     qkv, attn, xn, first, lse, table, small, v, in_all, out_all, w_all, g_all, xs = front(
         tokens, seg_ids, routes, cos, sin, in_proj, out_proj, tiny, mine, other, out_grad
     )
-    mix_sum, dx_own, dx_in, grads, xq, aq = run_group(v, out_grad, xs, g_all, w_all, xn, attn)
-    tokens_grad, terms, expert_sum, mix_in, dense = run_back(
+    mix_sum, dx_own, dx_in, grads, xq, _, _ = run_group(v, out_grad, xs, g_all, w_all, xn)
+    tokens_grad, expert_sum, mix_in, dense = run_back(
         dx_own, out_grad, first, table, small, v, tokens, qkv, lse, cos, sin, seg_ids,
-        dx_in, grads, mix_sum, attn, xq, aq, xn, in_all, out_all,
+        dx_in, grads, mix_sum, attn, xq, xn, in_all, out_all,
     )
     mixed = first + mix_sum[0].astype(f32)
-    for k in range(3):
+    for k in range(2):
         mixed = mixed + mix_in[k].astype(f32)
     cut = in_proj.shape[1] // 4
-    in_grad = dense[:, :, :cut].transpose(1, 0, 2).reshape(shard, -1)
-    out_proj_grad = dense[:, :, cut:].transpose(1, 0, 2).reshape(shard, -1)
+    in_grad = dense[:, :shard, :cut].transpose(1, 0, 2).reshape(shard, -1)
+    out_proj_grad = jnp.concatenate([dense[k, :shard, cut:] for k in (0, 2, 1, 3)], axis=1)
     expert_sum = expert_sum.transpose(1, 0, 2)
-    terms = lax.dynamic_slice_in_dim(terms, f * shard, shard, 1).T
+    terms = jnp.sum(dense[:, shard:, :cut].astype(f32), axis=0)
+    terms = jnp.where(f % 2 == 0, terms[:, :shard], terms[:, shard : 2 * shard]).T
     return (
         mixed.astype(bf16),
         tokens_grad,

time: 582 us -> 502 us (0.86)
  Pallas kernels: 537 us -> 456 us
    pallas_call x1, Pallas kernels: 190 us -> 132 us  [front(): pl.pallas_call(front_kernel, out_shape=[jax.ShapeDtypeStruct((length, col...]
    pallas_call x1, Pallas kernels: 226 us -> 185 us  [run_back(): pl.pallas_call(back_kernel, out_shape=[jax.ShapeDtypeStruct((length, widt...]
    pallas_call x1, Pallas kernels: 122 us -> 139 us  [run_group(): pl.pallas_call(group_kernel, out_shape=[jax.ShapeDtypeStruct((4, length,...]
where the time goes in v4:
time: 502 us; the launch traced here: 498 us
  Pallas kernels  456 us (91%)
  local copies, waits for them, and re-layouts  27.9 us (6%)
  other arithmetic  12.7 us (3%)
    pallas_call x1, Pallas kernels, run_back(): pl.pallas_call(back_kernel, out_shape=[jax.ShapeDtypeStruct((length, widt...  185 us
    pallas_call x1, Pallas kernels, run_group(): pl.pallas_call(group_kernel, out_shape=[jax.ShapeDtypeStruct((4, length,...  139 us
    pallas_call x1, Pallas kernels, front(): pl.pallas_call(front_kernel, out_shape=[jax.ShapeDtypeStruct((length, col...  132 us
    unnamed x14, local copies, waits for them, and re-layouts  16.9 us

profile of v4, /device:TPU:1, one launch (start us, length us, event | category | flops | bytes accessed | tf_op | source)
XLA Modules:
  0.0 497.8 jit_solution(5409102900068441488)
XLA Ops:
  0.7 0.1 pad.12.clone
  0.7 0.8 maximum_maximum_fusion
  1.5 0.7 pad_select_fusion.tiny_ref
  2.2 1.5 copy.25.seg_col
  3.7 1.5 copy.26.routes
  5.2 0.7 fusion.3
  6.0 0.0 copy-start.1
  6.0 0.9 pad_maximum_fusion.2
  6.9 4.2 constant_dynamic-slice_fusion
  11.1 0.1 copy_bitcast_fusion.2
  11.2 0.0 copy-done.1
  11.2 2.4 constant_dynamic-slice_fusion.1
  13.6 0.2 copy_bitcast_fusion
  13.8 1.0 pad_maximum_fusion.1.other_ref
  14.7 1.0 pad_maximum_fusion.mine_ref
  15.7 132.0 %front.1 = (bf16[384,2048]{1,0:T(8,128)(2,1)}, bf16[384,1536]{1,0:T(8,128)(2,1)}, bf16[384,1536]{1,0:T(8,128)(2,1)}, f32[384,1536]{1,0:T(8,128)}, f32[384,128]{1...) custom-call(bf16[384,1536]{1,0:T(8,128)(2,1)} %tokens.3, ...), custom_call_target="tpu_custom_call" | custom-call | tf_op jit(solution)/shard_map/front/pallas_call | solution.py:535
  147.7 138.5 %group.1 = (bf16[4,384,1536]{2,1,0:T(8,128)(2,1)}, bf16[384,1664]{1,0:T(8,128)(2,1)}, bf16[3,384,1664]{2,1,0:T(8,128)(2,1)}, bf16[1536,2304]{1,0:T(8,128)(2,1)},...) custom-call(bf16[384,1664]{1,0:T(8,128)(2,1)} %get-tuple-element.31.v_ref.v, ...), custom_call_target="tpu_custom_call" | custom-call | flops 65229815808 | bytes 51904512 | tf_op jit(solution)/shard_map/group/pallas_call | solution.py:854
  286.2 185.4 %back.1 = (bf16[384,1536]{1,0:T(8,128)(2,1)}, bf16[8,192,2304]{2,1,0:T(8,128)(2,1)}, bf16[2,384,1536]{2,1,0:T(8,128)(2,1)}, bf16[4,208,896]{2,1,0:T(8,128)(2,1)}) custom-call(bf16[384,1664]{1,0:T(8,128)(2,1)} %get-tuple-element.37.dx_own, bf16[384,1536]{1,0:T(8,128)(2,1)} %g_ref.5, f32[384,1536]{1,0:T(8,128)} %get-tuple-element.30.first, ...), custom_call_target="tpu_custom_call" | custom-call | tf_op jit(solution)/shard_map/back/pallas_call | solution.py:1215
  471.7 0.0 slice-start
  471.7 4.5 fusion
  476.2 0.1 fusion.4
  476.3 0.6 slice.63
  476.9 0.6 slice.62
  477.5 0.1 slice_bitcast_fusion.3
  477.5 0.2 convert_bitcast_fusion
  477.7 1.3 copy.35
  479.0 1.1 maximum_convert_fusion
  480.2 0.4 slice_convert_fusion.1
  480.6 4.9 copy.30
  485.5 1.3 slice_convert_fusion
  486.9 9.5 %copy.29 = f32[192,8,1536]{2,1,0:T(8,128)} copy(f32[192,8,1536]{2,0,1:T(8,128)S(1)} %slice_convert_fusion) | data formatting | bytes 18874368
  496.3 1.0 copy.41
  (11 shorter events, 0.0 us)
Async XLA Ops:
  6.0 5.2 %copy-start.1 = (bf16[192,8,1536]{2,1,0:T(8,128)(2,1)S(1)}, bf16[192,8,1536]{2,1,0:T(8,128)(2,1)}, u32[]{:S(2)}) copy-start(bf16[192,8,1536]{2,1,0:T(8,128)(2,1)} %param.17) | copy-start | bytes 14155780
  471.7 4.5 copy-start
  471.7 8.5 %slice-start = ((s8[7077888]{0:T(1024)(128)(4,1)}), s8[4194304]{0:T(1024)(128)(4,1)S(1)}, s32[]{:S(2)}) async-start(s8[7077888]{0:T(1024)(128)(4,1)} %bitcast.35), calls=%async_computation | async-start | bytes 8388608
  477.5 2.7 slice-start.1
  486.8 9.5 %copy-start.2 = (bf16[384,1536]{1,0:T(8,128)(2,1)S(1)}, bf16[384,1536]{1,0:T(8,128)(2,1)}, u32[]{:S(2)}) copy-start(bf16[384,1536]{1,0:T(8,128)(2,1)} %get-tuple-element.94) | copy-start | bytes 3538948

commit v5 on v4

--- a/solution.py
+++ b/solution.py
@@ -291,7 +291,7 @@
                 copy.wait_send()
 
 
-CUTS = 2
+CUTS = 4
 FRONT_SENDS = 2 * 28 + 7 + 7 * CUTS + 4 + 3
 PARTNERS = ((1, 0), (2, 0), (0, 1), (0, 2), (0, 4), (0, 6))
 ROWS = 64
@@ -450,6 +450,7 @@
 
     lax.fori_loop(0, 8, project, 0)
     pass_w(0, 2)
+    pass_w(0, 4)
     lane = lax.broadcasted_iota(jnp.int32, (length, HD), 1)
     lse[...] = jnp.zeros_like(lse)
 
@@ -469,9 +470,11 @@
 
     lax.fori_loop(0, HQ // 2, head, 0)
     side_pieces("out")
-    pass_w(0, 4)
+    pass_w(0, 6)
+    pass_w(1, 2)
     lax.fori_loop(HQ // 2, HQ, head, 0)
-    pass_w(0, 6)
+    pass_w(1, 4)
+    pass_w(1, 6)
     own_out.wait()
     all_pieces("out")
     kept.append(local(5, in_v, in_all))
@@ -506,7 +509,7 @@
 
     got_x[2] = wire.send(v, xs.at[2], 2, 0)
     got_x[1] = wire.send(v, xs.at[1], 1, 0)
-    for n in range(1, CUTS):
+    for n in range(2, CUTS):
         for m in (2, 4, 6):
             pass_w(n, m)
     got_g[2].wait_recv()
@@ -573,6 +576,8 @@
 
 
 ORDER = (3, 2, 4, 5, 7, 6, 1, 0)
+UNROLL = True
+WIDE_COLS = 256
 GROUP_AT = {2: (2, 0), 4: (0, 2), 6: (2, 2)}
 
 
@@ -584,8 +589,8 @@
 
 
 def group_kernel(
-    v_ref, g_ref, xs, g_all, w_ref, xn,
-    mix_sum, dx_own, dx_in, grads, xq, x_late, g_late,
+    v_ref, g_ref, xs, g_all, w_ref,
+    mix_sum, dx_own, dx_in, grads, x_late, g_late,
     wbuf, xbuf, gbuf, xt, gt_, hidg, dgu, deven, dodd, rc, meven, modd, mrc, acc, stage,
     sem_w, sem_x, sem_g, sem_m, sem_s, send_sem, recv_sem,
 ):
@@ -623,13 +628,10 @@
     wire.meet(PARTNERS_GROUP)
     late_x = {4: wire.send(v_ref, x_late.at[4], 0, 2)}
     far = [
-        wire.send(g_all.at[4, low], g_late.at[6, low], 2, 0),
+        wire.send(g_all.at[4], g_late.at[6], 2, 0),
         wire.send(xs.at[2, top], x_late.at[6, top], 0, 2),
-        wire.send(g_all.at[2, top], g_late.at[6, top], 0, 2),
     ]
     late_g = {5: wire.send(g_all.at[4], g_late.at[5], 1, 0)}
-    act = {2: wire.send(xn, xq.at[2], 2, 0), 1: wire.send(xn, xq.at[1], 1, 0)}
-    act[3] = wire.plan(xq.at[2], xq.at[3], 1, 0)
     far.append(wire.plan(x_late.at[4, low], x_late.at[6, low], 2, 0))
     late_x[5] = wire.plan(x_late.at[4], x_late.at[5], 1, 0)
     late_x[7] = wire.plan(x_late.at[6], x_late.at[7], 1, 0)
@@ -676,8 +678,9 @@
         extra = xbuf[slot, :, width:].astype(f32)
         mine = (lane == expert) | (lane == expert + 8)
         gate = jnp.sum(jnp.where(mine, extra, 0.0), axis=1, keepdims=True)
-        xt[...] = xbuf[slot, :, :width].T
-        gt_[...] = gbuf[slot].T
+        here = pl.ds(pl.multiple_of(slot * length, length), length)
+        xt[:, here] = xbuf[slot, :, :width].T
+        gt_[:, here] = gbuf[slot].T
 
         def first(c, dgate):
             at = pl.multiple_of(c * step_cols, step_cols)
@@ -687,17 +690,17 @@
             sig = 1.0 / (1.0 + jnp.exp(-u))
             act = u * sig
             hid = act * up
-            hidg[:, pl.ds(at, step_cols)] = (gate * hid).astype(bf16)
+            hidg[here, pl.ds(at, step_cols)] = (gate * hid).astype(bf16)
             dgate = dgate + jnp.sum(rev * hid, axis=1, keepdims=True)
             dhid = gate * rev
-            dgu[:, pl.ds(at, step_cols)] = (
+            dgu[here, pl.ds(at, step_cols)] = (
                 dhid * up * sig * (1.0 + u * (1.0 - sig))
             ).astype(bf16)
-            dgu[:, pl.ds(hidden + at, step_cols)] = (dhid * act).astype(bf16)
+            dgu[here, pl.ds(hidden + at, step_cols)] = (dhid * act).astype(bf16)
             return dgate
 
         dgate = lax.fori_loop(
-            0, hidden // step_cols, first, jnp.zeros((length, 1), f32)
+            0, hidden // step_cols, first, jnp.zeros((length, 1), f32), unroll=UNROLL
         )
         high = dgate.astype(bf16).astype(f32)
         rest = dgate - high
@@ -709,14 +712,14 @@
             def second(c, carry):
                 at = pl.multiple_of(c * step_cols, step_cols)
                 dst_d[n_d, :, pl.ds(at, step_cols)] = contract_cols(
-                    dgu[...], wbuf[pl.ds(at, step_cols), pl.ds(0, 2 * hidden)]
+                    dgu[here, :], wbuf[pl.ds(at, step_cols), pl.ds(0, 2 * hidden)]
                 ).astype(bf16)
                 dst_m[n_m, :, pl.ds(at, step_cols)] = contract_cols(
-                    hidg[...], wbuf[pl.ds(at, step_cols), pl.ds(2 * hidden, hidden)]
+                    hidg[here, :], wbuf[pl.ds(at, step_cols), pl.ds(2 * hidden, hidden)]
                 ).astype(bf16)
                 return carry
 
-            lax.fori_loop(0, width // step_cols, second, 0)
+            lax.fori_loop(0, width // step_cols, second, 0, unroll=UNROLL)
             dst_d[n_d, :, width:] = tail
 
         slot_two = pick(step, (0, 0, 1, 1, 0, 0, 1, 1))
@@ -756,8 +759,6 @@
                 copy.wait_recv()
             late_x[7].start()
             late_g[7].start()
-            act[2].wait_recv()
-            act[3].start()
 
         for at_step, todo in (
             (0, (lambda: send_core(2),)),
@@ -775,27 +776,29 @@
                 for do in todo:
                     do()
 
-        def third(c, carry):
-            at = pl.multiple_of(c * step_cols, step_cols)
-            acc[:, pl.ds(at, step_cols)] += matmul(xt[...], dgu[:, pl.ds(at, step_cols)])
-            return carry
-
-        lax.fori_loop(0, 2 * hidden // step_cols, third, 0)
-
-        def fourth(c, carry):
-            at = pl.multiple_of(c * step_cols, step_cols)
-            acc[:, pl.ds(2 * hidden + at, step_cols)] += matmul(
-                gt_[...], hidg[:, pl.ds(at, step_cols)]
-            )
-            return carry
-
-        lax.fori_loop(0, hidden // step_cols, fourth, 0)
+        @pl.when(slot == 1)
+        def _():
+            def third(c, carry):
+                at = pl.multiple_of(c * WIDE_COLS, WIDE_COLS)
+                acc[:, pl.ds(at, WIDE_COLS)] += matmul(xt[...], dgu[:, pl.ds(at, WIDE_COLS)])
+                return carry
+
+            lax.fori_loop(0, 2 * hidden // WIDE_COLS, third, 0, unroll=UNROLL)
+
+            def fourth(c, carry):
+                at = pl.multiple_of(c * WIDE_COLS, WIDE_COLS)
+                acc[:, pl.ds(2 * hidden + at, WIDE_COLS)] += matmul(
+                    gt_[...], hidg[:, pl.ds(at, WIDE_COLS)]
+                )
+                return carry
+
+            lax.fori_loop(0, hidden // WIDE_COLS, fourth, 0, unroll=UNROLL)
 
         @pl.when(step == 1)
         def _():
             late_x[4].wait_recv()
             late_x[5].start()
-            far[3].start()
+            far[2].start()
             back[2].start()
             load(step + 1)
 
@@ -834,18 +837,16 @@
         back[k].wait_send()
     sent_core(6)
     sent_core(0)
-    act[1].wait_recv()
-    act[3].wait_recv()
-    for copy in (act[3], far[3], late_x[5], late_x[7], late_g[7]):
+    for copy in (far[2], late_x[5], late_x[7], late_g[7]):
         copy.wait_send()
     wire.finish()
 
 
 PARTNERS_GROUP = ((1, 0), (2, 0), (0, 2), (2, 2))
-GROUP_SENDS = 12 + 8 + 3
-
-
-def run_group(v, grad, xs, g_all, w, xn):
+GROUP_SENDS = 8 + 8 + 3
+
+
+def run_group(v, grad, xs, g_all, w):
     length, width = grad.shape
     wide = v.shape[1]
     cols = w.shape[1]
@@ -858,20 +859,19 @@
             jax.ShapeDtypeStruct((length, wide), bf16),
             jax.ShapeDtypeStruct((3, length, wide), bf16),
             jax.ShapeDtypeStruct((width, cols), bf16),
-            jax.ShapeDtypeStruct((4, length, width), bf16),
             jax.ShapeDtypeStruct((8, length, wide), bf16),
             jax.ShapeDtypeStruct((8, length, width), bf16),
         ],
-        in_specs=[any_spec] * 6,
-        out_specs=[any_spec] * 7,
+        in_specs=[any_spec] * 5,
+        out_specs=[any_spec] * 6,
         scratch_shapes=[
             pltpu.VMEM((width, cols), bf16),
             pltpu.VMEM((2, length, wide), bf16),
             pltpu.VMEM((2, length, width), bf16),
-            pltpu.VMEM((width, length), bf16),
-            pltpu.VMEM((width, length), bf16),
-            pltpu.VMEM((length, hidden), bf16),
-            pltpu.VMEM((length, 2 * hidden), bf16),
+            pltpu.VMEM((width, 2 * length), bf16),
+            pltpu.VMEM((width, 2 * length), bf16),
+            pltpu.VMEM((2 * length, hidden), bf16),
+            pltpu.VMEM((2 * length, 2 * hidden), bf16),
             pltpu.VMEM((4, length, wide), bf16),
             pltpu.VMEM((2, length, wide), bf16),
             pltpu.VMEM((4, length, wide), bf16),
@@ -897,19 +897,19 @@
             transcendentals=8 * length * hidden,
         ),
         name="group",
-    )(v, grad, xs, g_all, w, xn)
+    )(v, grad, xs, g_all, w)
 
 
 PARTNERS_BACK = ((1, 0), (2, 0), (3, 0), (0, 1), (0, 2), (0, 4), (0, 6))
 TERMS = 16
-BACK_SENDS = 4 + 3 + 3 + 2 + 3 + 2 * 4 + 2 * 3 + 1 + 6 + 3
+BACK_SENDS = 3 + 8 + 6 + 3 + 2 + 3 + 2 * 4 + 2 * 3 + 1 + 6 + 3
 
 
 def back_kernel(
     dx_own, g_ref, first, table, tiny, v, tokens, qkv, lse, cos, sin, seg_col, seg_row,
-    dx_in, grads, mix_sum, attn, xq, xn, in_all, out_all,
+    dx_in, grads, mix_sum, attn, xn, in_all, out_all,
     tokens_grad,
-    g_out, mix_in, d_out,
+    g_out, mix_in, d_out, xn_core,
     in_v, out_v, mix_v, gl, gy, gz, act_v, aq_v, pq, wo, wi, wyo, wyi, wzo, wzi, wxo, own_d,
     dn, dxn, dl, dattn, dproj, dkv, bias, tbuf,
     local_sem, send_sem, recv_sem,
@@ -952,16 +952,19 @@
         local(dx_in.at[n], in_v.at[token_rows(n), pl.ds(0, dx_in.shape[2])]) for n in range(3)
     ]
     load_out = local(out_all, out_v)
-    load_g = {j: local(grads.at[shard_rows(j)], gl.at[j // 2]) for j in (4, 0, 2, 6)}
+    load_g = {j: local(grads.at[shard_rows(j)], gl.at[j // 2]) for j in (4, 6, 2, 0)}
     load_a = local(attn.at[:, half_of(half)], aq_v.at[token_rows(0)])
     load_mix = local(mix_sum.at[2], mix_v.at[0])
     wire.meet(PARTNERS_BACK)
     got_y, got_m = {}, {}
-    for j in (4, 0, 2, 6):
-        got_y[j] = wire.send(grads.at[shard_rows(j + 1)], gy.at[j // 2], 0, 1)
+    cut = shard // 2
+    for j in (4, 6, 2, 0):
+        for n in (0, 1):
+            at = pl.ds(pl.multiple_of(flips(f, j + 1) * shard + n * cut, cut), cut)
+            got_y[j, n] = wire.send(grads.at[at], gy.at[j // 2, pl.ds(n * cut, cut)], 0, 1)
     got_a = wire.send(attn.at[:, half_of(1 - half)], aq_v.at[token_rows(1)], 1, 0)
-    got_m[2] = wire.send(mix_sum.at[1], mix_in.at[0], 2, 0)
     got_m[6] = wire.send(mix_sum.at[3], mix_v.at[1], 2, 0)
+    got_n = {2: wire.send(xn, act_v.at[token_rows(2)], 2, 0), 1: wire.send(xn, xn_core, 1, 0)}
 
     spot = lax.broadcasted_iota(jnp.int32, bias.shape, 0)
     keys_at = lax.broadcasted_iota(jnp.int32, bias.shape, 1)
@@ -1016,6 +1019,20 @@
     gain_two = lax.fori_loop(0, length // ROWS, norm_two, jnp.zeros((1, width), f32))
     tbuf[experts + 1 : experts + 2, :] = gain_two
     got_r = wire.send(act_v.at[token_rows(0)], act_v.at[token_rows(1)], 1, 0)
+    got_z = {}
+
+    def pass_y(j, n):
+        if n == 0:
+            load_g[j].wait()
+        got_y[j, n].wait_recv()
+        at = pl.ds(n * cut, cut)
+        gl[j // 2, at] = add(gl[j // 2, at], gy[j // 2, at])
+        got_z[j, n] = wire.send(gl.at[j // 2, at], gz.at[j // 2 - 1, at], 0, j)
+
+    def came(got_some, j):
+        for n in (0, 1):
+            got_some[j, n].wait_recv()
+
     load_out.wait()
 
     def to_attn(c, carry):
@@ -1024,20 +1041,12 @@
         return carry
 
     lax.fori_loop(0, WQ // 256, to_attn, 0)
+    pass_y(4, 0)
     lane = lax.broadcasted_iota(jnp.int32, (length, HD), 1)
 
     def turn_back(w):
         return w * cos[...] - pltpu.roll(w, HD // 2, 1) * sin[...]
 
-    got_z = {}
-
-    def pass_y(j):
-        load_g[j].wait()
-        got_y[j].wait_recv()
-        gl[j // 2] = add(gl[j // 2], gy[j // 2])
-        got_z[j] = wire.send(gl.at[j // 2], gz.at[j // 2 - 1], 0, j)
-
-    pass_y(4)
     for group in range(KV):
         k_at = pl.ds(WQ + group * HD, HD)
         v_at = pl.ds(WQ + WK + group * HD, HD)
@@ -1059,6 +1068,12 @@
             return carry
 
         lax.fori_loop(0, GROUP, head, 0)
+        if group == 0:
+            pass_y(4, 1)
+            load_mix.wait()
+            got_m[6].wait_recv()
+            mix_v[0] = add(mix_v[0], mix_v[1])
+            got_m[4] = wire.send(mix_v.at[0], mix_in.at[1], 0, 2)
         dproj[:, k_at] = turn_back(dkv[0] * scale).astype(bf16)
         dproj[:, v_at] = dkv[1].astype(bf16)
 
@@ -1067,6 +1082,9 @@
     for k in (2, 3, 1):
         got_p[k] = wire.send(dproj.at[:, part_of(k, cols_p)], pq.at[token_rows(k)], k, 0)
 
+    got_m[2] = wire.send(mix_sum.at[1], mix_in.at[0], 2, 0)
+    pass_y(6, 0)
+
     load_a.wait()
     got_a.wait_recv()
     got_r.wait_recv()
@@ -1079,10 +1097,13 @@
     lax.fori_loop(0, width // 256, dense_out, 0)
     got_r.wait_send()
     load_x = [local(xn, act_v.at[token_rows(0)])]
-    load_x += [local(xq.at[k], act_v.at[token_rows(k)]) for k in (1, 2, 3)]
+    got_n[1].wait_recv()
+    load_x.append(local(xn_core, act_v.at[token_rows(1)]))
     got_wo, got_wi, got_wzo, got_wzi = {}, {}, {}, {}
-    for j in (2, 6, 4, 0):
+    for j in (4, 6, 2, 0):
         got_wo[j] = wire.send(wo.at[shard_rows(j + 1)], wyo.at[j // 2], 0, 1)
+
+    pass_y(6, 1)
 
     load_in.wait()
 
@@ -1107,25 +1128,25 @@
 
     gain_one = lax.fori_loop(0, length // ROWS, norm_one, jnp.zeros((1, width), f32))
     tbuf[experts : experts + 1, :] = gain_one
-    load_mix.wait()
-    got_m[6].wait_recv()
-    mix_v[0] = add(mix_v[0], mix_v[1])
-    got_m[4] = wire.send(mix_v.at[0], mix_in.at[1], 0, 2)
-    pass_y(2)
-
+
+    pass_y(2, 0)
+    pass_y(2, 1)
     mine, other = 2 * r + low, 2 * r + 1 - low
     load_g[0].wait()
-    got_y[0].wait_recv()
-    got_z[4].wait_recv()
+    came(got_y, 0)
+    came(got_z, 4)
     gl[0] = (gl[0].astype(f32) + gy[0].astype(f32) + gz[1].astype(f32)).astype(bf16)
     kept = [local(gl.at[0], g_out.at[mine])]
     got_e = {}
 
+    got_n[2].wait_recv()
+    got_n[3] = wire.send(act_v.at[token_rows(2)], act_v.at[token_rows(3)], 1, 0)
     keep_p.wait()
     for copy in load_x:
         copy.wait()
     for k in (1, 2, 3):
         got_p[k].wait_recv()
+    got_n[3].wait_recv()
     got_e[2, 0] = wire.send(gl.at[0], g_out.at[mine], 2, 0)
     got_e[1, 0] = wire.send(gl.at[0], g_out.at[mine], 1, 0)
 
@@ -1142,25 +1163,24 @@
             wi[top : top + shard, :] = both[y * shard : (y + 1) * shard]
             wi[top + shard : top + tall, :] = jnp.zeros((TERMS, cols_p), bf16)
             wi[top + shard : top + tall, 0 : 2 * shard] = tbuf[:, lanes].astype(bf16)
-    for j in (2, 6, 4, 0):
+    for j in (4, 6, 2, 0):
         got_wi[j] = wire.send(wi.at[tall_rows(j + 1)], wyi.at[j // 2], 0, 1)
-    pass_y(6)
-
-    for j in (2, 6, 4):
+    for j in (4, 6, 2):
         got_wo[j].wait_recv()
         wyo[j // 2] = add(wo[shard_rows(j), :], wyo[j // 2])
         got_wzo[j] = wire.send(wyo.at[j // 2], wzo.at[j // 2 - 1], 0, j)
-    for j in (2, 6, 4):
-        got_wi[j].wait_recv()
-        wyi[j // 2] = add(wi[tall_rows(j), :], wyi[j // 2])
-        got_wzi[j] = wire.send(wyi.at[j // 2], wzi.at[j // 2 - 1], 0, j)
-
-    got_z[2].wait_recv()
-    got_z[6].wait_recv()
+
+    came(got_z, 2)
+    came(got_z, 6)
     gz[0] = add(gz[0], gz[2])
     kept.append(local(gz.at[0], g_out.at[other]))
     got_e[2, 1] = wire.send(gz.at[0], g_out.at[other], 2, 0)
     got_e[1, 1] = wire.send(gz.at[0], g_out.at[other], 1, 0)
+
+    for j in (4, 6, 2):
+        got_wi[j].wait_recv()
+        wyi[j // 2] = add(wi[tall_rows(j), :], wyi[j // 2])
+        got_wzi[j] = wire.send(wyi.at[j // 2], wzi.at[j // 2 - 1], 0, j)
 
     def own_rows(w, rows, y, z, got_w, got_zs):
         got_w[0].wait_recv()
@@ -1184,16 +1204,18 @@
     own_d[shard:, cols_p:] = jnp.zeros((TERMS, quarter), bf16)
     own_d[0:shard, cols_p:] = add(wxo[0, :, quarter_of(side)], wxo[1, :, 0:quarter])
     kept.append(local(own_d, d_out.at[r]))
-    got_d = [wire.send(own_d, d_out.at[r], k, 0) for k in (2, 3, 1)]
+    got_d = [wire.send(own_d, d_out.at[r], k, 0) for k in (2, 1)]
 
     far = flips(r, 2)
     for n, e in ((0, 2 * far + low), (1, 2 * far + 1 - low)):
         got_e[2, n].wait_recv()
         got_e[3, n] = wire.send(g_out.at[e], g_out.at[e], 1, 0)
+    got_d[0].wait_recv()
+    got_d.append(wire.send(d_out.at[far], d_out.at[far], 1, 0))
     for k in (1, 3):
         for n in (0, 1):
             got_e[k, n].wait_recv()
-    for copy in got_d:
+    for copy in got_d[1:]:
         copy.wait_recv()
     for k in (2, 4):
         got_m[k].wait_recv()
@@ -1204,7 +1226,7 @@
 
 def run_back(
     dx_own, grad, first, table, tiny, v, tokens, qkv, lse, cos, sin, seg_ids,
-    dx_in, grads, mix_sum, attn, xq, xn, in_all, out_all,
+    dx_in, grads, mix_sum, attn, xn, in_all, out_all,
 ):
     any_spec = pl.BlockSpec(memory_space=pl.ANY)
     vmem = pl.BlockSpec(memory_space=pltpu.VMEM)
@@ -1219,9 +1241,10 @@
             jax.ShapeDtypeStruct((8, shard, cols), bf16),
             jax.ShapeDtypeStruct((2, length, width), bf16),
             jax.ShapeDtypeStruct((4, shard + TERMS, cols_p + cols_a // 2), bf16),
+            jax.ShapeDtypeStruct((length, width), bf16),
         ],
-        in_specs=[vmem] * 13 + [any_spec] * 8,
-        out_specs=[vmem] + [any_spec] * 3,
+        in_specs=[vmem] * 13 + [any_spec] * 7,
+        out_specs=[vmem] + [any_spec] * 4,
         scratch_shapes=[
             pltpu.VMEM(in_all.shape, bf16),
             pltpu.VMEM(out_all.shape, bf16),
@@ -1259,8 +1282,63 @@
     )(
         dx_own, grad, first, table, tiny, v, tokens, qkv, lse, cos, sin,
         seg_ids.reshape(length, 1), seg_ids,
-        dx_in, grads, mix_sum, attn, xq, xn, in_all, out_all,
-    )
+        dx_in, grads, mix_sum, attn, xn, in_all, out_all,
+    )
+
+
+def finish_kernel(sums, dense, first, own, parts, e_in, e_out, in_grad, out_grad, mixed):
+    split = e_in.shape[2]
+    for c in range(0, sums.shape[2], 128):
+        part = jnp.swapaxes(sums[:, :, c : c + 128].astype(f32), 0, 1)
+        if c < split:
+            e_in[:, :, c : c + 128] = part
+        else:
+            e_out[:, :, c - split : c - split + 128] = part
+    cut = in_grad.shape[1] // 4
+    quarter = out_grad.shape[1] // 4
+    for r in range(4):
+        in_grad[:, r * cut : (r + 1) * cut] = dense[r, :, :cut].astype(f32)
+        place = 2 * (r % 2) + r // 2
+        out_grad[:, place * quarter : (place + 1) * quarter] = dense[r, :, cut:].astype(f32)
+    total = first[...] + own[0].astype(f32)
+    for n in range(parts.shape[0]):
+        total = total + parts[n].astype(f32)
+    mixed[...] = total.astype(bf16)
+
+
+def run_finish(expert_sum, dense, first, mix_sum, mix_in, hidden):
+    n_experts, shard, cols = expert_sum.shape
+    length, width = first.shape
+    steps = 6
+    rows, tokens = shard // steps, length // steps
+    cut = dense.shape[2] - width // 4
+    return pl.pallas_call(
+        finish_kernel,
+        grid=(steps,),
+        out_shape=[
+            jax.ShapeDtypeStruct((shard, n_experts, 2 * hidden), f32),
+            jax.ShapeDtypeStruct((shard, n_experts, hidden), f32),
+            jax.ShapeDtypeStruct((shard, 4 * cut), f32),
+            jax.ShapeDtypeStruct((shard, width), f32),
+            jax.ShapeDtypeStruct((length, width), bf16),
+        ],
+        in_specs=[
+            pl.BlockSpec((n_experts, rows, cols), lambda i: (0, i, 0)),
+            pl.BlockSpec((4, rows, dense.shape[2]), lambda i: (0, i, 0)),
+            pl.BlockSpec((tokens, width), lambda i: (i, 0)),
+            pl.BlockSpec((1, tokens, width), lambda i: (0, i, 0)),
+            pl.BlockSpec((mix_in.shape[0], tokens, width), lambda i: (0, i, 0)),
+        ],
+        out_specs=[
+            pl.BlockSpec((rows, n_experts, 2 * hidden), lambda i: (i, 0, 0)),
+            pl.BlockSpec((rows, n_experts, hidden), lambda i: (i, 0, 0)),
+            pl.BlockSpec((rows, 4 * cut), lambda i: (i, 0)),
+            pl.BlockSpec((rows, width), lambda i: (i, 0)),
+            pl.BlockSpec((tokens, width), lambda i: (i, 0)),
+        ],
+        compiler_params=pltpu.CompilerParams(vmem_limit_bytes=48 * MIB),
+        name="finish",
+    )(expert_sum, dense, first, mix_sum, mix_in)
 
 
 def near_layer(
@@ -1298,29 +1376,25 @@
     qkv, attn, xn, first, lse, table, small, v, in_all, out_all, w_all, g_all, xs = front(
         tokens, seg_ids, routes, cos, sin, in_proj, out_proj, tiny, mine, other, out_grad
     )
-    mix_sum, dx_own, dx_in, grads, xq, _, _ = run_group(v, out_grad, xs, g_all, w_all, xn)
-    tokens_grad, expert_sum, mix_in, dense = run_back(
+    mix_sum, dx_own, dx_in, grads, _, _ = run_group(v, out_grad, xs, g_all, w_all)
+    tokens_grad, expert_sum, mix_in, dense, _ = run_back(
         dx_own, out_grad, first, table, small, v, tokens, qkv, lse, cos, sin, seg_ids,
-        dx_in, grads, mix_sum, attn, xq, xn, in_all, out_all,
-    )
-    mixed = first + mix_sum[0].astype(f32)
-    for k in range(2):
-        mixed = mixed + mix_in[k].astype(f32)
-    cut = in_proj.shape[1] // 4
-    in_grad = dense[:, :shard, :cut].transpose(1, 0, 2).reshape(shard, -1)
-    out_proj_grad = jnp.concatenate([dense[k, :shard, cut:] for k in (0, 2, 1, 3)], axis=1)
-    expert_sum = expert_sum.transpose(1, 0, 2)
-    terms = jnp.sum(dense[:, shard:, :cut].astype(f32), axis=0)
-    terms = jnp.where(f % 2 == 0, terms[:, :shard], terms[:, shard : 2 * shard]).T
+        dx_in, grads, mix_sum, attn, xn, in_all, out_all,
+    )
+    e_in, e_out, in_grad, out_proj_grad, mixed = run_finish(
+        expert_sum, dense, first, mix_sum, mix_in, hidden
+    )
+    terms = jnp.sum(dense[:, shard:, : 2 * shard].astype(f32), axis=0)
+    terms = jnp.where(f % 2 == 0, terms[:, :shard], terms[:, shard:]).T
     return (
-        mixed.astype(bf16),
+        mixed,
         tokens_grad,
-        in_grad.astype(f32),
-        out_proj_grad.astype(f32),
+        in_grad,
+        out_proj_grad,
         terms[:, :experts],
         terms[:, experts : experts + 2],
-        expert_sum[..., : 2 * hidden].astype(f32),
-        expert_sum[..., 2 * hidden :].astype(f32),
+        e_in,
+        e_out,
     )
 
 

time: 502 us -> 460 us (0.916)
  Pallas kernels: 456 us -> 435 us
  local copies, waits for them, and re-layouts: 27.9 us -> 16.8 us
  other arithmetic: 12.7 us -> 5.96 us
    pallas_call x1, Pallas kernels: 185 us -> 168 us  [run_back(): pl.pallas_call(back_kernel, out_shape=[jax.ShapeDtypeStruct((length, widt...]
    pallas_call x1, Pallas kernels: 139 us -> 125 us  [run_group(): pl.pallas_call(group_kernel, out_shape=[jax.ShapeDtypeStruct((4, length,...]
    pallas_call x0 -> x1, Pallas kernels: none -> 11 us  [run_finish(): pl.pallas_call(finish_kernel, grid=(steps,), out_shape=[jax.ShapeDtypeStr...]
    unnamed x14 -> x12, local copies, waits for them, and re-layouts: 16.9 us -> 7.24 us
    convert_element_type x4 -> x0, other arithmetic: 7.34 us -> none  [the longest x1 4.48 us: near_layer(): mixed.astype(bf16)]
where the time goes in v5:
time: 460 us; the launch traced here: 459 us
  Pallas kernels  435 us (95%)
  local copies, waits for them, and re-layouts  16.8 us (4%)
  other arithmetic  5.96 us (1%)
    pallas_call x1, Pallas kernels, run_back(): pl.pallas_call(back_kernel, out_shape=[jax.ShapeDtypeStruct((length, widt...  168 us
    pallas_call x1, Pallas kernels, front(): pl.pallas_call(front_kernel, out_shape=[jax.ShapeDtypeStruct((length, col...  132 us
    pallas_call x1, Pallas kernels, run_group(): pl.pallas_call(group_kernel, out_shape=[jax.ShapeDtypeStruct((4, length,...  125 us
    pallas_call x1, Pallas kernels, run_finish(): pl.pallas_call(finish_kernel, grid=(steps,), out_shape=[jax.ShapeDtypeStr...  11 us

profile of v5, /device:TPU:1, one launch (start us, length us, event | category | flops | bytes accessed | tf_op | source)
XLA Modules:
  0.0 458.9 jit_solution(12843405839926211495)
XLA Ops:
  0.7 0.1 pad.8.clone
  0.7 0.8 maximum_maximum_fusion
  1.5 0.7 pad_select_fusion.tiny_ref
  2.2 1.5 copy.23.seg_col
  3.7 1.5 copy.24.routes
  5.2 0.7 fusion.2
  6.0 0.0 copy-start.3
  6.0 0.9 pad_maximum_fusion.2
  6.9 4.2 constant_dynamic-slice_fusion
  11.1 0.1 copy_bitcast_fusion.2
  11.2 0.0 copy-done.3
  11.2 2.4 constant_dynamic-slice_fusion.1
  13.6 0.2 copy_bitcast_fusion
  13.8 1.0 pad_maximum_fusion.1.other_ref
  14.7 1.0 pad_maximum_fusion.mine_ref
  15.7 132.0 %front.1 = (bf16[384,2048]{1,0:T(8,128)(2,1)}, bf16[384,1536]{1,0:T(8,128)(2,1)}, bf16[384,1536]{1,0:T(8,128)(2,1)}, f32[384,1536]{1,0:T(8,128)}, f32[384,128]{1...) custom-call(bf16[384,1536]{1,0:T(8,128)(2,1)} %tokens.3, ...), custom_call_target="tpu_custom_call" | custom-call | tf_op jit(solution)/shard_map/front/pallas_call | solution.py:538
  147.7 124.9 %group.1 = (bf16[4,384,1536]{2,1,0:T(8,128)(2,1)}, bf16[384,1664]{1,0:T(8,128)(2,1)}, bf16[3,384,1664]{2,1,0:T(8,128)(2,1)}, bf16[1536,2304]{1,0:T(8,128)(2,1)},...) custom-call(bf16[384,1664]{1,0:T(8,128)(2,1)} %get-tuple-element.34.v_ref.v, bf16[384,1536]{1,0:T(8,128)(2,1)} %g_ref.5, ...), custom_call_target="tpu_custom_call" | custom-call | flops 65229815808 | bytes 51904512 | tf_op jit(solution)/shard_map/group/pallas_call | solution.py:855
  272.6 167.5 %back.1 = (bf16[384,1536]{1,0:T(8,128)(2,1)}, bf16[8,192,2304]{2,1,0:T(8,128)(2,1)}, bf16[2,384,1536]{2,1,0:T(8,128)(2,1)}, bf16[4,208,896]{2,1,0:T(8,128)(2,1)}, bf16[384,1536]{1,0:T(8,128)(2,1)}) custom-call(bf16[384,1664]{1,0:T(8,128)(2,1)} %get-tuple-element.38.dx_own, bf16[384,1536]{1,0:T(8,128)(2,1)} %g_ref.5, f32[384,1536]{1,0:T(8,128)} %get-tuple-element.39.first, ...), custom_call_target="tpu_custom_call" | custom-call | tf_op jit(solution)/shard_map/back/pallas_call | solution.py:1237
  440.1 0.8 convert_reduce_fusion
  440.9 0.1 fusion.3
  441.0 0.6 slice.23
  441.6 0.6 slice.22
  442.2 0.0 copy-start
  442.2 1.7 copy-done
  443.9 0.0 copy-start.1
  443.9 1.7 copy-done.1
  445.5 0.0 copy-start.2
  445.5 1.4 copy-done.2
  446.9 0.0 copy-start.4
  446.9 11.0 %finish.1 = (f32[192,8,1536]{2,1,0:T(8,128)}, f32[192,8,768]{2,1,0:T(8,128)}, f32[192,2048]{1,0:T(8,128)}, f32[192,1536]{1,0:T(8,128)}, bf16[384,1536]{1,0:T(8,128)(2,1)}) custom-call(bf16[8,192,2304]{2,1,0:T(8,128)(2,1)} %get-tuple-element.51.sums, bf16[4,208,896]{2,1,0:T(8,128)(2,1)S(1)} %copy-done.2, f32[384,1536]{1,0:T(8,128)S(1)} %copy-done, ...), custom_call_target="tpu_custom_call" | custom-call | tf_op jit(solution)/shard_map/finish/pallas_call | solution.py:1315
  457.9 0.0 copy-done.4
  457.9 1.0 copy.35
  (2 shorter events, 0.0 us)
Async XLA Ops:
  6.0 5.2 %copy-start.3 = (bf16[192,8,1536]{2,1,0:T(8,128)(2,1)S(1)}, bf16[192,8,1536]{2,1,0:T(8,128)(2,1)}, u32[]{:S(2)}) copy-start(bf16[192,8,1536]{2,1,0:T(8,128)(2,1)} %param.17) | copy-start | bytes 14155780
  442.2 1.7 copy-start
  443.9 1.7 copy-start.1
  445.5 1.4 copy-start.2
  446.9 11.0 %copy-start.4 = (bf16[384,1536]{1,0:T(8,128)(2,1)S(1)}, bf16[384,1536]{1,0:T(8,128)(2,1)}, u32[]{:S(2)}) copy-start(bf16[384,1536]{1,0:T(8,128)(2,1)} %get-tuple-element.82) | copy-start | bytes 3538948

commit v6 on v5

--- a/solution.py
+++ b/solution.py
@@ -902,7 +902,7 @@
 
 PARTNERS_BACK = ((1, 0), (2, 0), (3, 0), (0, 1), (0, 2), (0, 4), (0, 6))
 TERMS = 16
-BACK_SENDS = 3 + 8 + 6 + 3 + 2 + 3 + 2 * 4 + 2 * 3 + 1 + 6 + 3
+BACK_SENDS = 3 + 8 + 6 + 3 + 2 + 3 + 2 * 4 + 2 * 3 + 1 + 6 + 6
 
 
 def back_kernel(
@@ -957,11 +957,37 @@
     load_mix = local(mix_sum.at[2], mix_v.at[0])
     wire.meet(PARTNERS_BACK)
     got_y, got_m = {}, {}
+    place_z = f // 2
+    inner = (place_z == 1) | (place_z == 2)
     cut = shard // 2
+    got_z = {}
     for j in (4, 6, 2, 0):
         for n in (0, 1):
             at = pl.ds(pl.multiple_of(flips(f, j + 1) * shard + n * cut, cut), cut)
-            got_y[j, n] = wire.send(grads.at[at], gy.at[j // 2, pl.ds(n * cut, cut)], 0, 1)
+            got_y[j, n] = wire.plan(grads.at[at], gy.at[j // 2, pl.ds(n * cut, cut)], 0, 1)
+            wire.sent.append(got_y[j, n])
+            if j:
+                at = pl.ds(n * cut, cut)
+                got_z[j, n] = wire.plan(gl.at[j // 2, at], gz.at[j // 2 - 1, at], 0, j)
+                wire.sent.append(got_z[j, n])
+
+    def by_place(do, outer_j, inner_j, n):
+        @pl.when(inner)
+        def _():
+            do(inner_j, n)
+
+        @pl.when(jnp.logical_not(inner))
+        def _():
+            do(outer_j, n)
+
+    def send_y(j, n):
+        got_y[j, n].start()
+
+    for outer_j, inner_j in ((4, 2), (6, 4), (2, 6)):
+        for n in (0, 1):
+            by_place(send_y, outer_j, inner_j, n)
+    for n in (0, 1):
+        send_y(0, n)
     got_a = wire.send(attn.at[:, half_of(1 - half)], aq_v.at[token_rows(1)], 1, 0)
     got_m[6] = wire.send(mix_sum.at[3], mix_v.at[1], 2, 0)
     got_n = {2: wire.send(xn, act_v.at[token_rows(2)], 2, 0), 1: wire.send(xn, xn_core, 1, 0)}
@@ -1019,15 +1045,13 @@
     gain_two = lax.fori_loop(0, length // ROWS, norm_two, jnp.zeros((1, width), f32))
     tbuf[experts + 1 : experts + 2, :] = gain_two
     got_r = wire.send(act_v.at[token_rows(0)], act_v.at[token_rows(1)], 1, 0)
-    got_z = {}
-
     def pass_y(j, n):
         if n == 0:
             load_g[j].wait()
         got_y[j, n].wait_recv()
         at = pl.ds(n * cut, cut)
         gl[j // 2, at] = add(gl[j // 2, at], gy[j // 2, at])
-        got_z[j, n] = wire.send(gl.at[j // 2, at], gz.at[j // 2 - 1, at], 0, j)
+        got_z[j, n].start()
 
     def came(got_some, j):
         for n in (0, 1):
@@ -1041,7 +1065,7 @@
         return carry
 
     lax.fori_loop(0, WQ // 256, to_attn, 0)
-    pass_y(4, 0)
+    by_place(pass_y, 4, 2, 0)
     lane = lax.broadcasted_iota(jnp.int32, (length, HD), 1)
 
     def turn_back(w):
@@ -1069,7 +1093,7 @@
 
         lax.fori_loop(0, GROUP, head, 0)
         if group == 0:
-            pass_y(4, 1)
+            by_place(pass_y, 4, 2, 1)
             load_mix.wait()
             got_m[6].wait_recv()
             mix_v[0] = add(mix_v[0], mix_v[1])
@@ -1083,7 +1107,7 @@
         got_p[k] = wire.send(dproj.at[:, part_of(k, cols_p)], pq.at[token_rows(k)], k, 0)
 
     got_m[2] = wire.send(mix_sum.at[1], mix_in.at[0], 2, 0)
-    pass_y(6, 0)
+    by_place(pass_y, 6, 4, 0)
 
     load_a.wait()
     got_a.wait_recv()
@@ -1103,7 +1127,7 @@
     for j in (4, 6, 2, 0):
         got_wo[j] = wire.send(wo.at[shard_rows(j + 1)], wyo.at[j // 2], 0, 1)
 
-    pass_y(6, 1)
+    by_place(pass_y, 6, 4, 1)
 
     load_in.wait()
 
@@ -1129,8 +1153,8 @@
     gain_one = lax.fori_loop(0, length // ROWS, norm_one, jnp.zeros((1, width), f32))
     tbuf[experts : experts + 1, :] = gain_one
 
-    pass_y(2, 0)
-    pass_y(2, 1)
+    by_place(pass_y, 2, 6, 0)
+    by_place(pass_y, 2, 6, 1)
     mine, other = 2 * r + low, 2 * r + 1 - low
     load_g[0].wait()
     came(got_y, 0)
@@ -1199,24 +1223,35 @@
     got_x = wire.send(
         wxo.at[0, :, quarter_of(1 - side)], wxo.at[1, :, pl.ds(0, quarter)], 2, 0
     )
-    own_d[:, 0:cols_p] = own_rows(wi, tall_rows(0), wyi, wzi, got_wi, got_wzi).astype(bf16)
     got_x.wait_recv()
     own_d[shard:, cols_p:] = jnp.zeros((TERMS, quarter), bf16)
     own_d[0:shard, cols_p:] = add(wxo[0, :, quarter_of(side)], wxo[1, :, 0:quarter])
-    kept.append(local(own_d, d_out.at[r]))
-    got_d = [wire.send(own_d, d_out.at[r], k, 0) for k in (2, 1)]
+    got_d = {}
+
+    def send_d(n, columns):
+        kept.append(local(own_d.at[:, columns], d_out.at[r, :, columns]))
+        for k in (2, 1):
+            got_d[k, n] = wire.send(own_d.at[:, columns], d_out.at[r, :, columns], k, 0)
+
+    parts_d = (pl.ds(cols_p, quarter), pl.ds(0, cols_p))
+    send_d(0, parts_d[0])
+    own_d[:, 0:cols_p] = own_rows(wi, tall_rows(0), wyi, wzi, got_wi, got_wzi).astype(bf16)
+    send_d(1, parts_d[1])
 
     far = flips(r, 2)
     for n, e in ((0, 2 * far + low), (1, 2 * far + 1 - low)):
         got_e[2, n].wait_recv()
         got_e[3, n] = wire.send(g_out.at[e], g_out.at[e], 1, 0)
-    got_d[0].wait_recv()
-    got_d.append(wire.send(d_out.at[far], d_out.at[far], 1, 0))
+    for n, columns in enumerate(parts_d):
+        got_d[2, n].wait_recv()
+        at = d_out.at[far, :, columns]
+        got_d[3, n] = wire.send(at, at, 1, 0)
     for k in (1, 3):
         for n in (0, 1):
             got_e[k, n].wait_recv()
-    for copy in got_d[1:]:
-        copy.wait_recv()
+    for k in (1, 3):
+        for n in (0, 1):
+            got_d[k, n].wait_recv()
     for k in (2, 4):
         got_m[k].wait_recv()
     for copy in kept:

time: 460 us -> 447 us (0.972)
  Pallas kernels: 435 us -> 423 us
    pallas_call x1, Pallas kernels: 168 us -> 155 us  [run_back(): pl.pallas_call(back_kernel, out_shape=[jax.ShapeDtypeStruct((length, widt...]
where the time goes in v6:
time: 447 us
  Pallas kernels  423 us (95%)
  local copies, waits for them, and re-layouts  16.8 us (4%)
  other arithmetic  5.96 us (1%)
    pallas_call x1, Pallas kernels, run_back(): pl.pallas_call(back_kernel, out_shape=[jax.ShapeDtypeStruct((length, widt...  155 us
    pallas_call x1, Pallas kernels, front(): pl.pallas_call(front_kernel, out_shape=[jax.ShapeDtypeStruct((length, col...  132 us
    pallas_call x1, Pallas kernels, run_group(): pl.pallas_call(group_kernel, out_shape=[jax.ShapeDtypeStruct((4, length,...  125 us
    pallas_call x1, Pallas kernels, run_finish(): pl.pallas_call(finish_kernel, grid=(steps,), out_shape=[jax.ShapeDtypeStr...  11 us

profile of v6, /device:TPU:1, one launch (start us, length us, event | category | flops | bytes accessed | tf_op | source)
XLA Modules:
  0.0 446.5 jit_solution(13112536071235623041)
XLA Ops:
  0.7 0.1 pad.8.clone
  0.7 0.8 maximum_maximum_fusion
  1.5 0.7 pad_select_fusion.tiny_ref
  2.2 1.5 copy.23.seg_col
  3.7 1.5 copy.24.routes
  5.2 0.7 fusion.2
  6.0 0.0 copy-start.3
  6.0 0.9 pad_maximum_fusion.2
  6.9 4.2 constant_dynamic-slice_fusion
  11.1 0.1 copy_bitcast_fusion.2
  11.2 0.0 copy-done.3
  11.2 2.4 constant_dynamic-slice_fusion.1
  13.6 0.2 copy_bitcast_fusion
  13.8 1.0 pad_maximum_fusion.1.other_ref
  14.7 1.0 pad_maximum_fusion.mine_ref
  15.7 132.0 %front.1 = (bf16[384,2048]{1,0:T(8,128)(2,1)}, bf16[384,1536]{1,0:T(8,128)(2,1)}, bf16[384,1536]{1,0:T(8,128)(2,1)}, f32[384,1536]{1,0:T(8,128)}, f32[384,128]{1...) custom-call(bf16[384,1536]{1,0:T(8,128)(2,1)} %tokens.3, ...), custom_call_target="tpu_custom_call" | custom-call | tf_op jit(solution)/shard_map/front/pallas_call | solution.py:538
  147.7 124.9 %group.1 = (bf16[4,384,1536]{2,1,0:T(8,128)(2,1)}, bf16[384,1664]{1,0:T(8,128)(2,1)}, bf16[3,384,1664]{2,1,0:T(8,128)(2,1)}, bf16[1536,2304]{1,0:T(8,128)(2,1)},...) custom-call(bf16[384,1664]{1,0:T(8,128)(2,1)} %get-tuple-element.34.v_ref.v, bf16[384,1536]{1,0:T(8,128)(2,1)} %g_ref.5, ...), custom_call_target="tpu_custom_call" | custom-call | flops 65229815808 | bytes 51904512 | tf_op jit(solution)/shard_map/group/pallas_call | solution.py:855
  272.6 155.2 %back.1 = (bf16[384,1536]{1,0:T(8,128)(2,1)}, bf16[8,192,2304]{2,1,0:T(8,128)(2,1)}, bf16[2,384,1536]{2,1,0:T(8,128)(2,1)}, bf16[4,208,896]{2,1,0:T(8,128)(2,1)}, bf16[384,1536]{1,0:T(8,128)(2,1)}) custom-call(bf16[384,1664]{1,0:T(8,128)(2,1)} %get-tuple-element.38.dx_own, bf16[384,1536]{1,0:T(8,128)(2,1)} %g_ref.5, f32[384,1536]{1,0:T(8,128)} %get-tuple-element.39.first, ...), custom_call_target="tpu_custom_call" | custom-call | tf_op jit(solution)/shard_map/back/pallas_call | solution.py:1272
  427.7 0.8 convert_reduce_fusion
  428.6 0.1 fusion.3
  428.6 0.6 slice.23
  429.2 0.6 slice.22
  429.8 0.0 copy-start
  429.8 1.7 copy-done
  431.5 0.0 copy-start.1
  431.5 1.7 copy-done.1
  433.1 0.0 copy-start.2
  433.1 1.4 copy-done.2
  434.5 0.0 copy-start.4
  434.5 11.0 %finish.1 = (f32[192,8,1536]{2,1,0:T(8,128)}, f32[192,8,768]{2,1,0:T(8,128)}, f32[192,2048]{1,0:T(8,128)}, f32[192,1536]{1,0:T(8,128)}, bf16[384,1536]{1,0:T(8,128)(2,1)}) custom-call(bf16[8,192,2304]{2,1,0:T(8,128)(2,1)} %get-tuple-element.51.sums, bf16[4,208,896]{2,1,0:T(8,128)(2,1)S(1)} %copy-done.2, f32[384,1536]{1,0:T(8,128)S(1)} %copy-done, ...), custom_call_target="tpu_custom_call" | custom-call | tf_op jit(solution)/shard_map/finish/pallas_call | solution.py:1350
  445.5 0.0 copy-done.4
  445.5 1.0 copy.35
  (2 shorter events, 0.0 us)
Async XLA Ops:
  6.0 5.2 %copy-start.3 = (bf16[192,8,1536]{2,1,0:T(8,128)(2,1)S(1)}, bf16[192,8,1536]{2,1,0:T(8,128)(2,1)}, u32[]{:S(2)}) copy-start(bf16[192,8,1536]{2,1,0:T(8,128)(2,1)} %param.17) | copy-start | bytes 14155780
  429.8 1.7 copy-start
  431.5 1.7 copy-start.1
  433.1 1.4 copy-start.2
  434.5 11.0 %copy-start.4 = (bf16[384,1536]{1,0:T(8,128)(2,1)S(1)}, bf16[384,1536]{1,0:T(8,128)(2,1)}, u32[]{:S(2)}) copy-start(bf16[384,1536]{1,0:T(8,128)(2,1)} %get-tuple-element.82) | copy-start | bytes 3538948

commit v7 on v6

--- a/solution.py
+++ b/solution.py
@@ -297,16 +297,23 @@
 ROWS = 64
 
 
+def as_columns(rows):
+    rows = rows.astype(f32)
+    rest = jnp.zeros((128 - rows.shape[0], rows.shape[1]), f32)
+    return jnp.concatenate([rows, rest], axis=0).T
+
+
 def turn(v, cosine, sine):
     return v * cosine + pltpu.roll(v, HD // 2, 1) * sine
 
 
 def front_kernel(
-    tokens, seg_col, seg_row, routes, cos, sin,
-    in_ref, out_ref, tiny_ref, mine_ref, other_ref, g_ref,
+    tokens, seg_row, routes, cos, sin,
+    in_ref, out_ref, tiny_ref, e_in_ref, e_out_ref, g_ref,
     qkv, attn, xn, first, lse, table, tiny_out, v,
     in_all, out_all, w_all, g_all, xs,
-    in_v, out_v, tiny_v, rt, bias, w_buf, local_sem, send_sem, recv_sem,
+    in_v, out_v, tiny_v, rt, bias, e_in, e_out, e_part, mine_ref, other_ref,
+    local_sem, send_sem, recv_sem,
 ):
     wire = Wire(send_sem, recv_sem)
     r, f = wire.r, wire.f
@@ -331,7 +338,7 @@
     own_in = local(0, in_ref, in_v.at[shard_rows(0)])
     own_out = local(1, out_ref, out_v.at[shard_rows(0)])
     own_tiny = local(2, tiny_ref, tiny_v.at[f])
-    own_w = local(3, mine_ref, w_buf)
+    own_w = (local(3, e_in_ref, e_in), local(7, e_out_ref, e_out))
     wire.meet(PARTNERS)
 
     own = pl.ds(pl.multiple_of(r * quarter, quarter), quarter)
@@ -378,8 +385,6 @@
 
     own_pieces("in")
     own_pieces("out")
-    own_w.wait()
-    kept = [local(4, w_buf, w_all.at[shard_rows(0)])]
 
     for m in (2, 4, 6):
         got_t[m].wait_recv()
@@ -406,8 +411,19 @@
     lax.fori_loop(0, length // ROWS, norm_one, 0)
     spot = lax.broadcasted_iota(jnp.int32, bias.shape, 0)
     keys_at = lax.broadcasted_iota(jnp.int32, bias.shape, 1)
-    bias[...] = jnp.where((spot >= keys_at) & (seg_col[...] == seg_row[...]), 0.0, -1e30)
-
+    seg_col = as_columns(seg_row[...])[:, 0:1].astype(jnp.int32)
+    bias[...] = jnp.where((spot >= keys_at) & (seg_col == seg_row[...]), 0.0, -1e30)
+
+    for copy in own_w:
+        copy.wait()
+    plane = lax.rem(f // 2, 2)
+    split = e_in.shape[2]
+    for c in range(0, mine_ref.shape[1], 128):
+        part = e_in[:, :, c : c + 128] if c < split else e_out[:, :, c - split : c - split + 128]
+        e_part[...] = jnp.swapaxes(part.astype(f32), 0, 1)
+        mine_ref[:, c : c + 128] = e_part[2 * r + plane].astype(bf16)
+        other_ref[:, c : c + 128] = e_part[2 * r + 1 - plane].astype(bf16)
+    kept = [local(4, mine_ref, w_all.at[shard_rows(0)])]
     cut = shard // CUTS
 
     def send_w(n, src, d_f):
@@ -496,9 +512,10 @@
 
     lax.fori_loop(0, length // ROWS, norm_two, 0)
     logits = contract_cols(v[:, 0:width], rt[...])
-    chosen = lane == routes[:, 0:1]
-    for j in range(1, routes.shape[1]):
-        chosen = chosen | (lane == routes[:, j : j + 1])
+    named = as_columns(routes[...]).astype(jnp.int32)
+    chosen = lane == named[:, 0:1]
+    for j in range(1, routes.shape[0]):
+        chosen = chosen | (lane == named[:, j : j + 1])
     logits = jnp.where(chosen, logits, -1e30)
     expo = jnp.exp(logits - jnp.max(logits, axis=-1, keepdims=True))
     expo = jnp.where(chosen, expo, 0.0)
@@ -528,13 +545,16 @@
     wire.finish()
 
 
-def front(tokens, seg_ids, routes, cos, sin, in_proj, out_proj, tiny, mine, other, grad):
+def front(
+    tokens, seg_ids, routes, cos, sin, in_proj, out_proj, tiny, expert_in, expert_out, grad
+):
     any_spec = pl.BlockSpec(memory_space=pl.ANY)
     vmem = pl.BlockSpec(memory_space=pltpu.VMEM)
     length, width = tokens.shape
     shard, cols = in_proj.shape
     whole = 8 * shard
     wide = width + EXTRA
+    e_cols = expert_in.shape[2] + expert_out.shape[2]
     return pl.pallas_call(
         front_kernel,
         out_shape=[
@@ -548,11 +568,11 @@
             jax.ShapeDtypeStruct((length, wide), bf16),
             jax.ShapeDtypeStruct((whole, cols), bf16),
             jax.ShapeDtypeStruct((whole, out_proj.shape[1]), bf16),
-            jax.ShapeDtypeStruct((whole, mine.shape[1]), bf16),
+            jax.ShapeDtypeStruct((whole, e_cols), bf16),
             jax.ShapeDtypeStruct((5,) + grad.shape, bf16),
             jax.ShapeDtypeStruct((4, length, wide), bf16),
         ],
-        in_specs=[vmem] * 6 + [any_spec] * 6,
+        in_specs=[vmem] * 5 + [any_spec] * 6,
         out_specs=[vmem] * 8 + [any_spec] * 5,
         scratch_shapes=[
             pltpu.VMEM((whole, cols), bf16),
@@ -560,7 +580,11 @@
             pltpu.VMEM((8,) + tiny.shape, bf16),
             pltpu.VMEM((EXTRA, width), bf16),
             pltpu.VMEM((length, length), f32),
-            pltpu.VMEM(mine.shape, bf16),
+            pltpu.VMEM(expert_in.shape, bf16),
+            pltpu.VMEM(expert_out.shape, bf16),
+            pltpu.VMEM((expert_in.shape[1], shard, 128), f32),
+            pltpu.VMEM((shard, e_cols), bf16),
+            pltpu.VMEM((shard, e_cols), bf16),
             pltpu.SemaphoreType.DMA((8,)),
             pltpu.SemaphoreType.DMA((FRONT_SENDS,)),
             pltpu.SemaphoreType.DMA((FRONT_SENDS,)),
@@ -570,8 +594,8 @@
         ),
         name="front",
     )(
-        tokens, seg_ids.reshape(length, 1), seg_ids, routes, cos, sin,
-        in_proj, out_proj, tiny, mine, other, grad,
+        tokens, seg_ids, routes.T, cos, sin,
+        in_proj, out_proj, tiny, expert_in, expert_out, grad,
     )
 
 
@@ -906,7 +930,7 @@
 
 
 def back_kernel(
-    dx_own, g_ref, first, table, tiny, v, tokens, qkv, lse, cos, sin, seg_col, seg_row,
+    dx_own, g_ref, first, table, tiny, v, tokens, qkv, lse, cos, sin, seg_row,
     dx_in, grads, mix_sum, attn, xn, in_all, out_all,
     tokens_grad,
     g_out, mix_in, d_out, xn_core,
@@ -994,7 +1018,8 @@
 
     spot = lax.broadcasted_iota(jnp.int32, bias.shape, 0)
     keys_at = lax.broadcasted_iota(jnp.int32, bias.shape, 1)
-    bias[...] = jnp.where((spot >= keys_at) & (seg_col[...] == seg_row[...]), 0.0, -1e30)
+    seg_col = as_columns(seg_row[...])[:, 0:1].astype(jnp.int32)
+    bias[...] = jnp.where((spot >= keys_at) & (seg_col == seg_row[...]), 0.0, -1e30)
     tbuf[...] = jnp.zeros_like(tbuf)
     for copy in load_dx:
         copy.wait()
@@ -1278,7 +1303,7 @@
             jax.ShapeDtypeStruct((4, shard + TERMS, cols_p + cols_a // 2), bf16),
             jax.ShapeDtypeStruct((length, width), bf16),
         ],
-        in_specs=[vmem] * 13 + [any_spec] * 7,
+        in_specs=[vmem] * 12 + [any_spec] * 7,
         out_specs=[vmem] + [any_spec] * 4,
         scratch_shapes=[
             pltpu.VMEM(in_all.shape, bf16),
@@ -1316,7 +1341,7 @@
         name="back",
     )(
         dx_own, grad, first, table, tiny, v, tokens, qkv, lse, cos, sin,
-        seg_ids.reshape(length, 1), seg_ids,
+        seg_ids,
         dx_in, grads, mix_sum, attn, xn, in_all, out_all,
     )
 
@@ -1371,7 +1396,7 @@
             pl.BlockSpec((rows, width), lambda i: (i, 0)),
             pl.BlockSpec((tokens, width), lambda i: (i, 0)),
         ],
-        compiler_params=pltpu.CompilerParams(vmem_limit_bytes=48 * MIB),
+        compiler_params=pltpu.CompilerParams(vmem_limit_bytes=62 * MIB),
         name="finish",
     )(expert_sum, dense, first, mix_sum, mix_in)
 
@@ -1384,7 +1409,7 @@
     experts = router.shape[1]
     hidden = expert_out.shape[2]
     shard = router.shape[0]
-    r, f = lax.axis_index("replica"), lax.axis_index("fsdp")
+    f = lax.axis_index("fsdp")
     cosine, sine = [t[:, 0] for t in tables(length)]
     cos = jnp.concatenate([cosine, cosine], axis=1)
     sin = jnp.concatenate([-sine, sine], axis=1)
@@ -1397,19 +1422,9 @@
         jnp.concatenate([tiny, none], axis=1),
         jnp.concatenate([none, tiny], axis=1),
     )
-    low = (f >> 1) & 1
-    mine, other = [
-        jnp.concatenate(
-            [
-                lax.dynamic_index_in_dim(expert_in, e, 1, keepdims=False),
-                lax.dynamic_index_in_dim(expert_out, e, 1, keepdims=False),
-            ],
-            axis=1,
-        )
-        for e in (2 * r + low, 2 * r + 1 - low)
-    ]
     qkv, attn, xn, first, lse, table, small, v, in_all, out_all, w_all, g_all, xs = front(
-        tokens, seg_ids, routes, cos, sin, in_proj, out_proj, tiny, mine, other, out_grad
+        tokens, seg_ids, routes, cos, sin, in_proj, out_proj, tiny, expert_in, expert_out,
+        out_grad,
     )
     mix_sum, dx_own, dx_in, grads, _, _ = run_group(v, out_grad, xs, g_all, w_all)
     tokens_grad, expert_sum, mix_in, dense, _ = run_back(

time: 447 us -> 432 us (0.966)
  local copies, waits for them, and re-layouts: 16.8 us -> 2.28 us
    dynamic_slice x2 -> x0, local copies, waits for them, and re-layouts: 6.62 us -> none  [the longest x1 4.19 us: near_layer(): lax.dynamic_index_in_dim(expert_out, e, 1, keepdims=False)]
    unnamed x12 -> x3, local copies, waits for them, and re-layouts: 7.24 us -> 1.02 us
where the time goes in v7:
time: 432 us
  Pallas kernels  425 us (98%)
    pallas_call x1, Pallas kernels, run_back(): pl.pallas_call(back_kernel, out_shape=[jax.ShapeDtypeStruct((length, widt...  155 us
    pallas_call x1, Pallas kernels, front(): pl.pallas_call(front_kernel, out_shape=[jax.ShapeDtypeStruct((length, col...  136 us
    pallas_call x1, Pallas kernels, run_group(): pl.pallas_call(group_kernel, out_shape=[jax.ShapeDtypeStruct((4, length,...  121 us
    pallas_call x1, Pallas kernels, run_finish(): pl.pallas_call(finish_kernel, grid=(steps,), out_shape=[jax.ShapeDtypeStr...  12.9 us

profile of v7, /device:TPU:1, one launch (start us, length us, event | category | flops | bytes accessed | tf_op | source)
XLA Modules:
  0.0 431.9 jit_solution(17863200260329332992)
XLA Ops:
  0.7 0.1 pad.4.clone
  0.7 0.8 maximum_maximum_fusion
  1.5 0.7 pad_select_fusion.tiny_ref
  2.2 0.7 fusion.2
  2.9 0.9 pad_maximum_fusion
  3.9 135.5 %front.1 = (bf16[384,2048]{1,0:T(8,128)(2,1)}, bf16[384,1536]{1,0:T(8,128)(2,1)}, bf16[384,1536]{1,0:T(8,128)(2,1)}, f32[384,1536]{1,0:T(8,128)}, f32[384,128]{1...) custom-call(bf16[384,1536]{1,0:T(8,128)(2,1)} %tokens.3, ...), custom_call_target="tpu_custom_call" | custom-call | tf_op jit(solution)/shard_map/front/pallas_call | solution.py:558
  139.4 121.3 %group.1 = (bf16[4,384,1536]{2,1,0:T(8,128)(2,1)}, bf16[384,1664]{1,0:T(8,128)(2,1)}, bf16[3,384,1664]{2,1,0:T(8,128)(2,1)}, bf16[1536,2304]{1,0:T(8,128)(2,1)},...) custom-call(bf16[384,1664]{1,0:T(8,128)(2,1)} %get-tuple-element.34.v_ref.v, bf16[384,1536]{1,0:T(8,128)(2,1)} %g_ref.5, ...), custom_call_target="tpu_custom_call" | custom-call | flops 65229815808 | bytes 51904512 | tf_op jit(solution)/shard_map/group/pallas_call | solution.py:879
  260.7 155.2 %back.1 = (bf16[384,1536]{1,0:T(8,128)(2,1)}, bf16[8,192,2304]{2,1,0:T(8,128)(2,1)}, bf16[2,384,1536]{2,1,0:T(8,128)(2,1)}, bf16[4,208,896]{2,1,0:T(8,128)(2,1)}, bf16[384,1536]{1,0:T(8,128)(2,1)}) custom-call(bf16[384,1664]{1,0:T(8,128)(2,1)} %get-tuple-element.38.dx_own, bf16[384,1536]{1,0:T(8,128)(2,1)} %g_ref.5, f32[384,1536]{1,0:T(8,128)} %get-tuple-element.39.first, ...), custom_call_target="tpu_custom_call" | custom-call | tf_op jit(solution)/shard_map/back/pallas_call | solution.py:1297
  415.9 0.8 convert_reduce_fusion
  416.7 0.1 fusion.3
  416.8 0.6 slice.23
  417.3 0.6 slice.22
  417.9 0.0 copy-start
  417.9 12.9 %finish.1 = (f32[192,8,1536]{2,1,0:T(8,128)}, f32[192,8,768]{2,1,0:T(8,128)}, f32[192,2048]{1,0:T(8,128)}, f32[192,1536]{1,0:T(8,128)}, bf16[384,1536]{1,0:T(8,128)(2,1)}) custom-call(bf16[8,192,2304]{2,1,0:T(8,128)(2,1)} %get-tuple-element.51.sums, bf16[4,208,896]{2,1,0:T(8,128)(2,1)} %get-tuple-element.52.dense, f32[384,1536]{1,0:T(8,128)} %get-tuple-element.39.first, ...), custom_call_target="tpu_custom_call" | custom-call | tf_op jit(solution)/shard_map/finish/pallas_call | solution.py:1375
  430.9 0.0 copy-done
  430.9 1.0 copy.19
  (2 shorter events, 0.0 us)
Async XLA Ops:
  417.9 12.9 %copy-start = (bf16[384,1536]{1,0:T(8,128)(2,1)S(1)}, bf16[384,1536]{1,0:T(8,128)(2,1)}, u32[]{:S(2)}) copy-start(bf16[384,1536]{1,0:T(8,128)(2,1)} %get-tuple-element.74) | copy-start | bytes 3538948

commit v8 on v7

--- a/solution.py
+++ b/solution.py
@@ -310,10 +310,10 @@
 def front_kernel(
     tokens, seg_row, routes, cos, sin,
     in_ref, out_ref, tiny_ref, e_in_ref, e_out_ref, g_ref,
-    qkv, attn, xn, first, lse, table, tiny_out, v,
+    qkv_o, attn_o, xn_o, first_o, lse, table, tiny_out, v_o,
     in_all, out_all, w_all, g_all, xs,
     in_v, out_v, tiny_v, rt, bias, e_in, e_out, e_part, mine_ref, other_ref,
-    local_sem, send_sem, recv_sem,
+    qkv, attn, xn, first, v, local_sem, send_sem, recv_sem,
 ):
     wire = Wire(send_sem, recv_sem)
     r, f = wire.r, wire.f
@@ -526,6 +526,10 @@
 
     got_x[2] = wire.send(v, xs.at[2], 2, 0)
     got_x[1] = wire.send(v, xs.at[1], 1, 0)
+    for n, (src, dst) in enumerate(
+        ((qkv, qkv_o), (attn, attn_o), (xn, xn_o), (first, first_o), (v, v_o))
+    ):
+        kept.append(local(8 + n, src, dst))
     for n in range(2, CUTS):
         for m in (2, 4, 6):
             pass_w(n, m)
@@ -573,7 +577,7 @@
             jax.ShapeDtypeStruct((4, length, wide), bf16),
         ],
         in_specs=[vmem] * 5 + [any_spec] * 6,
-        out_specs=[vmem] * 8 + [any_spec] * 5,
+        out_specs=[any_spec] * 4 + [vmem] * 3 + [any_spec] * 6,
         scratch_shapes=[
             pltpu.VMEM((whole, cols), bf16),
             pltpu.VMEM((whole, out_proj.shape[1]), bf16),
@@ -585,7 +589,12 @@
             pltpu.VMEM((expert_in.shape[1], shard, 128), f32),
             pltpu.VMEM((shard, e_cols), bf16),
             pltpu.VMEM((shard, e_cols), bf16),
-            pltpu.SemaphoreType.DMA((8,)),
+            pltpu.VMEM((length, cols), bf16),
+            pltpu.VMEM((length, WQ), bf16),
+            pltpu.VMEM((length, width), bf16),
+            pltpu.VMEM((length, width), f32),
+            pltpu.VMEM((length, wide), bf16),
+            pltpu.SemaphoreType.DMA((13,)),
             pltpu.SemaphoreType.DMA((FRONT_SENDS,)),
             pltpu.SemaphoreType.DMA((FRONT_SENDS,)),
         ],
@@ -930,18 +939,19 @@
 
 
 def back_kernel(
-    dx_own, g_ref, first, table, tiny, v, tokens, qkv, lse, cos, sin, seg_row,
+    dx_h, g_h, first_h, table, tiny, v_h, tokens_h, qkv_h, lse, cos, sin, seg_row,
     dx_in, grads, mix_sum, attn, xn, in_all, out_all,
     tokens_grad,
     g_out, mix_in, d_out, xn_core,
     in_v, out_v, mix_v, gl, gy, gz, act_v, aq_v, pq, wo, wi, wyo, wyi, wzo, wzi, wxo, own_d,
     dn, dxn, dl, dattn, dproj, dkv, bias, tbuf,
+    dx_own, g_ref, first, v, tokens, qkv,
     local_sem, send_sem, recv_sem,
 ):
     wire = Wire(send_sem, recv_sem)
     r, f = wire.r, wire.f
     shard = gl.shape[1]
-    length, width = tokens.shape
+    length, width = tokens_h.shape
     experts = 8
     low = lax.rem(f // 2, 2)
     cols_p, cols_a = pq.shape[1], aq_v.shape[1]
@@ -974,6 +984,10 @@
 
     load_dx = [
         local(dx_in.at[n], in_v.at[token_rows(n), pl.ds(0, dx_in.shape[2])]) for n in range(3)
+    ]
+    load_dx += [
+        local(dx_h, dx_own), local(v_h, v), local(first_h, first), local(g_h, g_ref),
+        local(qkv_h, qkv), local(tokens_h, tokens),
     ]
     load_out = local(out_all, out_v)
     load_g = {j: local(grads.at[shard_rows(j)], gl.at[j // 2]) for j in (4, 6, 2, 0)}
@@ -1303,7 +1317,7 @@
             jax.ShapeDtypeStruct((4, shard + TERMS, cols_p + cols_a // 2), bf16),
             jax.ShapeDtypeStruct((length, width), bf16),
         ],
-        in_specs=[vmem] * 12 + [any_spec] * 7,
+        in_specs=[any_spec] * 3 + [vmem] * 2 + [any_spec] * 3 + [vmem] * 4 + [any_spec] * 7,
         out_specs=[vmem] + [any_spec] * 4,
         scratch_shapes=[
             pltpu.VMEM(in_all.shape, bf16),
@@ -1331,7 +1345,13 @@
             pltpu.VMEM((2, length, HD), f32),
             pltpu.VMEM((length, length), f32),
             pltpu.VMEM((TERMS, width), f32),
-            pltpu.SemaphoreType.DMA((20,)),
+            pltpu.VMEM(dx_own.shape, bf16),
+            pltpu.VMEM(grad.shape, bf16),
+            pltpu.VMEM(first.shape, f32),
+            pltpu.VMEM(v.shape, bf16),
+            pltpu.VMEM(tokens.shape, bf16),
+            pltpu.VMEM(qkv.shape, bf16),
+            pltpu.SemaphoreType.DMA((26,)),
             pltpu.SemaphoreType.DMA((BACK_SENDS,)),
             pltpu.SemaphoreType.DMA((BACK_SENDS,)),
         ],

time: 432 us -> 428 us (level)
  Pallas kernels: 425 us -> 420 us
where the time goes in v8:
time: 428 us; the launch traced here: 427 us
  Pallas kernels  420 us (98%)
    pallas_call x1, Pallas kernels, run_back(): pl.pallas_call(back_kernel, out_shape=[jax.ShapeDtypeStruct((length, widt...  153 us
    pallas_call x1, Pallas kernels, front(): pl.pallas_call(front_kernel, out_shape=[jax.ShapeDtypeStruct((length, col...  133 us
    pallas_call x1, Pallas kernels, run_group(): pl.pallas_call(group_kernel, out_shape=[jax.ShapeDtypeStruct((4, length,...  121 us
    pallas_call x1, Pallas kernels, run_finish(): pl.pallas_call(finish_kernel, grid=(steps,), out_shape=[jax.ShapeDtypeStr...  12.9 us

profile of v8, /device:TPU:1, one launch (start us, length us, event | category | flops | bytes accessed | tf_op | source)
XLA Modules:
  0.0 427.1 jit_solution(10867039775345944787)
XLA Ops:
  0.7 0.1 pad.4.clone
  0.7 0.8 maximum_maximum_fusion
  1.5 0.7 pad_select_fusion.tiny_ref
  2.2 0.7 fusion.2
  2.9 0.9 pad_maximum_fusion
  3.9 133.2 %front.1 = (bf16[384,2048]{1,0:T(8,128)(2,1)}, bf16[384,1536]{1,0:T(8,128)(2,1)}, bf16[384,1536]{1,0:T(8,128)(2,1)}, f32[384,1536]{1,0:T(8,128)}, f32[384,128]{1...) custom-call(bf16[384,1536]{1,0:T(8,128)(2,1)} %tokens_h.1, ...), custom_call_target="tpu_custom_call" | custom-call | tf_op jit(solution)/shard_map/front/pallas_call | solution.py:562
  137.0 121.3 %group.1 = (bf16[4,384,1536]{2,1,0:T(8,128)(2,1)}, bf16[384,1664]{1,0:T(8,128)(2,1)}, bf16[3,384,1664]{2,1,0:T(8,128)(2,1)}, bf16[1536,2304]{1,0:T(8,128)(2,1)},...) custom-call(bf16[384,1664]{1,0:T(8,128)(2,1)} %get-tuple-element.34.v_ref.v_h, bf16[384,1536]{1,0:T(8,128)(2,1)} %g_h.1, ...), custom_call_target="tpu_custom_call" | custom-call | flops 65229815808 | bytes 51904512 | tf_op jit(solution)/shard_map/group/pallas_call | solution.py:888
  258.3 152.7 %back.1 = (bf16[384,1536]{1,0:T(8,128)(2,1)}, bf16[8,192,2304]{2,1,0:T(8,128)(2,1)}, bf16[2,384,1536]{2,1,0:T(8,128)(2,1)}, bf16[4,208,896]{2,1,0:T(8,128)(2,1)}, bf16[384,1536]{1,0:T(8,128)(2,1)}) custom-call(bf16[384,1664]{1,0:T(8,128)(2,1)} %get-tuple-element.38.dx_h, bf16[384,1536]{1,0:T(8,128)(2,1)} %g_h.1, ...), custom_call_target="tpu_custom_call" | custom-call | tf_op jit(solution)/shard_map/back/pallas_call | solution.py:1311
  411.1 0.8 convert_reduce_fusion
  411.9 0.1 fusion.3
  412.0 0.6 slice.23
  412.6 0.6 slice.22
  413.2 0.0 copy-start
  413.2 12.9 %finish.1 = (f32[192,8,1536]{2,1,0:T(8,128)}, f32[192,8,768]{2,1,0:T(8,128)}, f32[192,2048]{1,0:T(8,128)}, f32[192,1536]{1,0:T(8,128)}, bf16[384,1536]{1,0:T(8,128)(2,1)}) custom-call(bf16[8,192,2304]{2,1,0:T(8,128)(2,1)} %get-tuple-element.51.sums, bf16[4,208,896]{2,1,0:T(8,128)(2,1)} %get-tuple-element.52.dense, ...), custom_call_target="tpu_custom_call" | custom-call | tf_op jit(solution)/shard_map/finish/pallas_call | solution.py:1395
  426.1 0.0 copy-done
  426.1 1.0 copy.19
  (2 shorter events, 0.0 us)
Async XLA Ops:
  413.2 12.9 %copy-start = (bf16[384,1536]{1,0:T(8,128)(2,1)S(1)}, bf16[384,1536]{1,0:T(8,128)(2,1)}, u32[]{:S(2)}) copy-start(bf16[384,1536]{1,0:T(8,128)(2,1)} %get-tuple-element.74) | copy-start | bytes 3538948

commit v9 on v8

--- a/solution.py
+++ b/solution.py
@@ -1389,7 +1389,7 @@
 def run_finish(expert_sum, dense, first, mix_sum, mix_in, hidden):
     n_experts, shard, cols = expert_sum.shape
     length, width = first.shape
-    steps = 6
+    steps = 12
     rows, tokens = shard // steps, length // steps
     cut = dense.shape[2] - width // 4
     return pl.pallas_call(

time: 428 us -> 430 us (level)
  no operation moved by 1% of the time
where the time goes in v9:
time: 430 us
  Pallas kernels  423 us (98%)
    pallas_call x1, Pallas kernels, run_back(): pl.pallas_call(back_kernel, out_shape=[jax.ShapeDtypeStruct((length, widt...  153 us
    pallas_call x1, Pallas kernels, front(): pl.pallas_call(front_kernel, out_shape=[jax.ShapeDtypeStruct((length, col...  133 us
    pallas_call x1, Pallas kernels, run_group(): pl.pallas_call(group_kernel, out_shape=[jax.ShapeDtypeStruct((4, length,...  121 us
    pallas_call x1, Pallas kernels, run_finish(): pl.pallas_call(finish_kernel, grid=(steps,), out_shape=[jax.ShapeDtypeStr...  15.5 us

profile of v9, /device:TPU:1, one launch (start us, length us, event | category | flops | bytes accessed | tf_op | source)
XLA Modules:
  0.0 429.7 jit_solution(487728672789793558)
XLA Ops:
  0.7 0.1 pad.4.clone
  0.7 0.8 maximum_maximum_fusion
  1.5 0.7 pad_select_fusion.tiny_ref
  2.2 0.7 fusion.2
  2.9 0.9 pad_maximum_fusion
  3.9 133.2 %front.1 = (bf16[384,2048]{1,0:T(8,128)(2,1)}, bf16[384,1536]{1,0:T(8,128)(2,1)}, bf16[384,1536]{1,0:T(8,128)(2,1)}, f32[384,1536]{1,0:T(8,128)}, f32[384,128]{1...) custom-call(bf16[384,1536]{1,0:T(8,128)(2,1)} %tokens_h.1, ...), custom_call_target="tpu_custom_call" | custom-call | tf_op jit(solution)/shard_map/front/pallas_call | solution.py:562
  137.0 121.3 %group.1 = (bf16[4,384,1536]{2,1,0:T(8,128)(2,1)}, bf16[384,1664]{1,0:T(8,128)(2,1)}, bf16[3,384,1664]{2,1,0:T(8,128)(2,1)}, bf16[1536,2304]{1,0:T(8,128)(2,1)},...) custom-call(bf16[384,1664]{1,0:T(8,128)(2,1)} %get-tuple-element.34.v_ref.v_h, bf16[384,1536]{1,0:T(8,128)(2,1)} %g_h.1, ...), custom_call_target="tpu_custom_call" | custom-call | flops 65229815808 | bytes 51904512 | tf_op jit(solution)/shard_map/group/pallas_call | solution.py:888
  258.3 152.7 %back.1 = (bf16[384,1536]{1,0:T(8,128)(2,1)}, bf16[8,192,2304]{2,1,0:T(8,128)(2,1)}, bf16[2,384,1536]{2,1,0:T(8,128)(2,1)}, bf16[4,208,896]{2,1,0:T(8,128)(2,1)}, bf16[384,1536]{1,0:T(8,128)(2,1)}) custom-call(bf16[384,1664]{1,0:T(8,128)(2,1)} %get-tuple-element.38.dx_h, bf16[384,1536]{1,0:T(8,128)(2,1)} %g_h.1, ...), custom_call_target="tpu_custom_call" | custom-call | tf_op jit(solution)/shard_map/back/pallas_call | solution.py:1311
  411.1 0.8 convert_reduce_fusion
  411.9 0.1 fusion.3
  412.0 0.6 slice.23
  412.6 0.6 slice.22
  413.2 0.0 copy-start
  413.2 15.5 %finish.1 = (f32[192,8,1536]{2,1,0:T(8,128)}, f32[192,8,768]{2,1,0:T(8,128)}, f32[192,2048]{1,0:T(8,128)}, f32[192,1536]{1,0:T(8,128)}, bf16[384,1536]{1,0:T(8,128)(2,1)}) custom-call(bf16[8,192,2304]{2,1,0:T(8,128)(2,1)} %get-tuple-element.51.sums, bf16[4,208,896]{2,1,0:T(8,128)(2,1)} %get-tuple-element.52.dense, ...), custom_call_target="tpu_custom_call" | custom-call | tf_op jit(solution)/shard_map/finish/pallas_call | solution.py:1395
  428.7 0.0 copy-done
  428.7 1.0 copy.19
  (2 shorter events, 0.0 us)
Async XLA Ops:
  413.2 15.6 %copy-start = (bf16[384,1536]{1,0:T(8,128)(2,1)S(1)}, bf16[384,1536]{1,0:T(8,128)(2,1)}, u32[]{:S(2)}) copy-start(bf16[384,1536]{1,0:T(8,128)(2,1)} %get-tuple-element.74) | copy-start | bytes 3538948
